TPU v7x, 768 devices: a whole 4x8x12 slice. The times are simulated.
768 devices in a mesh: dp: 32 (over x, y_hi, core), tensor: 24 (over y_lo, z).
Axes of the slice: x: 4, y: 8 (y_hi: 4, y_lo: 2; y = y_hi * 2 + y_lo), z: 12, core: 2. Of those that a mesh axis runs over, the one named last changes fastest.
Arguments:
- gate_pre: bfloat16 [9216, 15360], P('dp', 'tensor'), may hold values from -6 to 6
- up_pre: bfloat16 [9216, 15360], P('dp', 'tensor'), may hold values from -6 to 6
- down_weight: bfloat16 [15360, 4096], P('tensor'), may hold values from -0.046875 to 0.046875
- cotangent: bfloat16 [9216, 4096], P(('dp', 'tensor')), may hold values from -6 to 6
Outputs:
- output: bfloat16 [9216, 4096], P(('dp', 'tensor'))
- gate_grad: bfloat16 [9216, 15360], P('dp', 'tensor')
- up_grad: bfloat16 [9216, 15360], P('dp', 'tensor')
- weight_grad: bfloat16 [15360, 4096], P('tensor', 'dp')
All inputs are finite; a program needn't handle non-finite values.
Results may differ from a plain program's by a relative error of at most 0.02.
Values may be sent and summed in bfloat16 or wider, within the bound.
No kernel may reach another device: no remote copies, remote signals or barrier semaphores. Data moves between devices by JAX's collectives and lax.ppermute only.
A program may use at most 64 MiB of HBM per device.

v0:
```python
import jax
import jax.numpy as jnp
from jax import lax
from jax.sharding import PartitionSpec as P


def per_device(gate_pre, up_pre, down_weight, cotangent):
    dp_count = lax.axis_size("dp")
    gate_wide = gate_pre.astype(jnp.float32)
    up_wide = up_pre.astype(jnp.float32)
    sigmoid_gate = jax.nn.sigmoid(gate_wide)
    activation = gate_wide * sigmoid_gate
    hidden = (activation * up_wide).astype(jnp.bfloat16)
    output = lax.psum_scatter(
        jnp.dot(hidden, down_weight, preferred_element_type=jnp.float32).astype(jnp.bfloat16),
        "tensor",
        scatter_dimension=0,
        tiled=True,
    )
    cot_piece = lax.all_gather(cotangent, "tensor", axis=0, tiled=True)
    back_rows = lax.dot_general(
        cot_piece, down_weight, (((1,), (1,)), ((), ())), preferred_element_type=jnp.float32
    )
    grad_acc = lax.dot_general(
        hidden, cot_piece, (((0,), (0,)), ((), ())), preferred_element_type=jnp.float32
    )
    weight_grad = lax.psum_scatter(
        (grad_acc / dp_count).astype(jnp.bfloat16), "dp", scatter_dimension=1, tiled=True
    )
    gate_grad = (
        back_rows * up_wide * sigmoid_gate * (1.0 + gate_wide * (1.0 - sigmoid_gate))
    ).astype(jnp.bfloat16)
    up_grad = (back_rows * activation).astype(jnp.bfloat16)
    return (output, gate_grad, up_grad, weight_grad)


def solution(mesh):
    return jax.shard_map(
        per_device,
        mesh=mesh,
        in_specs=(
            P("dp", "tensor"),
            P("dp", "tensor"),
            P("tensor", None),
            P(("dp", "tensor"), None),
        ),
        out_specs=(
            P(("dp", "tensor"), None),
            P("dp", "tensor"),
            P("dp", "tensor"),
            P("tensor", "dp"),
        ),
        check_vma=False,
    )
```

profile of v0, /device:TPU:1, one launch (start us, length us, event | category | flops | bytes accessed | tf_op | source)
XLA Modules:
  0.0 273.5 jit_solution(8831006870834733207)
XLA Ops:
  7.2 0.0 copy-start.1
  7.2 0.0 copy-start.2
  7.2 0.0 all-gather.3.cloned.1.call-start
  7.2 0.7 all-gather.3.cloned.1.call-update
  7.9 0.0 reduce-scatter.6.cloned.1.call-start
  8.0 104.0 %all-gather.3.cloned.1.call-done = bf16[24,12,4096]{2,1,0:T(8,128)(2,1)} async-done(((bf16[1,12,4096]{2,1,0:T(8,128)(2,1)}), bf16[24,12,4096]{2,1,0:T(8,128)(2,1)}) %all-gather.3.cloned.1.call-update) | async-done | bytes 2359312 | tf_op jit(solution)/shard_map/all_gather | solution.py:20
  112.0 2.8 %reshape.9 = bf16[288,4096]{1,0:T(8,128)(2,1)S(1)} reshape(bf16[24,12,4096]{2,1,0:T(8,128)(2,1)} %all-gather.3.cloned.1.call-done) | data formatting | bytes 4718592
  114.8 0.0 copy-done.1
  114.8 0.0 copy-done.2
  114.8 4.9 %multiply_convert_fusion = bf16[640,4096]{1,0:T(8,128)(2,1)} fusion(bf16[288,4096]{1,0:T(8,128)(2,1)S(1)} %reshape.9, bf16[288,640]{1,0:T(8,128)(2,1)S(1)} %copy-done.1, bf16[288,640]{1,0:T(8,128)(2,1)S(1)} %copy-done.2), kind=kOutput, calls=%fused_computation | convolution fusion | flops 1516666880 | bytes 8339456 | tf_op jit(solution)/shard_map/dot_general | solution.py:24
  119.7 7.8 %copy.8 = bf16[640,4096]{0,1:T(8,128)(2,1)} copy(bf16[640,4096]{1,0:T(8,128)(2,1)} %multiply_convert_fusion) | data formatting | bytes 10485760
  127.6 0.0 reduce-scatter.6.cloned.1.call-update
  127.6 4.5 %convolution_convert_fusion = bf16[288,4096]{1,0:T(8,128)(2,1)S(1)} fusion(bf16[640,4096]{1,0:T(8,128)(2,1)} %param.6, bf16[288,640]{1,0:T(8,128)(2,1)S(1)} %copy-done.1, bf16[288,640]{1,0:T(8,128)(2,1)S(1)} %copy-done.2), kind=kOutput, calls=%fused_computation.1 | convolution fusion | flops 1512603648 | bytes 8339456 | tf_op jit(solution)/shard_map/dot_general | solution.py:15
  132.1 51.6 %fusion = bf16[16,4096]{1,0:T(8,128)(2,1)S(1)} fusion(bf16[288,4096]{1,0:T(8,128)(2,1)S(1)} %convolution_convert_fusion), kind=kCustom, calls=%all-reduce-scatter | all-reduce-scatter fusion | flops 1572865 | bytes 2494464
  183.7 1.3 collective-permute-start.5
  185.1 6.7 %collective-permute-start.4 = (bf16[16,4096]{1,0:T(8,128)(2,1)S(1)}, bf16[16,4096]{1,0:T(8,128)(2,1)S(1)}, u32[]{:S(2)}, u32[]{:S(2)}) collective-permute-start(bf16[16,4096]{1,0:T(8,128)(2,1)S(1)} %fusion), channel_id=1, source_target_pairs={{0,5},{1,6},{2,7},{3,8},{4,9},{5,10},{6,11},{7,12},{8,13},{9,14},{... | collective-permute-start | bytes 393224
  191.7 3.8 %collective-permute-start.3 = (bf16[16,4096]{1,0:T(8,128)(2,1)S(1)}, bf16[16,4096]{1,0:T(8,128)(2,1)S(1)}, u32[]{:S(2)}, u32[]{:S(2)}) collective-permute-start(bf16[16,4096]{1,0:T(8,128)(2,1)S(1)} %fusion), channel_id=1, source_target_pairs={{0,4},{1,5},{2,6},{3,7},{4,8},{5,9},{6,10},{7,11},{8,12},{9,13},{1... | collective-permute-start | bytes 393224
  195.5 3.9 %collective-permute-start.2 = (bf16[16,4096]{1,0:T(8,128)(2,1)S(1)}, bf16[16,4096]{1,0:T(8,128)(2,1)S(1)}, u32[]{:S(2)}, u32[]{:S(2)}) collective-permute-start(bf16[16,4096]{1,0:T(8,128)(2,1)S(1)} %fusion), channel_id=1, source_target_pairs={{0,3},{1,4},{2,5},{3,6},{4,7},{5,8},{6,9},{7,10},{8,11},{9,12},{10... | collective-permute-start | bytes 393224
  199.5 3.1 %collective-permute-start.1 = (bf16[16,4096]{1,0:T(8,128)(2,1)S(1)}, bf16[16,4096]{1,0:T(8,128)(2,1)S(1)}, u32[]{:S(2)}, u32[]{:S(2)}) collective-permute-start(bf16[16,4096]{1,0:T(8,128)(2,1)S(1)} %fusion), channel_id=1, source_target_pairs={{0,2},{1,3},{2,4},{3,5},{4,6},{5,7},{6,8},{7,9},{8,10},{9,11},{10,... | collective-permute-start | bytes 393224
  202.6 0.0 collective-permute-done.5
  202.6 3.1 %collective-permute-start = (bf16[16,4096]{1,0:T(8,128)(2,1)S(1)}, bf16[16,4096]{1,0:T(8,128)(2,1)S(1)}, u32[]{:S(2)}, u32[]{:S(2)}) collective-permute-start(bf16[16,4096]{1,0:T(8,128)(2,1)S(1)} %fusion), channel_id=1, source_target_pairs={{0,1},{1,2},{2,3},{3,4},{4,5},{5,6},{6,7},{7,8},{8,9},{9,10},{10,1... | collective-permute-start | bytes 393224
  205.7 1.3 dynamic-slice.4
  207.6 0.0 collective-permute-done.4
  207.6 0.0 collective-permute-done.3
  207.6 6.1 %collective-permute-done.2 = bf16[16,4096]{1,0:T(8,128)(2,1)S(1)} collective-permute-done((bf16[16,4096]{1,0:T(8,128)(2,1)S(1)}, bf16[16,4096]{1,0:T(8,128)(2,1)S(1)}, u32[]{:S(2)}, u32[]{:S(2)}) %collective-permute-start.2) | collective-permute-done | bytes 131104
  213.7 3.0 %collective-permute-done.1 = bf16[16,4096]{1,0:T(8,128)(2,1)S(1)} collective-permute-done((bf16[16,4096]{1,0:T(8,128)(2,1)S(1)}, bf16[16,4096]{1,0:T(8,128)(2,1)S(1)}, u32[]{:S(2)}, u32[]{:S(2)}) %collective-permute-start.1) | collective-permute-done | bytes 131104
  216.8 1.8 collective-permute-done
  218.6 1.8 concatenate
  220.4 0.7 constant_dynamic-slice_fusion
  221.1 6.3 %multiply_convert_fusion.1 = (bf16[288,640]{1,0:T(8,128)(2,1)}, bf16[288,640]{1,0:T(8,128)(2,1)}) fusion(bf16[288,640]{1,0:T(8,128)(2,1)S(1)} %copy-done.2, bf16[288,640]{1,0:T(8,128)(2,1)S(1)} %copy-done.1, bf16[288,4096]{1,0:T(8,128)(2,1)} %copy-done, bf16[640,4096]{1,0:T(8,128)(2,1)} %param.6), kind=kOutput, calls=%fused_computation.15 | convolution fusion | flops 1512714240 | bytes 9076736 | tf_op jit(solution)/shard_map/dot_general | solution.py:21
  227.4 37.5 %reduce-scatter.6.cloned.1.call-done = bf16[128,640]{1,0:T(8,128)(2,1)} async-done(((bf16[4096,640]{1,0:T(8,128)(2,1)}), bf16[128,640]{1,0:T(8,128)(2,1)}) %reduce-scatter.6.cloned.1.call-update) | async-done | bytes 163856
  264.9 1.7 copy.9
  (3 shorter events, 0.0 us)
Async XLA Ops:
  7.2 107.6 %copy-start.1 = (bf16[288,640]{1,0:T(8,128)(2,1)S(1)}, bf16[288,640]{1,0:T(8,128)(2,1)}, u32[]{:S(2)}) copy-start(bf16[288,640]{1,0:T(8,128)(2,1)} %param.5) | copy-start | bytes 1105924
  7.2 107.6 %copy-start.2 = (bf16[288,640]{1,0:T(8,128)(2,1)S(1)}, bf16[288,640]{1,0:T(8,128)(2,1)}, u32[]{:S(2)}) copy-start(bf16[288,640]{1,0:T(8,128)(2,1)} %param.4) | copy-start | bytes 1105924
  7.2 104.8 %all-gather.3.cloned.1.call-start = ((), (), s32[]{:S(2)}) async-start(), calls=%async_computation.1 | async-start | bytes 3276800 | tf_op jit(solution)/shard_map/all_gather | solution.py:20
  7.9 257.0 %reduce-scatter.6.cloned.1.call-start = ((), (), s32[]{:S(2)}) async-start(), calls=%async_computation.2 | async-start | bytes 5406720
  114.8 4.9 %copy-start = (bf16[288,4096]{1,0:T(8,128)(2,1)}, bf16[288,4096]{1,0:T(8,128)(2,1)S(1)}, u32[]{:S(2)}) copy-start(bf16[288,4096]{1,0:T(8,128)(2,1)S(1)} %reshape.9) | copy-start | bytes 7077892
  183.7 18.8 %collective-permute-start.5 = (bf16[12,4096]{1,0:T(8,128)(2,1)S(1)}, bf16[12,4096]{1,0:T(8,128)(2,1)S(1)}, u32[]{:S(2)}, u32[]{:S(2)}) collective-permute-start(bf16[12,4096]{1,0:T(8,128)(2,1)S(1)} %slice), channel_id=1, source_target_pairs={{0,6},{1,7},{2,8},{3,9},{4,10},{5,11},{6,12},{7,13},{8,14},{9,15},... | collective-permute-start | bytes 294920
  185.1 22.6 %collective-permute-start.4 = (bf16[16,4096]{1,0:T(8,128)(2,1)S(1)}, bf16[16,4096]{1,0:T(8,128)(2,1)S(1)}, u32[]{:S(2)}, u32[]{:S(2)}) collective-permute-start(bf16[16,4096]{1,0:T(8,128)(2,1)S(1)} %fusion), channel_id=1, source_target_pairs={{0,5},{1,6},{2,7},{3,8},{4,9},{5,10},{6,11},{7,12},{8,13},{9,14},{... | collective-permute-start | bytes 393224
  191.7 15.9 %collective-permute-start.3 = (bf16[16,4096]{1,0:T(8,128)(2,1)S(1)}, bf16[16,4096]{1,0:T(8,128)(2,1)S(1)}, u32[]{:S(2)}, u32[]{:S(2)}) collective-permute-start(bf16[16,4096]{1,0:T(8,128)(2,1)S(1)} %fusion), channel_id=1, source_target_pairs={{0,4},{1,5},{2,6},{3,7},{4,8},{5,9},{6,10},{7,11},{8,12},{9,13},{1... | collective-permute-start | bytes 393224
  195.5 18.2 %collective-permute-start.2 = (bf16[16,4096]{1,0:T(8,128)(2,1)S(1)}, bf16[16,4096]{1,0:T(8,128)(2,1)S(1)}, u32[]{:S(2)}, u32[]{:S(2)}) collective-permute-start(bf16[16,4096]{1,0:T(8,128)(2,1)S(1)} %fusion), channel_id=1, source_target_pairs={{0,3},{1,4},{2,5},{3,6},{4,7},{5,8},{6,9},{7,10},{8,11},{9,12},{10... | collective-permute-start | bytes 393224
  199.5 17.3 %collective-permute-start.1 = (bf16[16,4096]{1,0:T(8,128)(2,1)S(1)}, bf16[16,4096]{1,0:T(8,128)(2,1)S(1)}, u32[]{:S(2)}, u32[]{:S(2)}) collective-permute-start(bf16[16,4096]{1,0:T(8,128)(2,1)S(1)} %fusion), channel_id=1, source_target_pairs={{0,2},{1,3},{2,4},{3,5},{4,6},{5,7},{6,8},{7,9},{8,10},{9,11},{10,... | collective-permute-start | bytes 393224
  202.6 16.0 %collective-permute-start = (bf16[16,4096]{1,0:T(8,128)(2,1)S(1)}, bf16[16,4096]{1,0:T(8,128)(2,1)S(1)}, u32[]{:S(2)}, u32[]{:S(2)}) collective-permute-start(bf16[16,4096]{1,0:T(8,128)(2,1)S(1)} %fusion), channel_id=1, source_target_pairs={{0,1},{1,2},{2,3},{3,4},{4,5},{5,6},{6,7},{7,8},{8,9},{9,10},{10,1... | collective-permute-start | bytes 393224
Sparse Core Ops, SparseCore 0:
  10.4 101.5 all-gather.2
  127.7 137.1 reduce-scatter.5
where the time goes:
time: 274 us; the launch traced here: 273 us
  waiting for transfers between devices  153 us (56%)
  blocking collectives  51.6 us (19%)
  starting transfers between devices  21.9 us (8%)
  local copies, waits for them, and re-layouts  16.2 us (6%)
  matrix products  15.7 us (6%)
  between operations  14.8 us (5%)
    all_gather x1, waiting for transfers between devices, per_device(): cot_piece = lax.all_gather(cotangent, 'tensor', axis=0, tiled=True)  104 us
    unnamed x1, blocking collectives  51.6 us
    unnamed x9, waiting for transfers between devices  49.2 us
    unnamed x7, starting transfers between devices  21.9 us
    unnamed x13, local copies, waits for them, and re-layouts  16.2 us
    dot_general x1, matrix products, per_device(): lax.dot_general(cot_piece, down_weight, (((1,), (1,)), ((), ())), preferr...  6.26 us
  transfers between devices with their start and end apart: 8, of which 5 were waited for; matrix products, arithmetic and copies ran while one was open for 24% of the time, Pallas kernels for 0%

commit v1 on v0

v1 whole, which is shorter than its diff:
```python
import jax
import jax.numpy as jnp
from jax import lax
from jax.sharding import Mesh, PartitionSpec as P

NX, NYH, NC, NYL, NZ = 4, 4, 2, 2, 12
BF, F32 = jnp.bfloat16, jnp.float32


tie = lax.optimization_barrier


def shift(n, by):
    return [(i, (i + by) % n) for i in range(n)]


def per_device(gate_pre, up_pre, down_weight, cotangent):
    tok, ff = gate_pre.shape
    rows, feat = cotangent.shape
    half = feat // NC
    lane = half // (NX * NYH)
    core, yl, z = lax.axis_index("c"), lax.axis_index("yl"), lax.axis_index("z")

    def halves(array):
        blocks = [array[:, i * lane : (i + 1) * lane] for i in range(NX * NYH * NC)]
        return jnp.concatenate(blocks[0::2], axis=1), jnp.concatenate(blocks[1::2], axis=1)

    even, odd = halves(cotangent)
    mine = jnp.where(core == 0, even, odd)
    other = jnp.where(core == 0, odd, even)
    swap2 = [(0, 1), (1, 0)]
    diagonal = [(0, 3), (1, 2), (2, 1), (3, 0)]
    from_core = lax.ppermute(other, "c", swap2)
    from_yl = lax.ppermute(mine, "yl", swap2)
    from_diag = lax.ppermute(other, ("c", "yl"), diagonal)
    first = yl == 0
    block = jnp.concatenate(
        [
            jnp.where(first, mine, from_yl),
            jnp.where(first, from_yl, mine),
            jnp.where(first, from_core, from_diag),
            jnp.where(first, from_diag, from_core),
        ],
        axis=0,
    )

    gate_wide = gate_pre.astype(F32)
    up_wide = up_pre.astype(F32)
    sig = jax.nn.sigmoid(gate_wide)
    act = gate_wide * sig
    hidden, block = tie(((act * up_wide).astype(BF), block))
    hidden_z = hidden.reshape(NYL, NZ, rows, ff).transpose(1, 0, 2, 3).reshape(tok, ff)
    partial = jnp.dot(hidden_z, down_weight, preferred_element_type=F32).astype(BF)
    hidden_peer = lax.ppermute(hidden_z, "c", swap2)
    hidden_both = jnp.concatenate(
        [hidden_z.reshape(NZ, NYL * rows, ff), hidden_peer.reshape(NZ, NYL * rows, ff)], axis=1
    ).reshape(NC * tok, ff)

    w_even, w_odd = halves(down_weight)
    w_half = jnp.where(core == 0, w_even, w_odd)

    ring = jnp.zeros((NZ,) + block.shape, BF)
    put = lambda buf, piece, at: lax.dynamic_update_slice(
        buf, piece[None], (lax.rem(at + NZ, NZ), 0, 0)
    )
    ring = put(ring, block, z)
    up, down = block, block
    for step in range(1, NZ // 2 + 1):
        up = lax.ppermute(up, "z", shift(NZ, 1))
        ring = put(ring, up, z - step)
        if step < NZ // 2:
            down = lax.ppermute(down, "z", shift(NZ, -1))
            ring = put(ring, down, z + step)
        if step == 1:
            up, down, partial = tie((up, down, partial))
            out_z = lax.psum_scatter(partial, "z", scatter_dimension=0, tiled=True)
        if step == 2:
            up, down, hidden_both = tie((up, down, hidden_both))
        if step == 3:
            up, down, w_half = tie((up, down, w_half))
    cot_both = ring.reshape(NC * tok, half)

    grad_acc = lax.dot_general(
        cot_both, hidden_both, (((0,), (0,)), ((), ())), preferred_element_type=F32
    )
    term = (grad_acc / (NX * NYH * NC)).astype(BF).reshape(NX, half // NX, ff)
    term, cot_both, up_pre, gate_pre = tie((term, cot_both, up_pre, gate_pre))
    by_x = lax.all_to_all(term, "x", 0, 0)
    sum_x = by_x.astype(F32).sum(0).astype(BF).reshape(NYH, lane, ff)
    by_y = lax.all_to_all(sum_x, "yh", 0, 0)
    weight_grad = by_y.astype(F32).sum(0).astype(BF).T

    back_part = lax.dot_general(
        cot_both, w_half, (((1,), (1,)), ((), ())), preferred_element_type=F32
    ).reshape(NZ, NC, NYL * rows, ff)
    back_z = back_part[:, 0] + lax.ppermute(back_part[:, 1], "c", swap2)
    gate_wide = gate_pre.astype(F32)
    up_wide = up_pre.astype(F32)
    sig = jax.nn.sigmoid(gate_wide)
    act = gate_wide * sig
    back = back_z.reshape(NZ, NYL, rows, ff).transpose(1, 0, 2, 3).reshape(tok, ff)
    gate_grad = (back * up_wide * sig * (1.0 + gate_wide * (1.0 - sig))).astype(BF)
    up_grad = (back * act).astype(BF)

    keep = lax.dynamic_slice_in_dim(out_z, yl * rows, rows, 0)
    give = lax.dynamic_slice_in_dim(out_z, (1 - yl) * rows, rows, 0)
    got = lax.ppermute(give, "yl", swap2)
    output = (keep.astype(F32) + got.astype(F32)).astype(BF)
    return output, gate_grad, up_grad, weight_grad


def solution(mesh):
    fine = Mesh(
        mesh.devices.reshape(NX, NYH, NC, NYL, NZ), ("x", "yh", "c", "yl", "z")
    )
    dp, tensor = ("x", "yh", "c"), ("yl", "z")
    return jax.shard_map(
        per_device,
        mesh=fine,
        in_specs=(P(dp, tensor), P(dp, tensor), P(tensor, None), P(dp + tensor, None)),
        out_specs=(P(dp + tensor, None), P(dp, tensor), P(dp, tensor), P(tensor, dp)),
        check_vma=False,
    )
```

time: 274 us -> 199 us (0.73)
  the two profiles are of different devices: /device:TPU:1 before, /device:TPU:2 now
where the time goes in v1:
time: 199 us; the launch traced here: 197 us
  starting transfers between devices  74.4 us (37%)
  waiting for transfers between devices  52.7 us (26%)
  local copies, waits for them, and re-layouts  31.9 us (16%)
  between operations  14.8 us (7%)
  matrix products  14.5 us (7%)
  other arithmetic  8.98 us (5%)
    ppermute x5, starting transfers between devices, per_device(): down = lax.ppermute(down, 'z', shift(NZ, -1))  33.1 us
    ppermute x6, waiting for transfers between devices, per_device(): up = lax.ppermute(up, 'z', shift(NZ, 1))  25.9 us
    unnamed x46, local copies, waits for them, and re-layouts  23.1 us
    all_to_all x1, waiting for transfers between devices, per_device(): by_x = lax.all_to_all(term, 'x', 0, 0)  17 us
    ppermute x6, starting transfers between devices, per_device(): up = lax.ppermute(up, 'z', shift(NZ, 1))  14.5 us
    all_to_all x1, waiting for transfers between devices, per_device(): by_y = lax.all_to_all(sum_x, 'yh', 0, 0)  6.87 us
    all_to_all x1, starting transfers between devices, per_device(): by_y = lax.all_to_all(sum_x, 'yh', 0, 0)  6.31 us
    dot_general x1, matrix products, per_device(): jnp.dot(hidden_z, down_weight, preferred_element_type=F32).astype(BF)  6.05 us
  transfers between devices with their start and end apart: 20, of which 10 were waited for; matrix products, arithmetic and copies ran while one was open for 20% of the time, Pallas kernels for 0%

profile of v1, /device:TPU:2, one launch (start us, length us, event | category | flops | bytes accessed | tf_op | source)
XLA Modules:
  0.0 197.2 jit_solution(5891188052255753964)
XLA Ops:
  20.0 1.9 collective-permute-start.1
  21.9 3.6 %collective-permute-start.2 = (bf16[12,2048]{1,0:T(8,128)(2,1)S(1)}, bf16[12,2048]{1,0:T(8,128)(2,1)S(1)}, u32[]{:S(2)}, u32[]{:S(2)}) collective-permute-start(bf16[12,2048]{1,0:T(8,128)(2,1)S(1)} %get-tuple-element.75), channel_id=1, source_target_pairs={{0,36},{12,24},{24,12},{36,0},{1,37},{13,25},{25,13},{37,1},{2,38}... | collective-permute-start | bytes 147464 | tf_op jit(solution)/shard_map/ppermute | solution.py:35
  25.5 2.6 %collective-permute-start = (bf16[12,2048]{1,0:T(8,128)(2,1)S(1)}, bf16[12,2048]{1,0:T(8,128)(2,1)S(1)}, u32[]{:S(2)}, u32[]{:S(2)}) collective-permute-start(bf16[12,2048]{1,0:T(8,128)(2,1)S(1)} %get-tuple-element.74), channel_id=1, source_target_pairs={{0,12},{12,0},{1,13},{13,1},{2,14},{14,2},{3,15},{15,3},{4,16},{16... | collective-permute-start | bytes 147464 | tf_op jit(solution)/shard_map/ppermute | solution.py:34
  38.2 1.8 broadcast_select_fusion
  41.5 1.9 collective-permute-start.8
  43.4 6.1 %convolution_convert_fusion = bf16[288,4096]{1,0:T(8,128)(2,1)} fusion(bf16[288,640]{1,0:T(8,128)(2,1)} %reshape.39, bf16[640,4096]{1,0:T(8,128)(2,1)} %param.6), kind=kOutput, calls=%fused_computation | convolution fusion | flops 1511129088 | bytes 7970816 | tf_op jit(solution)/shard_map/dot_general | solution.py:53
  49.5 4.3 %collective-permute-start.3 = (bf16[48,2048]{1,0:T(8,128)(2,1)S(1)}, bf16[48,2048]{1,0:T(8,128)(2,1)}, u32[]{:S(2)}, u32[]{:S(2)}) collective-permute-start(bf16[48,2048]{1,0:T(8,128)(2,1)S(1)} %pad_maximum_fusion.1), channel_id=1, source_target_pairs={{0,1},{1,2},{2,3},{3,4},{4,5},{5,6},{6,7},{7,8},{8,9},{9,10},{10,1... | collective-permute-start | bytes 589832 | tf_op jit(solution)/shard_map/ppermute | solution.py:69
  53.7 12.2 %collective-permute-start.4 = (bf16[48,2048]{1,0:T(8,128)(2,1)S(1)}, bf16[48,2048]{1,0:T(8,128)(2,1)}, u32[]{:S(2)}, u32[]{:S(2)}) collective-permute-start(bf16[48,2048]{1,0:T(8,128)(2,1)S(1)} %pad_maximum_fusion.1), channel_id=1, source_target_pairs={{0,11},{1,0},{2,1},{3,2},{4,3},{5,4},{6,5},{7,6},{8,7},{9,8},{10,9... | collective-permute-start | bytes 589832 | tf_op jit(solution)/shard_map/ppermute | solution.py:72
  67.1 2.6 %collective-permute-done.3 = bf16[48,2048]{1,0:T(8,128)(2,1)} collective-permute-done((bf16[48,2048]{1,0:T(8,128)(2,1)S(1)}, bf16[48,2048]{1,0:T(8,128)(2,1)}, u32[]{:S(2)}, u32[]{:S(2)}) %collective-permute-start.3) | collective-permute-done | bytes 196640 | tf_op jit(solution)/shard_map/ppermute | solution.py:69
  70.8 1.9 collective-permute-start.6
  72.7 5.7 %collective-permute-start.7 = (bf16[48,2048]{1,0:T(8,128)(2,1)}, bf16[48,2048]{1,0:T(8,128)(2,1)}, u32[]{:S(2)}, u32[]{:S(2)}) collective-permute-start(bf16[48,2048]{1,0:T(8,128)(2,1)} %collective-permute-done.4), channel_id=1, source_target_pairs={{0,11},{1,0},{2,1},{3,2},{4,3},{5,4},{6,5},{7,6},{8,7},{9,8},{10,9... | collective-permute-start | bytes 589832 | tf_op jit(solution)/shard_map/ppermute | solution.py:72
  82.7 5.6 %collective-permute-start.10 = (bf16[48,2048]{1,0:T(8,128)(2,1)}, bf16[48,2048]{1,0:T(8,128)(2,1)S(1)}, u32[]{:S(2)}, u32[]{:S(2)}) collective-permute-start(bf16[48,2048]{1,0:T(8,128)(2,1)} %collective-permute-done.7), channel_id=1, source_target_pairs={{0,11},{1,0},{2,1},{3,2},{4,3},{5,4},{6,5},{7,6},{8,7},{9,8},{10,9... | collective-permute-start | bytes 589832 | tf_op jit(solution)/shard_map/ppermute | solution.py:72
  88.3 1.9 collective-permute-start.9
  91.8 5.3 %collective-permute-done.9 = bf16[48,2048]{1,0:T(8,128)(2,1)S(1)} collective-permute-done((bf16[48,2048]{1,0:T(8,128)(2,1)S(1)}, bf16[48,2048]{1,0:T(8,128)(2,1)S(1)}, u32[]{:S(2)}, u32[]{:S(2)}) %collective-permute-start.9) | collective-permute-done | bytes 196640 | tf_op jit(solution)/shard_map/ppermute | solution.py:69
  97.1 2.6 %collective-permute-start.11 = (bf16[48,2048]{1,0:T(8,128)(2,1)S(1)}, bf16[48,2048]{1,0:T(8,128)(2,1)S(1)}, u32[]{:S(2)}, u32[]{:S(2)}) collective-permute-start(bf16[48,2048]{1,0:T(8,128)(2,1)S(1)} %collective-permute-done.9), channel_id=1, source_target_pairs={{0,1},{1,2},{2,3},{3,4},{4,5},{5,6},{6,7},{7,8},{8,9},{9,10},{10,1... | collective-permute-start | bytes 589832 | tf_op jit(solution)/shard_map/ppermute | solution.py:69
  99.7 4.4 %collective-permute-start.12 = (bf16[48,2048]{1,0:T(8,128)(2,1)S(1)}, bf16[48,2048]{1,0:T(8,128)(2,1)S(1)}, u32[]{:S(2)}, u32[]{:S(2)}) collective-permute-start(bf16[48,2048]{1,0:T(8,128)(2,1)S(1)} %collective-permute-done.10), channel_id=1, source_target_pairs={{0,11},{1,0},{2,1},{3,2},{4,3},{5,4},{6,5},{7,6},{8,7},{9,8},{10,9... | collective-permute-start | bytes 589832 | tf_op jit(solution)/shard_map/ppermute | solution.py:72
  104.2 4.7 %collective-permute-done.11 = bf16[48,2048]{1,0:T(8,128)(2,1)S(1)} collective-permute-done((bf16[48,2048]{1,0:T(8,128)(2,1)S(1)}, bf16[48,2048]{1,0:T(8,128)(2,1)S(1)}, u32[]{:S(2)}, u32[]{:S(2)}) %collective-permute-start.11) | collective-permute-done | bytes 196640 | tf_op jit(solution)/shard_map/ppermute | solution.py:69
  108.9 1.9 collective-permute-start.13
  110.9 5.1 %collective-permute-start.14 = (bf16[48,2048]{1,0:T(8,128)(2,1)S(1)}, bf16[48,2048]{1,0:T(8,128)(2,1)S(1)}, u32[]{:S(2)}, u32[]{:S(2)}) collective-permute-start(bf16[48,2048]{1,0:T(8,128)(2,1)S(1)} %collective-permute-done.12), channel_id=1, source_target_pairs={{0,11},{1,0},{2,1},{3,2},{4,3},{5,4},{6,5},{7,6},{8,7},{9,8},{10,9... | collective-permute-start | bytes 589832 | tf_op jit(solution)/shard_map/ppermute | solution.py:72
  116.1 4.3 %collective-permute-done.13 = bf16[48,2048]{1,0:T(8,128)(2,1)S(1)} collective-permute-done((bf16[48,2048]{1,0:T(8,128)(2,1)S(1)}, bf16[48,2048]{1,0:T(8,128)(2,1)S(1)}, u32[]{:S(2)}, u32[]{:S(2)}) %collective-permute-start.13) | collective-permute-done | bytes 196640 | tf_op jit(solution)/shard_map/ppermute | solution.py:69
  120.4 1.9 collective-permute-start.15
  122.4 8.9 %collective-permute-done.15 = bf16[48,2048]{1,0:T(8,128)(2,1)S(1)} collective-permute-done((bf16[48,2048]{1,0:T(8,128)(2,1)S(1)}, bf16[48,2048]{1,0:T(8,128)(2,1)S(1)}, u32[]{:S(2)}, u32[]{:S(2)}) %collective-permute-start.15) | collective-permute-done | bytes 196640 | tf_op jit(solution)/shard_map/ppermute | solution.py:69
  131.3 3.9 %multiply_convert_fusion = bf16[2048,640]{1,0:T(8,128)(2,1)} fusion(bf16[576,2048]{1,0:T(8,128)(2,1)S(1)} %bitcast.51, bf16[576,640]{1,0:T(8,128)(2,1)S(1)} %bitcast.56), kind=kOutput, calls=%fused_computation.1 | convolution fusion | flops 1512570880 | bytes 5718016 | tf_op jit(solution)/shard_map/dot_general | solution.py:83
  135.2 4.7 %all-to-all-start = ((bf16[4,512,640]{2,1,0:T(8,128)(2,1)}), bf16[4,512,640]{2,1,0:T(8,128)(2,1)S(1)}, u32[]{:S(2)}, u32[]{:S(2)}) async-start(bf16[4,512,640]{2,1,0:T(8,128)(2,1)} %bitcast.50), calls=%async_computation.1 | async-start | bytes 5242880 | tf_op jit(solution)/shard_map/all_to_all | solution.py:88
  139.9 4.5 %fusion.14 = f32[576,640]{1,0:T(8,128)S(1)} fusion(bf16[576,2048]{1,0:T(8,128)(2,1)} %bitcast.52, bf16[640,2048]{1,0:T(8,128)(2,1)} %broadcast_select_fusion), kind=kOutput, calls=%fused_computation.110 | convolution fusion | flops 1509949440 | bytes 6455296 | tf_op jit(solution)/shard_map/dot_general | solution.py:93
  146.5 1.9 collective-permute-start.16
  148.5 17.0 %all-to-all-done = bf16[4,512,640]{2,1,0:T(8,128)(2,1)S(1)} async-done(((bf16[4,512,640]{2,1,0:T(8,128)(2,1)}), bf16[4,512,640]{2,1,0:T(8,128)(2,1)S(1)}, u32[]{:S(2)}, u32[]{:S(2)}) %all-to-all-start) | async-done | bytes 2621472 | tf_op jit(solution)/shard_map/all_to_all | solution.py:88
  166.8 6.3 %all-to-all-start.1 = ((bf16[4,128,640]{2,1,0:T(8,128)(2,1)}), bf16[4,128,640]{2,1,0:T(8,128)(2,1)S(1)}, u32[]{:S(2)}, u32[]{:S(2)}) async-start(bf16[4,128,640]{2,1,0:T(8,128)(2,1)} %bitcast.21), calls=%async_computation.2 | async-start | bytes 1310720 | tf_op jit(solution)/shard_map/all_to_all | solution.py:90
  173.1 1.4 fusion.12
  175.8 3.8 %collective-permute-start.5 = (bf16[12,4096]{1,0:T(8,128)(2,1)S(1)}, bf16[12,4096]{1,0:T(8,128)(2,1)S(1)}, u32[]{:S(2)}, u32[]{:S(2)}) collective-permute-start(bf16[12,4096]{1,0:T(8,128)(2,1)S(1)} %constant_dynamic-slice_fusion), channel_id=1, source_target_pairs={{0,12},{12,0},{1,13},{13,1},{2,14},{14,2},{3,15},{15,3},{4,16},{16... | collective-permute-start | bytes 294920 | tf_op jit(solution)/shard_map/ppermute | solution.py:107
  179.6 2.2 %fusion.11 = (bf16[288,640]{1,0:T(8,128)(2,1)}, bf16[288,640]{1,0:T(8,128)(2,1)}) fusion(f32[288,640]{1,0:T(8,128)S(1)} %reshape.46, bf16[288,640]{1,0:T(8,128)(2,1)} %param.4, bf16[288,640]{1,0:T(8,128)(2,1)S(1)} %copy-done.3), kind=kLoop, calls=%fused_computation.19 | loop fusion | flops 2764800 | bytes 2211840 | tf_op jit(solution)/shard_map/convert_element_type | solution.py:103
  181.9 6.9 %all-to-all-done.1 = bf16[4,128,640]{2,1,0:T(8,128)(2,1)S(1)} async-done(((bf16[4,128,640]{2,1,0:T(8,128)(2,1)}), bf16[4,128,640]{2,1,0:T(8,128)(2,1)S(1)}, u32[]{:S(2)}, u32[]{:S(2)}) %all-to-all-start.1) | async-done | bytes 655392 | tf_op jit(solution)/shard_map/all_to_all | solution.py:90
  (95 shorter events, 38.6 us)
Async XLA Ops:
  7.2 167.7 %reduce-scatter.2.cloned.1.call-start = ((), (), s32[]{:S(2)}) async-start(), calls=%async_computation.3 | async-start | bytes 2555904 | tf_op jit(solution)/shard_map/reduce_scatter | solution.py:76
  20.0 20.4 %collective-permute-start.1 = (bf16[12,2048]{1,0:T(8,128)(2,1)S(1)}, bf16[12,2048]{1,0:T(8,128)(2,1)S(1)}, u32[]{:S(2)}, u32[]{:S(2)}) collective-permute-start(bf16[12,2048]{1,0:T(8,128)(2,1)S(1)} %get-tuple-element.75), channel_id=1, source_target_pairs={{0,24},{24,0},{1,25},{25,1},{2,26},{26,2},{3,27},{27,3},{4,28},{28... | collective-permute-start | bytes 147464 | tf_op jit(solution)/shard_map/ppermute | solution.py:33
  21.9 18.5 %collective-permute-start.2 = (bf16[12,2048]{1,0:T(8,128)(2,1)S(1)}, bf16[12,2048]{1,0:T(8,128)(2,1)S(1)}, u32[]{:S(2)}, u32[]{:S(2)}) collective-permute-start(bf16[12,2048]{1,0:T(8,128)(2,1)S(1)} %get-tuple-element.75), channel_id=1, source_target_pairs={{0,36},{12,24},{24,12},{36,0},{1,37},{13,25},{25,13},{37,1},{2,38}... | collective-permute-start | bytes 147464 | tf_op jit(solution)/shard_map/ppermute | solution.py:35
  25.5 11.6 %copy-start = (bf16[640,4096]{1,0:T(8,128)(2,1)S(1)}, bf16[640,4096]{1,0:T(8,128)(2,1)}, u32[]{:S(2)}) copy-start(bf16[640,4096]{1,0:T(8,128)(2,1)} %param.6) | copy-start | bytes 15728644
  25.5 14.9 %collective-permute-start = (bf16[12,2048]{1,0:T(8,128)(2,1)S(1)}, bf16[12,2048]{1,0:T(8,128)(2,1)S(1)}, u32[]{:S(2)}, u32[]{:S(2)}) collective-permute-start(bf16[12,2048]{1,0:T(8,128)(2,1)S(1)} %get-tuple-element.74), channel_id=1, source_target_pairs={{0,12},{12,0},{1,13},{13,1},{2,14},{14,2},{3,15},{15,3},{4,16},{16... | collective-permute-start | bytes 147464 | tf_op jit(solution)/shard_map/ppermute | solution.py:34
  38.2 1.8 copy-start.3
  38.2 1.8 copy-start.4
  41.5 38.8 %collective-permute-start.8 = (bf16[288,640]{1,0:T(8,128)(2,1)}, bf16[288,640]{1,0:T(8,128)(2,1)}, u32[]{:S(2)}, u32[]{:S(2)}) collective-permute-start(bf16[288,640]{1,0:T(8,128)(2,1)} %reshape.39), channel_id=1, source_target_pairs={{0,24},{24,0},{1,25},{25,1},{2,26},{26,2},{3,27},{27,3},{4,28},{28... | collective-permute-start | bytes 1105928 | tf_op jit(solution)/shard_map/ppermute | solution.py:54
  49.5 20.2 %collective-permute-start.3 = (bf16[48,2048]{1,0:T(8,128)(2,1)S(1)}, bf16[48,2048]{1,0:T(8,128)(2,1)}, u32[]{:S(2)}, u32[]{:S(2)}) collective-permute-start(bf16[48,2048]{1,0:T(8,128)(2,1)S(1)} %pad_maximum_fusion.1), channel_id=1, source_target_pairs={{0,1},{1,2},{2,3},{3,4},{4,5},{5,6},{6,7},{7,8},{8,9},{9,10},{10,1... | collective-permute-start | bytes 589832 | tf_op jit(solution)/shard_map/ppermute | solution.py:69
  53.7 17.0 %collective-permute-start.4 = (bf16[48,2048]{1,0:T(8,128)(2,1)S(1)}, bf16[48,2048]{1,0:T(8,128)(2,1)}, u32[]{:S(2)}, u32[]{:S(2)}) collective-permute-start(bf16[48,2048]{1,0:T(8,128)(2,1)S(1)} %pad_maximum_fusion.1), channel_id=1, source_target_pairs={{0,11},{1,0},{2,1},{3,2},{4,3},{5,4},{6,5},{7,6},{8,7},{9,8},{10,9... | collective-permute-start | bytes 589832 | tf_op jit(solution)/shard_map/ppermute | solution.py:72
  67.1 13.2 %copy-start.5 = (bf16[12,24,640]{2,1,0:T(8,128)(2,1)S(1)}, bf16[12,24,640]{2,1,0:T(8,128)(2,1)}, u32[]{:S(2)}) copy-start(bf16[12,24,640]{2,1,0:T(8,128)(2,1)} %reshape_reshape.3) | copy-start | bytes 1105924
  70.8 10.7 %collective-permute-start.6 = (bf16[48,2048]{1,0:T(8,128)(2,1)}, bf16[48,2048]{1,0:T(8,128)(2,1)S(1)}, u32[]{:S(2)}, u32[]{:S(2)}) collective-permute-start(bf16[48,2048]{1,0:T(8,128)(2,1)} %collective-permute-done.3), channel_id=1, source_target_pairs={{0,1},{1,2},{2,3},{3,4},{4,5},{5,6},{6,7},{7,8},{8,9},{9,10},{10,1... | collective-permute-start | bytes 589832 | tf_op jit(solution)/shard_map/ppermute | solution.py:69
  72.7 10.0 %collective-permute-start.7 = (bf16[48,2048]{1,0:T(8,128)(2,1)}, bf16[48,2048]{1,0:T(8,128)(2,1)}, u32[]{:S(2)}, u32[]{:S(2)}) collective-permute-start(bf16[48,2048]{1,0:T(8,128)(2,1)} %collective-permute-done.4), channel_id=1, source_target_pairs={{0,11},{1,0},{2,1},{3,2},{4,3},{5,4},{6,5},{7,6},{8,7},{9,8},{10,9... | collective-permute-start | bytes 589832 | tf_op jit(solution)/shard_map/ppermute | solution.py:72
  82.7 9.1 %collective-permute-start.10 = (bf16[48,2048]{1,0:T(8,128)(2,1)}, bf16[48,2048]{1,0:T(8,128)(2,1)S(1)}, u32[]{:S(2)}, u32[]{:S(2)}) collective-permute-start(bf16[48,2048]{1,0:T(8,128)(2,1)} %collective-permute-done.7), channel_id=1, source_target_pairs={{0,11},{1,0},{2,1},{3,2},{4,3},{5,4},{6,5},{7,6},{8,7},{9,8},{10,9... | collective-permute-start | bytes 589832 | tf_op jit(solution)/shard_map/ppermute | solution.py:72
  88.3 8.8 %collective-permute-start.9 = (bf16[48,2048]{1,0:T(8,128)(2,1)S(1)}, bf16[48,2048]{1,0:T(8,128)(2,1)S(1)}, u32[]{:S(2)}, u32[]{:S(2)}) collective-permute-start(bf16[48,2048]{1,0:T(8,128)(2,1)S(1)} %collective-permute-done.6), channel_id=1, source_target_pairs={{0,1},{1,2},{2,3},{3,4},{4,5},{5,6},{6,7},{7,8},{8,9},{9,10},{10,1... | collective-permute-start | bytes 589832 | tf_op jit(solution)/shard_map/ppermute | solution.py:69
  97.1 11.8 %collective-permute-start.11 = (bf16[48,2048]{1,0:T(8,128)(2,1)S(1)}, bf16[48,2048]{1,0:T(8,128)(2,1)S(1)}, u32[]{:S(2)}, u32[]{:S(2)}) collective-permute-start(bf16[48,2048]{1,0:T(8,128)(2,1)S(1)} %collective-permute-done.9), channel_id=1, source_target_pairs={{0,1},{1,2},{2,3},{3,4},{4,5},{5,6},{6,7},{7,8},{8,9},{9,10},{10,1... | collective-permute-start | bytes 589832 | tf_op jit(solution)/shard_map/ppermute | solution.py:69
  99.7 11.1 %collective-permute-start.12 = (bf16[48,2048]{1,0:T(8,128)(2,1)S(1)}, bf16[48,2048]{1,0:T(8,128)(2,1)S(1)}, u32[]{:S(2)}, u32[]{:S(2)}) collective-permute-start(bf16[48,2048]{1,0:T(8,128)(2,1)S(1)} %collective-permute-done.10), channel_id=1, source_target_pairs={{0,11},{1,0},{2,1},{3,2},{4,3},{5,4},{6,5},{7,6},{8,7},{9,8},{10,9... | collective-permute-start | bytes 589832 | tf_op jit(solution)/shard_map/ppermute | solution.py:72
  108.9 11.4 %collective-permute-start.13 = (bf16[48,2048]{1,0:T(8,128)(2,1)S(1)}, bf16[48,2048]{1,0:T(8,128)(2,1)S(1)}, u32[]{:S(2)}, u32[]{:S(2)}) collective-permute-start(bf16[48,2048]{1,0:T(8,128)(2,1)S(1)} %collective-permute-done.11), channel_id=1, source_target_pairs={{0,1},{1,2},{2,3},{3,4},{4,5},{5,6},{6,7},{7,8},{8,9},{9,10},{10,1... | collective-permute-start | bytes 589832 | tf_op jit(solution)/shard_map/ppermute | solution.py:69
  110.9 11.5 %collective-permute-start.14 = (bf16[48,2048]{1,0:T(8,128)(2,1)S(1)}, bf16[48,2048]{1,0:T(8,128)(2,1)S(1)}, u32[]{:S(2)}, u32[]{:S(2)}) collective-permute-start(bf16[48,2048]{1,0:T(8,128)(2,1)S(1)} %collective-permute-done.12), channel_id=1, source_target_pairs={{0,11},{1,0},{2,1},{3,2},{4,3},{5,4},{6,5},{7,6},{8,7},{9,8},{10,9... | collective-permute-start | bytes 589832 | tf_op jit(solution)/shard_map/ppermute | solution.py:72
  120.4 10.9 %collective-permute-start.15 = (bf16[48,2048]{1,0:T(8,128)(2,1)S(1)}, bf16[48,2048]{1,0:T(8,128)(2,1)S(1)}, u32[]{:S(2)}, u32[]{:S(2)}) collective-permute-start(bf16[48,2048]{1,0:T(8,128)(2,1)S(1)} %collective-permute-done.13), channel_id=1, source_target_pairs={{0,1},{1,2},{2,3},{3,4},{4,5},{5,6},{6,7},{7,8},{8,9},{9,10},{10,1... | collective-permute-start | bytes 589832 | tf_op jit(solution)/shard_map/ppermute | solution.py:69
  131.3 3.9 %copy-start.1 = (bf16[12,48,2048]{2,1,0:T(8,128)(2,1)}, bf16[12,48,2048]{2,1,0:T(8,128)(2,1)S(1)}, u32[]{:S(2)}) copy-start(bf16[12,48,2048]{2,1,0:T(8,128)(2,1)S(1)} %bitcast_dynamic-update-slice_fusion) | copy-start | bytes 7077892
  135.2 30.2 %all-to-all-start = ((bf16[4,512,640]{2,1,0:T(8,128)(2,1)}), bf16[4,512,640]{2,1,0:T(8,128)(2,1)S(1)}, u32[]{:S(2)}, u32[]{:S(2)}) async-start(bf16[4,512,640]{2,1,0:T(8,128)(2,1)} %bitcast.50), calls=%async_computation.1 | async-start | bytes 5242880 | tf_op jit(solution)/shard_map/all_to_all | solution.py:88
  144.4 1.2 copy-start.2
  146.5 26.6 %collective-permute-start.16 = (f32[12,24,640]{2,1,0:T(8,128)}, f32[12,24,640]{2,1,0:T(8,128)}, u32[]{:S(2)}, u32[]{:S(2)}) collective-permute-start(f32[12,24,640]{2,1,0:T(8,128)} %slice_bitcast_fusion), channel_id=1, source_target_pairs={{0,24},{24,0},{1,25},{25,1},{2,26},{26,2},{3,27},{27,3},{4,28},{28... | collective-permute-start | bytes 2211848 | tf_op jit(solution)/shard_map/ppermute | solution.py:96
  166.8 21.9 %all-to-all-start.1 = ((bf16[4,128,640]{2,1,0:T(8,128)(2,1)}), bf16[4,128,640]{2,1,0:T(8,128)(2,1)S(1)}, u32[]{:S(2)}, u32[]{:S(2)}) async-start(bf16[4,128,640]{2,1,0:T(8,128)(2,1)} %bitcast.21), calls=%async_computation.2 | async-start | bytes 1310720 | tf_op jit(solution)/shard_map/all_to_all | solution.py:90
  174.8 14.8 %copy-start.6 = (bf16[24,4096]{1,0:T(8,128)(2,1)S(1)}, bf16[24,4096]{1,0:T(8,128)(2,1)}, u32[]{:S(2)}) copy-start(bf16[24,4096]{1,0:T(8,128)(2,1)} %reduce-scatter.2.cloned.1.call-done) | copy-start | bytes 589828
  175.8 13.8 %collective-permute-start.5 = (bf16[12,4096]{1,0:T(8,128)(2,1)S(1)}, bf16[12,4096]{1,0:T(8,128)(2,1)S(1)}, u32[]{:S(2)}, u32[]{:S(2)}) collective-permute-start(bf16[12,4096]{1,0:T(8,128)(2,1)S(1)} %constant_dynamic-slice_fusion), channel_id=1, source_target_pairs={{0,12},{12,0},{1,13},{13,1},{2,14},{14,2},{3,15},{15,3},{4,16},{16... | collective-permute-start | bytes 294920 | tf_op jit(solution)/shard_map/ppermute | solution.py:107
Sparse Core Ops, SparseCore 0:
  78.5 62.4 reduce-scatter.1

commit v2 on v1

v2 whole, which is shorter than its diff:
```python
import jax
import jax.numpy as jnp
from jax import lax
from jax.experimental import pallas as pl
from jax.experimental.pallas import tpu as pltpu
from jax.sharding import Mesh, PartitionSpec as P

NX, NYH, NC, NYL, NZ = 4, 4, 2, 2, 12
CHUNKS = 2
PER = NYH // CHUNKS
BF, F32 = jnp.bfloat16, jnp.float32
SWAP = [(0, 1), (1, 0)]
tie = lax.optimization_barrier


def source_block(slot):
    chunk, rest = slot // (NX * PER), slot % (NX * PER)
    return (rest // PER) * NYH + chunk * PER + rest % PER


def split_kernel(core_ref, cot_ref, mine_ref, other_ref):
    lane = mine_ref.shape[1] // (NX * NYH)
    zero = core_ref[0] == 0
    for slot in range(NX * NYH):
        at = source_block(slot) * NC * lane
        even = cot_ref[:, at : at + lane]
        odd = cot_ref[:, at + lane : at + NC * lane]
        mine_ref[:, slot * lane : (slot + 1) * lane] = jnp.where(zero, even, odd)
        other_ref[:, slot * lane : (slot + 1) * lane] = jnp.where(zero, odd, even)


def split_columns(core, cot):
    rows, feat = cot.shape
    shape = jax.ShapeDtypeStruct((rows, feat // NC), cot.dtype)
    return pl.pallas_call(
        split_kernel,
        out_shape=(shape, shape),
        in_specs=[
            pl.BlockSpec(memory_space=pltpu.SMEM),
            pl.BlockSpec(memory_space=pltpu.VMEM),
        ],
        out_specs=(pl.BlockSpec(memory_space=pltpu.VMEM),) * 2,
        name="split_columns",
    )(core.reshape(1), cot)


def half_kernel(core_ref, a_ref, b_ref, out_ref):
    lane = a_ref.shape[1]
    out_ref[:, :lane] = a_ref[...]
    out_ref[:, lane:] = b_ref[...]


def half_weight(core, weight):
    ff, feat = weight.shape
    lane = feat // (NX * NYH * NC)
    pick = lambda k: pl.BlockSpec(
        (ff, lane), lambda i, core_ref: (0, source_block(2 * i + k) * NC + core_ref[0])
    )
    return pl.pallas_call(
        half_kernel,
        out_shape=jax.ShapeDtypeStruct((ff, feat // NC), weight.dtype),
        grid_spec=pltpu.PrefetchScalarGridSpec(
            num_scalar_prefetch=1,
            grid=(NX * NYH // 2,),
            in_specs=[pick(0), pick(1)],
            out_specs=pl.BlockSpec((ff, 2 * lane), lambda i, core_ref: (0, i)),
        ),
        name="half_weight",
    )(core.reshape(1), weight, weight)


def per_device(gate_pre, up_pre, down_weight, cotangent):
    tok, ff = gate_pre.shape
    rows, feat = cotangent.shape
    half = feat // NC
    width = half // CHUNKS
    lane = half // (NX * NYH)
    core, yl = lax.axis_index("c"), lax.axis_index("yl")
    first = yl == 0

    mine, other = split_columns(core, cotangent)
    from_core = lax.ppermute(other, "c", SWAP)

    gate_wide = gate_pre.astype(F32)
    up_wide = up_pre.astype(F32)
    sig = jax.nn.sigmoid(gate_wide)
    act = gate_wide * sig
    hidden = (act * up_wide).astype(BF)
    hidden_z = hidden.reshape(NYL, NZ, rows, ff).transpose(1, 0, 2, 3)
    hidden_z, from_core = tie((hidden_z, from_core))
    partial = jnp.dot(hidden_z.reshape(tok, ff), down_weight, preferred_element_type=F32).astype(BF)
    partial, from_core, hidden_z = tie((partial, from_core, hidden_z))
    out_z = lax.psum_scatter(partial, "z", scatter_dimension=0, tiled=True)
    hidden_peer = lax.ppermute(hidden_z, "c", SWAP)

    shard = jnp.concatenate([mine, from_core], axis=0)
    w_half = half_weight(core, down_weight)
    own = [None] * CHUNKS
    theirs = [None] * CHUNKS
    for k in range(CHUNKS):
        piece = shard[:, k * width : (k + 1) * width]
        if k:
            piece, own[k - 1] = tie((piece, own[k - 1]))
        own[k] = lax.all_gather(piece, "z", axis=0, tiled=True)
        theirs[k] = lax.ppermute(own[k], "yl", SWAP)

    pair = jnp.stack([hidden_z, hidden_peer], axis=2)
    low, high = pair[:, 0], pair[:, 1]
    hidden_both = jnp.stack(
        [jnp.where(first, low, high), jnp.where(first, high, low)], axis=0
    ).reshape(NC * tok, ff)

    back_part = 0.0
    sums = []
    for k in range(CHUNKS):
        cot_k = jnp.concatenate([own[k], theirs[k]], axis=0)
        grad_acc = lax.dot_general(
            cot_k, hidden_both, (((0,), (0,)), ((), ())), preferred_element_type=F32
        )
        term = (grad_acc / (NX * NYH * NC)).astype(BF).reshape(NX, PER * lane, ff)
        term, cot_k, gate_pre, up_pre = tie((term, cot_k, gate_pre, up_pre))
        by_x = lax.all_to_all(term, "x", 0, 0)
        back_part = back_part + lax.dot_general(
            cot_k,
            w_half[:, k * width : (k + 1) * width],
            (((1,), (1,)), ((), ())),
            preferred_element_type=F32,
        )
        sums.append(by_x.astype(F32).sum(0).astype(BF).reshape(PER, lane, ff))
    by_y = lax.all_to_all(jnp.concatenate(sums, axis=0), "yh", 0, 0)
    weight_grad = by_y.astype(F32).sum(0).astype(BF).T

    back_part = back_part.reshape(NYL, NZ, NC, rows, ff)
    back = back_part[:, :, 0].reshape(tok, ff)
    back = back + lax.ppermute(back_part[:, :, 1].reshape(tok, ff), "c", SWAP)
    near, far = back[: tok // NYL], back[tok // NYL :]
    back = jnp.concatenate([jnp.where(first, near, far), jnp.where(first, far, near)], axis=0)
    gate_wide = gate_pre.astype(F32)
    up_wide = up_pre.astype(F32)
    sig = jax.nn.sigmoid(gate_wide)
    act = gate_wide * sig
    gate_grad = (back * up_wide * sig * (1.0 + gate_wide * (1.0 - sig))).astype(BF)
    up_grad = (back * act).astype(BF)

    keep = lax.dynamic_slice_in_dim(out_z, yl * rows, rows, 0)
    give = lax.dynamic_slice_in_dim(out_z, (1 - yl) * rows, rows, 0)
    got = lax.ppermute(give, "yl", SWAP)
    output = (keep.astype(F32) + got.astype(F32)).astype(BF)
    return output, gate_grad, up_grad, weight_grad


def solution(mesh):
    fine = Mesh(
        mesh.devices.reshape(NX, NYH, NC, NYL, NZ), ("x", "yh", "c", "yl", "z")
    )
    dp, tensor = ("x", "yh", "c"), ("yl", "z")
    return jax.shard_map(
        per_device,
        mesh=fine,
        in_specs=(P(dp, tensor), P(dp, tensor), P(tensor, None), P(dp + tensor, None)),
        out_specs=(P(dp + tensor, None), P(dp, tensor), P(dp, tensor), P(tensor, dp)),
        check_vma=False,
    )
```

time: 199 us -> 171 us (0.86)
  blocking collectives: 0 us -> 62.5 us
  starting transfers between devices: 74.4 us -> 33.2 us
  waiting for transfers between devices: 52.7 us -> 15.1 us
  local copies, waits for them, and re-layouts: 31.9 us -> 10.5 us
  Pallas kernels: 0 us -> 7.83 us
  matrix products: 14.5 us -> 18.5 us
    all_gather x0 -> x2, blocking collectives: none -> 62.5 us  [per_device(): own[k] = lax.all_gather(piece, 'z', axis=0, tiled=True)]
    ppermute x17 -> x6, starting transfers between devices: 63.4 us -> 15.8 us  [the longest x2 7.15 us: per_device(): theirs[k] = lax.ppermute(own[k], 'yl', SWAP)]
    ppermute x17 -> x6, waiting for transfers between devices: 28.8 us -> 0.02 us  [the longest x2 0.01 us: per_device(): theirs[k] = lax.ppermute(own[k], 'yl', SWAP)]
    unnamed x46 -> x17, local copies, waits for them, and re-layouts: 23.1 us -> 1.73 us
    all_to_all x1 -> x2, waiting for transfers between devices: 17 us -> 0.47 us  [per_device(): by_x = lax.all_to_all(term, 'x', 0, 0)]
    pallas_call x0 -> x2, Pallas kernels: none -> 7.83 us  [the longest x1 6.25 us: half_weight(): pl.pallas_call(half_kernel, out_shape=jax.ShapeDtypeStruct((ff, feat // N...]
    all_to_all x1, waiting for transfers between devices: 6.87 us -> 14.6 us  [per_device(): by_y = lax.all_to_all(jnp.concatenate(sums, axis=0), 'yh', 0, 0)]
    all_to_all x1 -> x2, starting transfers between devices: 4.69 us -> 10.3 us  [per_device(): by_x = lax.all_to_all(term, 'x', 0, 0)]
  transfers between devices with their start and end apart: 20 -> 10, of which waited for: 10 -> 2; matrix products, arithmetic and copies ran while one was open for 20% -> 18% of each run, Pallas kernels for 0% -> 4%
where the time goes in v2:
time: 171 us; the launch traced here: 170 us
  blocking collectives  62.5 us (37%)
  starting transfers between devices  33.2 us (19%)
  matrix products  18.5 us (11%)
  waiting for transfers between devices  15.1 us (9%)
  between operations  14.3 us (8%)
  local copies, waits for them, and re-layouts  10.5 us (6%)
  other arithmetic  8.08 us (5%)
  Pallas kernels  7.83 us (5%)
    all_gather x2, blocking collectives, per_device(): own[k] = lax.all_gather(piece, 'z', axis=0, tiled=True)  62.5 us
    all_to_all x1, waiting for transfers between devices, per_device(): by_y = lax.all_to_all(jnp.concatenate(sums, axis=0), 'yh', 0, 0)  14.6 us
    all_to_all x2, starting transfers between devices, per_device(): by_x = lax.all_to_all(term, 'x', 0, 0)  10.3 us
    ppermute x2, starting transfers between devices, per_device(): theirs[k] = lax.ppermute(own[k], 'yl', SWAP)  7.15 us
    all_to_all x1, starting transfers between devices, per_device(): by_y = lax.all_to_all(jnp.concatenate(sums, axis=0), 'yh', 0, 0)  7 us
    dot_general x2, matrix products, per_device(): lax.dot_general(cot_k, w_half[:, k * width:(k + 1) * width], (((1,), (1,)...  6.33 us
    pallas_call x1, Pallas kernels, half_weight(): pl.pallas_call(half_kernel, out_shape=jax.ShapeDtypeStruct((ff, feat // N...  6.25 us
    dot_general x2, matrix products, per_device(): lax.dot_general(cot_k, hidden_both, (((0,), (0,)), ((), ())), preferred_e...  6.2 us
  transfers between devices with their start and end apart: 10, of which 2 were waited for; matrix products, arithmetic and copies ran while one was open for 18% of the time, Pallas kernels for 4%

profile of v2, /device:TPU:2, one launch (start us, length us, event | category | flops | bytes accessed | tf_op | source)
XLA Modules:
  0.0 170.0 jit_solution(6582545556015331266)
XLA Ops:
  7.2 1.6 split_columns.1
  8.8 1.9 %collective-permute-start = (bf16[12,2048]{1,0:T(8,128)(2,1)}, bf16[12,2048]{1,0:T(8,128)(2,1)S(1)}, u32[]{:S(2)}, u32[]{:S(2)}) collective-permute-start(bf16[12,2048]{1,0:T(8,128)(2,1)} %get-tuple-element.21), channel_id=1, source_target_pairs={{0,24},{24,0},{1,25},{25,1},{2,26},{26,2},{3,27},{27,3},{4,28},{28... | collective-permute-start | bytes 147464 | tf_op jit(solution)/shard_map/ppermute | solution.py:82
  10.7 1.3 fusion.15
  12.3 5.9 %convolution_convert_fusion = bf16[288,4096]{1,0:T(8,128)(2,1)} fusion(bf16[288,640]{1,0:T(8,128)(2,1)S(1)} %reshape.76, bf16[640,4096]{1,0:T(8,128)(2,1)} %b_ref.1), kind=kOutput, calls=%fused_computation | convolution fusion | flops 1511129088 | bytes 7970816 | tf_op jit(solution)/shard_map/dot_general | solution.py:91
  18.3 2.4 %collective-permute-start.3 = (bf16[12,2,12,640]{3,2,0,1:T(8,128)(2,1)S(1)}, bf16[12,2,12,640]{3,2,0,1:T(8,128)(2,1)S(1)}, u32[]{:S(2)}, u32[]{:S(2)}) collective-permute-start(bf16[12,2,12,640]{3,2,0,1:T(8,128)(2,1)S(1)} %bitcast.34), channel_id=1, source_target_pairs={{0,24},{24,0},{1,25},{25,1},{2,26},{26,2},{3,27},{27,3},{4,28},{28... | collective-permute-start | bytes 1105928 | tf_op jit(solution)/shard_map/ppermute | solution.py:94
  20.7 37.3 %all_gather.6 = bf16[288,1024]{1,0:T(8,128)(2,1)S(1)} all-gather(bf16[24,1024]{1,0:T(8,128)(2,1)S(1)} %get-tuple-element.48), channel_id=1, replica_groups=mesh['x'=4,'yh'=4,'c'=2,'yl'=2,'z'=12] {'z'}, dimensions={0}, use_global_device_ids=true | all-gather | bytes 638976 | tf_op jit(solution)/shard_map/all_gather | solution.py:104
  58.0 3.5 %collective-permute-start.2 = (bf16[288,1024]{1,0:T(8,128)(2,1)S(1)}, bf16[288,1024]{1,0:T(8,128)(2,1)}, u32[]{:S(2)}, u32[]{:S(2)}) collective-permute-start(bf16[288,1024]{1,0:T(8,128)(2,1)S(1)} %all_gather.6), channel_id=1, source_target_pairs={{0,12},{12,0},{1,13},{13,1},{2,14},{14,2},{3,15},{15,3},{4,16},{16... | collective-permute-start | bytes 1769480 | tf_op jit(solution)/shard_map/ppermute | solution.py:105
  61.5 25.3 %all_gather.7 = bf16[288,1024]{1,0:T(8,128)(2,1)S(1)} all-gather(bf16[24,1024]{1,0:T(8,128)(2,1)S(1)} %get-tuple-element.30), channel_id=1, replica_groups=mesh['x'=4,'yh'=4,'c'=2,'yl'=2,'z'=12] {'z'}, dimensions={0}, use_global_device_ids=true | all-gather | bytes 638976 | tf_op jit(solution)/shard_map/all_gather | solution.py:104
  86.8 3.6 %collective-permute-start.4 = (bf16[288,1024]{1,0:T(8,128)(2,1)S(1)}, bf16[288,1024]{1,0:T(8,128)(2,1)}, u32[]{:S(2)}, u32[]{:S(2)}) collective-permute-start(bf16[288,1024]{1,0:T(8,128)(2,1)S(1)} %all_gather.7), channel_id=1, source_target_pairs={{0,12},{12,0},{1,13},{13,1},{2,14},{14,2},{3,15},{15,3},{4,16},{16... | collective-permute-start | bytes 1769480 | tf_op jit(solution)/shard_map/ppermute | solution.py:105
  90.4 0.8 constant_dynamic-update-slice_fusion.1
  92.1 1.9 %constant_dynamic-update-slice_fusion = bf16[576,1024]{1,0:T(8,128)(2,1)} fusion(bf16[576,1024]{1,0:T(8,128)(2,1)} %constant_dynamic-update-slice_fusion.1, bf16[288,1024]{1,0:T(8,128)(2,1)} %collective-permute-done.2), kind=kLoop, calls=%fused_computation.43 | loop fusion | bytes 1179648 | tf_op jit(solution)/shard_map/concatenate | solution.py:116
  94.0 3.8 %multiply_convert_fusion.1 = bf16[1024,640]{1,0:T(8,128)(2,1)} fusion(bf16[576,1024]{1,0:T(8,128)(2,1)} %constant_dynamic-update-slice_fusion, bf16[576,640]{1,0:T(8,128)(2,1)S(1)} %reshape.77), kind=kOutput, calls=%fused_computation.2 | convolution fusion | flops 756285440 | bytes 3227648 | tf_op jit(solution)/shard_map/dot_general | solution.py:117
  97.8 5.4 %all-to-all-start = ((bf16[4,256,640]{2,1,0:T(8,128)(2,1)}), bf16[4,256,640]{2,1,0:T(8,128)(2,1)S(1)}, u32[]{:S(2)}, u32[]{:S(2)}) async-start(bf16[4,256,640]{2,1,0:T(8,128)(2,1)} %bitcast.9), calls=%async_computation.1 | async-start | bytes 2621440 | tf_op jit(solution)/shard_map/all_to_all | solution.py:122
  103.2 6.3 %half_weight.1 = bf16[640,2048]{1,0:T(8,128)(2,1)} custom-call(s32[1]{0:T(128)} %bitcast.1.core_ref, bf16[640,4096]{1,0:T(8,128)(2,1)} %b_ref.1, bf16[640,4096]{1,0:T(8,128)(2,1)} %b_ref.1), custom_call_target="tpu_custom_call" | custom-call | tf_op jit(solution)/shard_map/half_weight/pallas_call | solution.py:59
  109.5 1.1 constant_dynamic-update-slice_fusion.2
  110.7 2.4 %multiply_convert_fusion = bf16[1024,640]{1,0:T(8,128)(2,1)} fusion(bf16[576,1024]{1,0:T(8,128)(2,1)S(1)} %constant_dynamic-update-slice_fusion.2, bf16[576,640]{1,0:T(8,128)(2,1)S(1)} %reshape.77), kind=kOutput, calls=%fused_computation.1 | convolution fusion | flops 756285440 | bytes 3227648 | tf_op jit(solution)/shard_map/dot_general | solution.py:117
  113.1 2.3 %fusion = f32[576,640]{1,0:T(8,128)} fusion(bf16[576,1024]{1,0:T(8,128)(2,1)S(1)} %constant_dynamic-update-slice_fusion.2, bf16[640,2048]{1,0:T(8,128)(2,1)S(1)} %copy-done.1), kind=kOutput, calls=%fused_computation.4 | convolution fusion | flops 754974720 | bytes 3964928 | tf_op jit(solution)/shard_map/dot_general | solution.py:123
  115.4 4.9 %all-to-all-start.1 = ((bf16[4,256,640]{2,1,0:T(8,128)(2,1)}), bf16[4,256,640]{2,1,0:T(8,128)(2,1)}, u32[]{:S(2)}, u32[]{:S(2)}) async-start(bf16[4,256,640]{2,1,0:T(8,128)(2,1)} %bitcast.10), calls=%async_computation.2 | async-start | bytes 2621440 | tf_op jit(solution)/shard_map/all_to_all | solution.py:122
  120.3 4.0 %convolution_add_fusion = f32[576,640]{1,0:T(8,128)} fusion(f32[576,640]{1,0:T(8,128)} %fusion, bf16[576,1024]{1,0:T(8,128)(2,1)S(1)} %copy-done.5, bf16[640,2048]{1,0:T(8,128)(2,1)} %half_weight.1), kind=kOutput, calls=%fused_computation.3 | convolution fusion | flops 755343360 | bytes 5439488 | tf_op jit(solution)/shard_map/dot_general | solution.py:123
  124.4 1.4 reshape.80
  125.8 1.5 fusion.20
  127.2 1.3 reshape_squeeze.7
  128.5 1.9 %collective-permute-start.5 = (f32[288,640]{1,0:T(8,128)S(1)}, f32[288,640]{1,0:T(8,128)}, u32[]{:S(2)}, u32[]{:S(2)}) collective-permute-start(f32[288,640]{1,0:T(8,128)S(1)} %reshape_squeeze.7), channel_id=1, source_target_pairs={{0,24},{24,0},{1,25},{25,1},{2,26},{26,2},{3,27},{27,3},{4,28},{28... | collective-permute-start | bytes 2211848 | tf_op jit(solution)/shard_map/ppermute | solution.py:135
  131.3 1.6 reduce_sum.37
  132.9 0.9 pad_maximum_fusion.2
  133.8 7.0 %all-to-all-start.2 = ((bf16[4,128,640]{2,1,0:T(8,128)(2,1)}), bf16[4,128,640]{2,1,0:T(8,128)(2,1)S(1)}, u32[]{:S(2)}, u32[]{:S(2)}) async-start(bf16[4,128,640]{2,1,0:T(8,128)(2,1)} %pad_maximum_fusion.2), calls=%async_computation.3 | async-start | bytes 1310720 | tf_op jit(solution)/shard_map/all_to_all | solution.py:130
  140.9 1.2 add.31
  142.2 1.0 constant_dynamic-slice_fusion
  143.2 2.4 %collective-permute-start.1 = (bf16[12,4096]{1,0:T(8,128)(2,1)S(1)}, bf16[12,4096]{1,0:T(8,128)(2,1)S(1)}, u32[]{:S(2)}, u32[]{:S(2)}) collective-permute-start(bf16[12,4096]{1,0:T(8,128)(2,1)S(1)} %constant_dynamic-slice_fusion), channel_id=1, source_target_pairs={{0,12},{12,0},{1,13},{13,1},{2,14},{14,2},{3,15},{15,3},{4,16},{16... | collective-permute-start | bytes 294920 | tf_op jit(solution)/shard_map/ppermute | solution.py:147
  145.7 1.2 fusion.14
  146.9 14.6 %all-to-all-done.2 = bf16[4,128,640]{2,1,0:T(8,128)(2,1)S(1)} async-done(((bf16[4,128,640]{2,1,0:T(8,128)(2,1)}), bf16[4,128,640]{2,1,0:T(8,128)(2,1)S(1)}, u32[]{:S(2)}, u32[]{:S(2)}) %all-to-all-start.2) | async-done | bytes 655392 | tf_op jit(solution)/shard_map/all_to_all | solution.py:130
  161.6 0.8 copy.24
  (40 shorter events, 2.9 us)
Async XLA Ops:
  7.2 135.1 %reduce-scatter.2.cloned.1.call-start = ((), (), s32[]{:S(2)}) async-start(), calls=%async_computation.4 | async-start | bytes 2555904 | tf_op jit(solution)/shard_map/reduce_scatter | solution.py:93
  8.8 3.4 %collective-permute-start = (bf16[12,2048]{1,0:T(8,128)(2,1)}, bf16[12,2048]{1,0:T(8,128)(2,1)S(1)}, u32[]{:S(2)}, u32[]{:S(2)}) collective-permute-start(bf16[12,2048]{1,0:T(8,128)(2,1)} %get-tuple-element.21), channel_id=1, source_target_pairs={{0,24},{24,0},{1,25},{25,1},{2,26},{26,2},{3,27},{27,3},{4,28},{28... | collective-permute-start | bytes 147464 | tf_op jit(solution)/shard_map/ppermute | solution.py:82
  18.2 2.5 %copy-start.6 = (bf16[12,2048]{1,0:T(8,128)(2,1)S(1)}, bf16[12,2048]{1,0:T(8,128)(2,1)}, u32[]{:S(2)}) copy-start(bf16[12,2048]{1,0:T(8,128)(2,1)} %get-tuple-element.25) | copy-start | bytes 147460
  18.3 73.0 %collective-permute-start.3 = (bf16[12,2,12,640]{3,2,0,1:T(8,128)(2,1)S(1)}, bf16[12,2,12,640]{3,2,0,1:T(8,128)(2,1)S(1)}, u32[]{:S(2)}, u32[]{:S(2)}) collective-permute-start(bf16[12,2,12,640]{3,2,0,1:T(8,128)(2,1)S(1)} %bitcast.34), channel_id=1, source_target_pairs={{0,24},{24,0},{1,25},{25,1},{2,26},{26,2},{3,27},{27,3},{4,28},{28... | collective-permute-start | bytes 1105928 | tf_op jit(solution)/shard_map/ppermute | solution.py:94
  58.0 34.1 %collective-permute-start.2 = (bf16[288,1024]{1,0:T(8,128)(2,1)S(1)}, bf16[288,1024]{1,0:T(8,128)(2,1)}, u32[]{:S(2)}, u32[]{:S(2)}) collective-permute-start(bf16[288,1024]{1,0:T(8,128)(2,1)S(1)} %all_gather.6), channel_id=1, source_target_pairs={{0,12},{12,0},{1,13},{13,1},{2,14},{14,2},{3,15},{15,3},{4,16},{16... | collective-permute-start | bytes 1769480 | tf_op jit(solution)/shard_map/ppermute | solution.py:105
  86.8 22.7 %collective-permute-start.4 = (bf16[288,1024]{1,0:T(8,128)(2,1)S(1)}, bf16[288,1024]{1,0:T(8,128)(2,1)}, u32[]{:S(2)}, u32[]{:S(2)}) collective-permute-start(bf16[288,1024]{1,0:T(8,128)(2,1)S(1)} %all_gather.7), channel_id=1, source_target_pairs={{0,12},{12,0},{1,13},{13,1},{2,14},{14,2},{3,15},{15,3},{4,16},{16... | collective-permute-start | bytes 1769480 | tf_op jit(solution)/shard_map/ppermute | solution.py:105
  97.8 17.6 %all-to-all-start = ((bf16[4,256,640]{2,1,0:T(8,128)(2,1)}), bf16[4,256,640]{2,1,0:T(8,128)(2,1)S(1)}, u32[]{:S(2)}, u32[]{:S(2)}) async-start(bf16[4,256,640]{2,1,0:T(8,128)(2,1)} %bitcast.9), calls=%async_computation.1 | async-start | bytes 2621440 | tf_op jit(solution)/shard_map/all_to_all | solution.py:122
  110.6 2.5 %copy-start.1 = (bf16[640,2048]{1,0:T(8,128)(2,1)S(1)}, bf16[640,2048]{1,0:T(8,128)(2,1)}, u32[]{:S(2)}) copy-start(bf16[640,2048]{1,0:T(8,128)(2,1)} %half_weight.1) | copy-start | bytes 7864324
  115.4 4.9 %copy-start.5 = (bf16[576,1024]{1,0:T(8,128)(2,1)S(1)}, bf16[576,1024]{1,0:T(8,128)(2,1)}, u32[]{:S(2)}) copy-start(bf16[576,1024]{1,0:T(8,128)(2,1)} %constant_dynamic-update-slice_fusion) | copy-start | bytes 3538948
  115.4 15.9 %all-to-all-start.1 = ((bf16[4,256,640]{2,1,0:T(8,128)(2,1)}), bf16[4,256,640]{2,1,0:T(8,128)(2,1)}, u32[]{:S(2)}, u32[]{:S(2)}) async-start(bf16[4,256,640]{2,1,0:T(8,128)(2,1)} %bitcast.10), calls=%async_computation.2 | async-start | bytes 2621440 | tf_op jit(solution)/shard_map/all_to_all | solution.py:122
  128.5 12.4 %collective-permute-start.5 = (f32[288,640]{1,0:T(8,128)S(1)}, f32[288,640]{1,0:T(8,128)}, u32[]{:S(2)}, u32[]{:S(2)}) collective-permute-start(f32[288,640]{1,0:T(8,128)S(1)} %reshape_squeeze.7), channel_id=1, source_target_pairs={{0,24},{24,0},{1,25},{25,1},{2,26},{26,2},{3,27},{27,3},{4,28},{28... | collective-permute-start | bytes 2211848 | tf_op jit(solution)/shard_map/ppermute | solution.py:135
  132.9 7.9 %copy-start = (f32[2,12,1,12,640]{4,3,2,1,0:T(8,128)S(1)}, f32[2,12,1,12,640]{4,3,2,1,0:T(8,128)}, u32[]{:S(2)}) copy-start(f32[2,12,1,12,640]{4,3,2,1,0:T(8,128)} %get-tuple-element.43) | copy-start | bytes 2211844
  133.8 27.7 %all-to-all-start.2 = ((bf16[4,128,640]{2,1,0:T(8,128)(2,1)}), bf16[4,128,640]{2,1,0:T(8,128)(2,1)S(1)}, u32[]{:S(2)}, u32[]{:S(2)}) async-start(bf16[4,128,640]{2,1,0:T(8,128)(2,1)} %pad_maximum_fusion.2), calls=%async_computation.3 | async-start | bytes 1310720 | tf_op jit(solution)/shard_map/all_to_all | solution.py:130
  142.1 3.5 %copy-start.2 = (bf16[288,640]{1,0:T(8,128)(2,1)S(1)}, bf16[288,640]{1,0:T(8,128)(2,1)}, u32[]{:S(2)}) copy-start(bf16[288,640]{1,0:T(8,128)(2,1)} %param.5) | copy-start | bytes 1105924
  142.1 3.5 %copy-start.3 = (bf16[288,640]{1,0:T(8,128)(2,1)S(1)}, bf16[288,640]{1,0:T(8,128)(2,1)}, u32[]{:S(2)}) copy-start(bf16[288,640]{1,0:T(8,128)(2,1)} %param.4) | copy-start | bytes 1105924
  143.2 19.2 %collective-permute-start.1 = (bf16[12,4096]{1,0:T(8,128)(2,1)S(1)}, bf16[12,4096]{1,0:T(8,128)(2,1)S(1)}, u32[]{:S(2)}, u32[]{:S(2)}) collective-permute-start(bf16[12,4096]{1,0:T(8,128)(2,1)S(1)} %constant_dynamic-slice_fusion), channel_id=1, source_target_pairs={{0,12},{12,0},{1,13},{13,1},{2,14},{14,2},{3,15},{15,3},{4,16},{16... | collective-permute-start | bytes 294920 | tf_op jit(solution)/shard_map/ppermute | solution.py:147
  145.7 16.7 %copy-start.4 = (bf16[24,4096]{1,0:T(8,128)(2,1)S(1)}, bf16[24,4096]{1,0:T(8,128)(2,1)}, u32[]{:S(2)}) copy-start(bf16[24,4096]{1,0:T(8,128)(2,1)} %reduce-scatter.2.cloned.1.call-done) | copy-start | bytes 589828
Sparse Core Ops, SparseCore 0:
  18.4 72.6 reduce-scatter.1

commit v3 on v2

v3 whole, which is shorter than its diff:
```python
import jax
import jax.numpy as jnp
from jax import lax
from jax.experimental import pallas as pl
from jax.experimental.pallas import tpu as pltpu
from jax.sharding import Mesh, PartitionSpec as P

NX, NYH, NC, NYL, NZ = 4, 4, 2, 2, 12
LANES = (64, 64)
BF, F32 = jnp.bfloat16, jnp.float32
SWAP = [(0, 1), (1, 0)]
tie = lax.optimization_barrier


def pick_chunk(ref, half, lane, chunk):
    start = sum(LANES[:chunk])
    pieces = []
    for pair in range(NX * NYH):
        at = (pair * NC + half) * lane
        pieces.append(ref[:, at : at + lane][:, start : start + LANES[chunk]])
    return jnp.concatenate(pieces, axis=1)


def split_kernel(core_ref, cot_ref, *out_refs):
    lane = cot_ref.shape[1] // (NX * NYH * NC)
    mine_refs, other_refs = out_refs[: len(LANES)], out_refs[len(LANES) :]
    for core in range(NC):

        @pl.when(core_ref[0] == core)
        def _():
            for chunk in range(len(LANES)):
                mine_refs[chunk][...] = pick_chunk(cot_ref, core, lane, chunk)
                other_refs[chunk][...] = pick_chunk(cot_ref, 1 - core, lane, chunk)


def split_columns(core, cot):
    rows, feat = cot.shape
    shapes = [jax.ShapeDtypeStruct((rows, NX * NYH * n), cot.dtype) for n in LANES]
    vmem = pl.BlockSpec(memory_space=pltpu.VMEM)
    outs = pl.pallas_call(
        split_kernel,
        out_shape=shapes * 2,
        in_specs=[pl.BlockSpec(memory_space=pltpu.SMEM), vmem],
        out_specs=[vmem] * (2 * len(LANES)),
        name="split_columns",
    )(core.reshape(1), cot)
    return outs[: len(LANES)], outs[len(LANES) :]


def half_kernel(core_ref, weight_ref, *out_refs):
    lane = weight_ref.shape[1] // (NX * NYH * NC)
    for core in range(NC):

        @pl.when(core_ref[0] == core)
        def _():
            for chunk, out_ref in enumerate(out_refs):
                out_ref[...] = pick_chunk(weight_ref, core, lane, chunk)


def half_weight(core, weight):
    ff, feat = weight.shape
    step = 128
    return pl.pallas_call(
        half_kernel,
        out_shape=[jax.ShapeDtypeStruct((ff, NX * NYH * n), weight.dtype) for n in LANES],
        grid=(ff // step,),
        in_specs=[
            pl.BlockSpec(memory_space=pltpu.SMEM),
            pl.BlockSpec((step, feat), lambda i: (i, 0)),
        ],
        out_specs=[pl.BlockSpec((step, NX * NYH * n), lambda i: (i, 0)) for n in LANES],
        name="half_weight",
    )(core.reshape(1), weight)


def scatter_sum(terms, axis):
    size = terms.shape[0]
    me = lax.axis_index(axis)
    total = lax.dynamic_index_in_dim(terms, me, 0, False).astype(F32)
    for by in (1, size - 1, 2):
        to = lax.rem(me + by, size)
        pairs = [(i, (i + by) % size) for i in range(size)]
        piece = lax.dynamic_index_in_dim(terms, to, 0, False)
        total = total + lax.ppermute(piece, axis, pairs).astype(F32)
    return total.astype(BF)


def per_device(gate_pre, up_pre, down_weight, cotangent):
    tok, ff = gate_pre.shape
    rows, feat = cotangent.shape
    core, yl = lax.axis_index("c"), lax.axis_index("yl")
    first = yl == 0
    part = tok // NYL

    mine, other = split_columns(core, cotangent)
    from_core = lax.ppermute(jnp.concatenate(other, axis=1), "c", SWAP)

    gate_wide = gate_pre.astype(F32)
    up_wide = up_pre.astype(F32)
    sig = jax.nn.sigmoid(gate_wide)
    act = gate_wide * sig
    hidden = (act * up_wide).astype(BF)
    hidden, from_core = tie((hidden, from_core))
    partial = jnp.dot(hidden, down_weight, preferred_element_type=F32).astype(BF)
    partial, from_core, hidden = tie((partial, from_core, hidden))
    keep = lax.dynamic_slice_in_dim(partial, yl * part, part, 0)
    give = lax.dynamic_slice_in_dim(partial, (1 - yl) * part, part, 0)
    got = lax.ppermute(give, "yl", SWAP)
    hidden_peer = lax.ppermute(hidden, "c", SWAP)

    own, theirs = [], []
    for k, n in enumerate(LANES):
        start = NX * NYH * sum(LANES[:k])
        piece = jnp.concatenate([mine[k], from_core[:, start : start + NX * NYH * n]], axis=0)
        if k == 1:
            kept = (keep.astype(F32) + got.astype(F32)).astype(BF).reshape(NZ, rows, feat)
            piece, kept, own[0] = tie((piece, kept, own[0]))
            by_z = lax.all_to_all(kept, "z", 0, 0)
        elif k:
            piece, own[k - 1] = tie((piece, own[k - 1]))
        own.append(lax.all_gather(piece, "z", axis=0, tiled=True))
        theirs.append(lax.ppermute(own[k], "yl", SWAP))
    w_half = half_weight(core, down_weight)

    pair = jnp.stack([hidden, hidden_peer]).reshape(NC, NYL, NZ, rows, ff).transpose(1, 2, 0, 3, 4)
    hidden_both = jnp.stack(
        [jnp.where(first, pair[0], pair[1]), jnp.where(first, pair[1], pair[0])]
    ).reshape(NC * tok, ff)

    back_part = 0.0
    grads = []
    for k, n in enumerate(LANES):
        cot_k = jnp.concatenate([own[k], theirs[k]], axis=0)
        grad_acc = lax.dot_general(
            cot_k, hidden_both, (((0,), (0,)), ((), ())), preferred_element_type=F32
        )
        term = (grad_acc / (NX * NYH * NC)).astype(BF).reshape(NX, NYH * n, ff)
        term, cot_k, gate_pre, up_pre = tie((term, cot_k, gate_pre, up_pre))
        if k < len(LANES) - 1:
            sum_x = scatter_sum(term, "x")
        else:
            term, by_z = tie((term, by_z))
            sum_x = lax.all_to_all(term, "x", 0, 0).astype(F32).sum(0).astype(BF)
        back_part = back_part + lax.dot_general(
            cot_k, w_half[k], (((1,), (1,)), ((), ())), preferred_element_type=F32
        )
        sum_x = sum_x.reshape(NYH, n, ff)
        if k < len(LANES) - 1:
            grads.append(scatter_sum(sum_x, "yh"))
        else:
            grads.append(lax.all_to_all(sum_x, "yh", 0, 0).astype(F32).sum(0).astype(BF))
    weight_grad = jnp.concatenate(grads, axis=0).T

    output = by_z.astype(F32).sum(0).astype(BF)

    back_part = back_part.reshape(NYL, NZ, NC, rows, ff)
    back = back_part[:, :, 0].reshape(tok, ff)
    back = back + lax.ppermute(back_part[:, :, 1].reshape(tok, ff), "c", SWAP)
    near, far = back[: tok // NYL], back[tok // NYL :]
    back = jnp.concatenate([jnp.where(first, near, far), jnp.where(first, far, near)], axis=0)
    gate_wide = gate_pre.astype(F32)
    up_wide = up_pre.astype(F32)
    sig = jax.nn.sigmoid(gate_wide)
    act = gate_wide * sig
    gate_grad = (back * up_wide * sig * (1.0 + gate_wide * (1.0 - sig))).astype(BF)
    up_grad = (back * act).astype(BF)

    return output, gate_grad, up_grad, weight_grad


def solution(mesh):
    fine = Mesh(
        mesh.devices.reshape(NX, NYH, NC, NYL, NZ), ("x", "yh", "c", "yl", "z")
    )
    dp, tensor = ("x", "yh", "c"), ("yl", "z")
    return jax.shard_map(
        per_device,
        mesh=fine,
        in_specs=(P(dp, tensor), P(dp, tensor), P(tensor, None), P(dp + tensor, None)),
        out_specs=(P(dp + tensor, None), P(dp, tensor), P(dp, tensor), P(tensor, dp)),
        check_vma=False,
    )
```

time: 171 us -> 216 us (1.26)
  the two profiles are of different devices: /device:TPU:2 before, /device:TPU:1 now
where the time goes in v3:
time: 216 us; the launch traced here: 213 us
  blocking collectives  78.2 us (36%)
  starting transfers between devices  75 us (35%)
  waiting for transfers between devices  14.7 us (7%)
  local copies, waits for them, and re-layouts  12.6 us (6%)
  other arithmetic  12.5 us (6%)
  matrix products  11.7 us (5%)
  Pallas kernels  7.57 us (4%)
    all_gather x2, blocking collectives, per_device(): own.append(lax.all_gather(piece, 'z', axis=0, tiled=True))  78.2 us
    ppermute x6, starting transfers between devices, scatter_sum(): total = total + lax.ppermute(piece, axis, pairs).astype(F32)  24.5 us
    ppermute x1, starting transfers between devices, per_device(): from_core = lax.ppermute(jnp.concatenate(other, axis=1), 'c', SWAP)  12.4 us
    ppermute x1, starting transfers between devices, per_device(): back = back + lax.ppermute(back_part[:, :, 1].reshape(tok, ff), 'c', SWAP)  8.27 us
    all_to_all x1, starting transfers between devices, per_device(): lax.all_to_all(sum_x, 'yh', 0, 0).astype(F32).sum(0).astype(BF)  8.2 us
    all_to_all x1, waiting for transfers between devices, per_device(): lax.all_to_all(sum_x, 'yh', 0, 0).astype(F32).sum(0).astype(BF)  8.09 us
    ppermute x2, starting transfers between devices, per_device(): theirs.append(lax.ppermute(own[k], 'yl', SWAP))  6.53 us
    pallas_call x1, Pallas kernels, half_weight(): pl.pallas_call(half_kernel, out_shape=[jax.ShapeDtypeStruct((ff, NX * NYH...  5.91 us
  transfers between devices with their start and end apart: 15, of which 4 were waited for; matrix products, arithmetic and copies ran while one was open for 11% of the time, Pallas kernels for 3%

profile of v3, /device:TPU:1, one launch (start us, length us, event | category | flops | bytes accessed | tf_op | source)
XLA Modules:
  0.0 213.4 jit_solution(2471381625199996388)
XLA Ops:
  0.6 1.7 split_columns.1
  3.1 12.4 %collective-permute-start = (bf16[12,2048]{1,0:T(8,128)(2,1)S(1)}, bf16[12,2048]{1,0:T(8,128)(2,1)S(1)}, u32[]{:S(2)}, u32[]{:S(2)}) collective-permute-start(bf16[12,2048]{1,0:T(8,128)(2,1)S(1)} %pad_maximum_fusion.2), channel_id=1, source_target_pairs={{0,24},{24,0},{1,25},{25,1},{2,26},{26,2},{3,27},{27,3},{4,28},{28... | collective-permute-start | bytes 147464 | tf_op jit(solution)/shard_map/ppermute | solution.py:96
  16.9 4.5 %convolution_convert_fusion = bf16[288,4096]{1,0:T(8,128)(2,1)S(1)} fusion(bf16[288,640]{1,0:T(8,128)(2,1)S(1)} %fusion.12, bf16[640,4096]{1,0:T(8,128)(2,1)} %weight_ref.1), kind=kOutput, calls=%fused_computation | convolution fusion | flops 1511129088 | bytes 7970816 | tf_op jit(solution)/shard_map/dot_general | solution.py:104
  21.4 1.4 copy-done.1
  22.9 1.9 collective-permute-start.1
  25.5 22.7 %all_gather.6 = bf16[288,1024]{1,0:T(8,128)(2,1)S(1)} all-gather(bf16[24,1024]{1,0:T(8,128)(2,1)S(1)} %pad_maximum_fusion.4), channel_id=1, replica_groups=mesh['x'=4,'yh'=4,'c'=2,'yl'=2,'z'=12] {'z'}, dimensions={0}, use_global_device_ids=true | all-gather | bytes 638976 | tf_op jit(solution)/shard_map/all_gather | solution.py:121
  48.2 4.3 %collective-permute-done.1 = bf16[144,4096]{1,0:T(8,128)(2,1)} collective-permute-done((bf16[144,4096]{1,0:T(8,128)(2,1)S(1)}, bf16[144,4096]{1,0:T(8,128)(2,1)}, u32[]{:S(2)}, u32[]{:S(2)}) %collective-permute-start.1) | collective-permute-done | bytes 1179680 | tf_op jit(solution)/shard_map/ppermute | solution.py:108
  52.5 1.9 add_convert_fusion
  55.7 5.9 %all-to-all-start = ((bf16[12,12,4096]{2,1,0:T(8,128)(2,1)}), bf16[12,12,4096]{2,1,0:T(8,128)(2,1)S(1)}, u32[]{:S(2)}, u32[]{:S(2)}) async-start(bf16[12,12,4096]{2,1,0:T(8,128)(2,1)} %reshape.43), calls=%async_computation | async-start | bytes 3145728 | tf_op jit(solution)/shard_map/all_to_all | solution.py:118
  61.6 3.0 %collective-permute-start.3 = (bf16[288,640]{1,0:T(8,128)(2,1)S(1)}, bf16[288,640]{1,0:T(8,128)(2,1)S(1)}, u32[]{:S(2)}, u32[]{:S(2)}) collective-permute-start(bf16[288,640]{1,0:T(8,128)(2,1)S(1)} %fusion.12), channel_id=1, source_target_pairs={{0,24},{24,0},{1,25},{25,1},{2,26},{26,2},{3,27},{27,3},{4,28},{28... | collective-permute-start | bytes 1105928 | tf_op jit(solution)/shard_map/ppermute | solution.py:109
  64.6 5.9 %half_weight.1 = (bf16[640,1024]{1,0:T(8,128)(2,1)}, bf16[640,1024]{1,0:T(8,128)(2,1)}) custom-call(s32[1]{0:T(128)} %bitcast.core_ref, bf16[640,4096]{1,0:T(8,128)(2,1)} %weight_ref.1), custom_call_target="tpu_custom_call" | custom-call | tf_op jit(solution)/shard_map/half_weight/pallas_call | solution.py:63
  70.6 3.2 %collective-permute-start.4 = (bf16[288,1024]{1,0:T(8,128)(2,1)S(1)}, bf16[288,1024]{1,0:T(8,128)(2,1)}, u32[]{:S(2)}, u32[]{:S(2)}) collective-permute-start(bf16[288,1024]{1,0:T(8,128)(2,1)S(1)} %all_gather.6), channel_id=1, source_target_pairs={{0,12},{12,0},{1,13},{13,1},{2,14},{14,2},{3,15},{15,3},{4,16},{16... | collective-permute-start | bytes 1769480 | tf_op jit(solution)/shard_map/ppermute | solution.py:122
  75.5 55.5 %all_gather.7 = bf16[288,1024]{1,0:T(8,128)(2,1)S(1)} all-gather(bf16[24,1024]{1,0:T(8,128)(2,1)S(1)} %copy-done.6), channel_id=1, replica_groups=mesh['x'=4,'yh'=4,'c'=2,'yl'=2,'z'=12] {'z'}, dimensions={0}, use_global_device_ids=true | all-gather | bytes 638976 | tf_op jit(solution)/shard_map/all_gather | solution.py:121
  131.0 3.3 %collective-permute-start.2 = (bf16[288,1024]{1,0:T(8,128)(2,1)S(1)}, bf16[288,1024]{1,0:T(8,128)(2,1)S(1)}, u32[]{:S(2)}, u32[]{:S(2)}) collective-permute-start(bf16[288,1024]{1,0:T(8,128)(2,1)S(1)} %all_gather.7), channel_id=1, source_target_pairs={{0,12},{12,0},{1,13},{13,1},{2,14},{14,2},{3,15},{15,3},{4,16},{16... | collective-permute-start | bytes 1769480 | tf_op jit(solution)/shard_map/ppermute | solution.py:122
  138.0 3.1 %collective-permute-start.6 = (bf16[256,640]{1,0:T(8,128)(2,1)}, bf16[256,640]{1,0:T(8,128)(2,1)}, u32[]{:S(2)}, u32[]{:S(2)}) collective-permute-start(bf16[256,640]{1,0:T(8,128)(2,1)} %get-tuple-element.62), channel_id=1, source_target_pairs={{0,192},{192,384},{384,576},{576,0},{1,193},{193,385},{385,577},{5... | collective-permute-start | bytes 983048 | tf_op jit(solution)/shard_map/ppermute | solution.py:84
  141.1 4.4 %collective-permute-start.8 = (bf16[256,640]{1,0:T(8,128)(2,1)}, bf16[256,640]{1,0:T(8,128)(2,1)}, u32[]{:S(2)}, u32[]{:S(2)}) collective-permute-start(bf16[256,640]{1,0:T(8,128)(2,1)} %get-tuple-element.63), channel_id=1, source_target_pairs={{0,384},{192,576},{384,0},{576,192},{1,385},{193,577},{385,1},{577... | collective-permute-start | bytes 983048 | tf_op jit(solution)/shard_map/ppermute | solution.py:84
  145.5 3.1 %collective-permute-start.7 = (bf16[256,640]{1,0:T(8,128)(2,1)}, bf16[256,640]{1,0:T(8,128)(2,1)}, u32[]{:S(2)}, u32[]{:S(2)}) collective-permute-start(bf16[256,640]{1,0:T(8,128)(2,1)} %get-tuple-element.64), channel_id=1, source_target_pairs={{0,576},{192,0},{384,192},{576,384},{1,577},{193,1},{385,193},{577... | collective-permute-start | bytes 983048 | tf_op jit(solution)/shard_map/ppermute | solution.py:84
  148.7 2.4 %multiply_convert_fusion.1 = bf16[1024,640]{1,0:T(8,128)(2,1)} fusion(bf16[576,1024]{1,0:T(8,128)(2,1)S(1)} %constant_dynamic-update-slice_fusion, bf16[576,640]{1,0:T(8,128)(2,1)S(1)} %copy-done.5), kind=kOutput, calls=%fused_computation.2 | convolution fusion | flops 756285440 | bytes 3227648 | tf_op jit(solution)/shard_map/dot_general | solution.py:134
  152.4 2.3 %convolution_add_fusion = f32[576,640]{1,0:T(8,128)} fusion(f32[576,640]{1,0:T(8,128)S(1)} %fusion.21, bf16[576,1024]{1,0:T(8,128)(2,1)S(1)} %constant_dynamic-update-slice_fusion.2, bf16[640,1024]{1,0:T(8,128)(2,1)S(1)} %copy-done.9), kind=kOutput, calls=%fused_computation.4 | convolution fusion | flops 755343360 | bytes 5439488 | tf_op jit(solution)/shard_map/dot_general | solution.py:144
  154.7 1.4 reshape.47
  156.1 4.3 %all-to-all-start.1 = ((bf16[4,256,640]{2,1,0:T(8,128)(2,1)}), bf16[4,256,640]{2,1,0:T(8,128)(2,1)}, u32[]{:S(2)}, u32[]{:S(2)}) async-start(bf16[4,256,640]{2,1,0:T(8,128)(2,1)} %bitcast.37), calls=%async_computation.1 | async-start | bytes 2621440 | tf_op jit(solution)/shard_map/all_to_all | solution.py:143
  160.4 1.5 fusion.19
  162.0 2.1 %reshape_squeeze.7 = f32[288,640]{1,0:T(8,128)} reshape(f32[2,12,1,12,640]{4,3,2,1,0:T(8,128)} %get-tuple-element.60) | data formatting | bytes 1474560 | tf_op jit(solution)/shard_map/reshape;squeeze | solution.py:158
  164.1 8.3 %collective-permute-start.5 = (f32[288,640]{1,0:T(8,128)}, f32[288,640]{1,0:T(8,128)}, u32[]{:S(2)}, u32[]{:S(2)}) collective-permute-start(f32[288,640]{1,0:T(8,128)} %reshape_squeeze.7), channel_id=1, source_target_pairs={{0,24},{24,0},{1,25},{25,1},{2,26},{26,2},{3,27},{27,3},{4,28},{28... | collective-permute-start | bytes 2211848 | tf_op jit(solution)/shard_map/ppermute | solution.py:158
  172.4 1.5 fusion.15
  174.0 4.2 %collective-permute-start.9 = (bf16[64,640]{1,0:T(8,128)(2,1)S(1)}, bf16[64,640]{1,0:T(8,128)(2,1)S(1)}, u32[]{:S(2)}, u32[]{:S(2)}) collective-permute-start(bf16[64,640]{1,0:T(8,128)(2,1)S(1)} %get-tuple-element.71), channel_id=1, source_target_pairs={{0,48},{48,96},{96,144},{144,0},{1,49},{49,97},{97,145},{145,1},{2... | collective-permute-start | bytes 245768 | tf_op jit(solution)/shard_map/ppermute | solution.py:84
  178.2 4.7 %collective-permute-start.11 = (bf16[64,640]{1,0:T(8,128)(2,1)S(1)}, bf16[64,640]{1,0:T(8,128)(2,1)S(1)}, u32[]{:S(2)}, u32[]{:S(2)}) collective-permute-start(bf16[64,640]{1,0:T(8,128)(2,1)S(1)} %get-tuple-element.72), channel_id=1, source_target_pairs={{0,96},{48,144},{96,0},{144,48},{1,97},{49,145},{97,1},{145,49},{2... | collective-permute-start | bytes 245768 | tf_op jit(solution)/shard_map/ppermute | solution.py:84
  183.0 5.0 %collective-permute-start.10 = (bf16[64,640]{1,0:T(8,128)(2,1)S(1)}, bf16[64,640]{1,0:T(8,128)(2,1)S(1)}, u32[]{:S(2)}, u32[]{:S(2)}) collective-permute-start(bf16[64,640]{1,0:T(8,128)(2,1)S(1)} %get-tuple-element.73), channel_id=1, source_target_pairs={{0,144},{48,0},{96,48},{144,96},{1,145},{49,1},{97,49},{145,97},{2... | collective-permute-start | bytes 245768 | tf_op jit(solution)/shard_map/ppermute | solution.py:84
  188.0 1.7 collective-permute-done.11
  191.7 2.3 %reduce_sum.37 = bf16[256,640]{1,0:T(8,128)(2,1)} reduce(bf16[4,256,640]{2,1,0:T(8,128)(2,1)} %all-to-all-done.1, bf16[]{:T(256)} %constant.66.clone.1), dimensions={0}, to_apply=%region_1.2 | reduce | flops 491520 | bytes 1638402 | tf_op jit(solution)/shard_map/reduce_sum | solution.py:143
  194.0 8.2 %all-to-all-start.2 = ((bf16[4,64,640]{2,1,0:T(8,128)(2,1)}), bf16[4,64,640]{2,1,0:T(8,128)(2,1)S(1)}, u32[]{:S(2)}, u32[]{:S(2)}) async-start(bf16[4,64,640]{2,1,0:T(8,128)(2,1)} %bitcast.42), calls=%async_computation.2 | async-start | bytes 655360 | tf_op jit(solution)/shard_map/all_to_all | solution.py:151
  204.4 8.1 %all-to-all-done.2 = bf16[4,64,640]{2,1,0:T(8,128)(2,1)S(1)} async-done(((bf16[4,64,640]{2,1,0:T(8,128)(2,1)}), bf16[4,64,640]{2,1,0:T(8,128)(2,1)S(1)}, u32[]{:S(2)}, u32[]{:S(2)}) %all-to-all-start.2) | async-done | bytes 327712 | tf_op jit(solution)/shard_map/all_to_all | solution.py:151
  (64 shorter events, 16.0 us)
Async XLA Ops:
  3.1 13.8 %collective-permute-start = (bf16[12,2048]{1,0:T(8,128)(2,1)S(1)}, bf16[12,2048]{1,0:T(8,128)(2,1)S(1)}, u32[]{:S(2)}, u32[]{:S(2)}) collective-permute-start(bf16[12,2048]{1,0:T(8,128)(2,1)S(1)} %pad_maximum_fusion.2), channel_id=1, source_target_pairs={{0,24},{24,0},{1,25},{25,1},{2,26},{26,2},{3,27},{27,3},{4,28},{28... | collective-permute-start | bytes 147464 | tf_op jit(solution)/shard_map/ppermute | solution.py:96
  21.4 1.4 copy-start.1
  22.8 2.0 copy-start.8
  22.8 2.1 copy-start.7
  22.9 29.6 %collective-permute-start.1 = (bf16[144,4096]{1,0:T(8,128)(2,1)S(1)}, bf16[144,4096]{1,0:T(8,128)(2,1)}, u32[]{:S(2)}, u32[]{:S(2)}) collective-permute-start(bf16[144,4096]{1,0:T(8,128)(2,1)S(1)} %constant_dynamic-slice_fusion), channel_id=1, source_target_pairs={{0,12},{12,0},{1,13},{13,1},{2,14},{14,2},{3,15},{15,3},{4,16},{16... | collective-permute-start | bytes 3538952 | tf_op jit(solution)/shard_map/ppermute | solution.py:108
  55.7 100.4 %all-to-all-start = ((bf16[12,12,4096]{2,1,0:T(8,128)(2,1)}), bf16[12,12,4096]{2,1,0:T(8,128)(2,1)S(1)}, u32[]{:S(2)}, u32[]{:S(2)}) async-start(bf16[12,12,4096]{2,1,0:T(8,128)(2,1)} %reshape.43), calls=%async_computation | async-start | bytes 3145728 | tf_op jit(solution)/shard_map/all_to_all | solution.py:118
  61.6 12.2 %collective-permute-start.3 = (bf16[288,640]{1,0:T(8,128)(2,1)S(1)}, bf16[288,640]{1,0:T(8,128)(2,1)S(1)}, u32[]{:S(2)}, u32[]{:S(2)}) collective-permute-start(bf16[288,640]{1,0:T(8,128)(2,1)S(1)} %fusion.12), channel_id=1, source_target_pairs={{0,24},{24,0},{1,25},{25,1},{2,26},{26,2},{3,27},{27,3},{4,28},{28... | collective-permute-start | bytes 1105928 | tf_op jit(solution)/shard_map/ppermute | solution.py:109
  70.6 63.8 %collective-permute-start.4 = (bf16[288,1024]{1,0:T(8,128)(2,1)S(1)}, bf16[288,1024]{1,0:T(8,128)(2,1)}, u32[]{:S(2)}, u32[]{:S(2)}) collective-permute-start(bf16[288,1024]{1,0:T(8,128)(2,1)S(1)} %all_gather.6), channel_id=1, source_target_pairs={{0,12},{12,0},{1,13},{13,1},{2,14},{14,2},{3,15},{15,3},{4,16},{16... | collective-permute-start | bytes 1769480 | tf_op jit(solution)/shard_map/ppermute | solution.py:122
  74.5 1.0 copy-start.6
  131.0 4.5 %copy-start.5 = (bf16[576,640]{1,0:T(8,128)(2,1)S(1)}, bf16[576,640]{1,0:T(8,128)(2,1)}, u32[]{:S(2)}) copy-start(bf16[576,640]{1,0:T(8,128)(2,1)} %reshape.44) | copy-start | bytes 2211844
  131.0 17.6 %collective-permute-start.2 = (bf16[288,1024]{1,0:T(8,128)(2,1)S(1)}, bf16[288,1024]{1,0:T(8,128)(2,1)S(1)}, u32[]{:S(2)}, u32[]{:S(2)}) collective-permute-start(bf16[288,1024]{1,0:T(8,128)(2,1)S(1)} %all_gather.7), channel_id=1, source_target_pairs={{0,12},{12,0},{1,13},{13,1},{2,14},{14,2},{3,15},{15,3},{4,16},{16... | collective-permute-start | bytes 1769480 | tf_op jit(solution)/shard_map/ppermute | solution.py:122
  136.9 11.7 %copy-start.4 = (bf16[1024,640]{1,0:T(8,128)(2,1)}, bf16[1024,640]{1,0:T(8,128)(2,1)S(1)}, u32[]{:S(2)}) copy-start(bf16[1024,640]{1,0:T(8,128)(2,1)S(1)} %multiply_convert_fusion) | copy-start | bytes 3932164
  138.0 34.4 %collective-permute-start.6 = (bf16[256,640]{1,0:T(8,128)(2,1)}, bf16[256,640]{1,0:T(8,128)(2,1)}, u32[]{:S(2)}, u32[]{:S(2)}) collective-permute-start(bf16[256,640]{1,0:T(8,128)(2,1)} %get-tuple-element.62), channel_id=1, source_target_pairs={{0,192},{192,384},{384,576},{576,0},{1,193},{193,385},{385,577},{5... | collective-permute-start | bytes 983048 | tf_op jit(solution)/shard_map/ppermute | solution.py:84
  141.1 31.3 %collective-permute-start.8 = (bf16[256,640]{1,0:T(8,128)(2,1)}, bf16[256,640]{1,0:T(8,128)(2,1)}, u32[]{:S(2)}, u32[]{:S(2)}) collective-permute-start(bf16[256,640]{1,0:T(8,128)(2,1)} %get-tuple-element.63), channel_id=1, source_target_pairs={{0,384},{192,576},{384,0},{576,192},{1,385},{193,577},{385,1},{577... | collective-permute-start | bytes 983048 | tf_op jit(solution)/shard_map/ppermute | solution.py:84
  145.5 27.0 %collective-permute-start.7 = (bf16[256,640]{1,0:T(8,128)(2,1)}, bf16[256,640]{1,0:T(8,128)(2,1)}, u32[]{:S(2)}, u32[]{:S(2)}) collective-permute-start(bf16[256,640]{1,0:T(8,128)(2,1)} %get-tuple-element.64), channel_id=1, source_target_pairs={{0,576},{192,0},{384,192},{576,384},{1,577},{193,1},{385,193},{577... | collective-permute-start | bytes 983048 | tf_op jit(solution)/shard_map/ppermute | solution.py:84
  148.7 2.5 %copy-start.10 = (bf16[640,1024]{1,0:T(8,128)(2,1)S(1)}, bf16[640,1024]{1,0:T(8,128)(2,1)}, u32[]{:S(2)}) copy-start(bf16[640,1024]{1,0:T(8,128)(2,1)} %get-tuple-element.47) | copy-start | bytes 3932164
  151.1 1.3 copy-start.9
  156.1 35.5 %all-to-all-start.1 = ((bf16[4,256,640]{2,1,0:T(8,128)(2,1)}), bf16[4,256,640]{2,1,0:T(8,128)(2,1)}, u32[]{:S(2)}, u32[]{:S(2)}) async-start(bf16[4,256,640]{2,1,0:T(8,128)(2,1)} %bitcast.37), calls=%async_computation.1 | async-start | bytes 2621440 | tf_op jit(solution)/shard_map/all_to_all | solution.py:143
  164.1 26.3 %collective-permute-start.5 = (f32[288,640]{1,0:T(8,128)}, f32[288,640]{1,0:T(8,128)}, u32[]{:S(2)}, u32[]{:S(2)}) collective-permute-start(f32[288,640]{1,0:T(8,128)} %reshape_squeeze.7), channel_id=1, source_target_pairs={{0,24},{24,0},{1,25},{25,1},{2,26},{26,2},{3,27},{27,3},{4,28},{28... | collective-permute-start | bytes 2211848 | tf_op jit(solution)/shard_map/ppermute | solution.py:158
  172.4 18.0 %copy-start = (f32[2,12,1,12,640]{4,3,2,1,0:T(8,128)S(1)}, f32[2,12,1,12,640]{4,3,2,1,0:T(8,128)}, u32[]{:S(2)}) copy-start(f32[2,12,1,12,640]{4,3,2,1,0:T(8,128)} %get-tuple-element.61) | copy-start | bytes 2211844
  174.0 14.0 %collective-permute-start.9 = (bf16[64,640]{1,0:T(8,128)(2,1)S(1)}, bf16[64,640]{1,0:T(8,128)(2,1)S(1)}, u32[]{:S(2)}, u32[]{:S(2)}) collective-permute-start(bf16[64,640]{1,0:T(8,128)(2,1)S(1)} %get-tuple-element.71), channel_id=1, source_target_pairs={{0,48},{48,96},{96,144},{144,0},{1,49},{49,97},{97,145},{145,1},{2... | collective-permute-start | bytes 245768 | tf_op jit(solution)/shard_map/ppermute | solution.py:84
  178.2 11.5 %collective-permute-start.11 = (bf16[64,640]{1,0:T(8,128)(2,1)S(1)}, bf16[64,640]{1,0:T(8,128)(2,1)S(1)}, u32[]{:S(2)}, u32[]{:S(2)}) collective-permute-start(bf16[64,640]{1,0:T(8,128)(2,1)S(1)} %get-tuple-element.72), channel_id=1, source_target_pairs={{0,96},{48,144},{96,0},{144,48},{1,97},{49,145},{97,1},{145,49},{2... | collective-permute-start | bytes 245768 | tf_op jit(solution)/shard_map/ppermute | solution.py:84
  183.0 7.3 %collective-permute-start.10 = (bf16[64,640]{1,0:T(8,128)(2,1)S(1)}, bf16[64,640]{1,0:T(8,128)(2,1)S(1)}, u32[]{:S(2)}, u32[]{:S(2)}) collective-permute-start(bf16[64,640]{1,0:T(8,128)(2,1)S(1)} %get-tuple-element.73), channel_id=1, source_target_pairs={{0,144},{48,0},{96,48},{144,96},{1,145},{49,1},{97,49},{145,97},{2... | collective-permute-start | bytes 245768 | tf_op jit(solution)/shard_map/ppermute | solution.py:84
  194.0 8.3 %copy-start.2 = (bf16[288,640]{1,0:T(8,128)(2,1)S(1)}, bf16[288,640]{1,0:T(8,128)(2,1)}, u32[]{:S(2)}) copy-start(bf16[288,640]{1,0:T(8,128)(2,1)} %param.5) | copy-start | bytes 1105924
  194.0 8.3 %copy-start.3 = (bf16[288,640]{1,0:T(8,128)(2,1)S(1)}, bf16[288,640]{1,0:T(8,128)(2,1)}, u32[]{:S(2)}) copy-start(bf16[288,640]{1,0:T(8,128)(2,1)} %param.4) | copy-start | bytes 1105924
  194.0 18.6 %all-to-all-start.2 = ((bf16[4,64,640]{2,1,0:T(8,128)(2,1)}), bf16[4,64,640]{2,1,0:T(8,128)(2,1)S(1)}, u32[]{:S(2)}, u32[]{:S(2)}) async-start(bf16[4,64,640]{2,1,0:T(8,128)(2,1)} %bitcast.42), calls=%async_computation.2 | async-start | bytes 655360 | tf_op jit(solution)/shard_map/all_to_all | solution.py:151

commit v4 on v2

--- a/solution.py
+++ b/solution.py
@@ -7,6 +7,7 @@
 
 NX, NYH, NC, NYL, NZ = 4, 4, 2, 2, 12
 CHUNKS = 2
+GATHERED = 14
 PER = NYH // CHUNKS
 BF, F32 = jnp.bfloat16, jnp.float32
 SWAP = [(0, 1), (1, 0)]
@@ -18,15 +19,20 @@
     return (rest // PER) * NYH + chunk * PER + rest % PER
 
 
+def copy_half(out_ref, ref, half):
+    lane = out_ref.shape[1] // (NX * NYH)
+    for slot in range(NX * NYH):
+        at = (source_block(slot) * NC + half) * lane
+        out_ref[:, slot * lane : (slot + 1) * lane] = ref[:, at : at + lane]
+
+
 def split_kernel(core_ref, cot_ref, mine_ref, other_ref):
-    lane = mine_ref.shape[1] // (NX * NYH)
-    zero = core_ref[0] == 0
-    for slot in range(NX * NYH):
-        at = source_block(slot) * NC * lane
-        even = cot_ref[:, at : at + lane]
-        odd = cot_ref[:, at + lane : at + NC * lane]
-        mine_ref[:, slot * lane : (slot + 1) * lane] = jnp.where(zero, even, odd)
-        other_ref[:, slot * lane : (slot + 1) * lane] = jnp.where(zero, odd, even)
+    for core in range(NC):
+
+        @pl.when(core_ref[0] == core)
+        def _():
+            copy_half(mine_ref, cot_ref, core)
+            copy_half(other_ref, cot_ref, 1 - core)
 
 
 def split_columns(core, cot):
@@ -44,29 +50,28 @@
     )(core.reshape(1), cot)
 
 
-def half_kernel(core_ref, a_ref, b_ref, out_ref):
-    lane = a_ref.shape[1]
-    out_ref[:, :lane] = a_ref[...]
-    out_ref[:, lane:] = b_ref[...]
+def half_kernel(core_ref, weight_ref, out_ref):
+    for core in range(NC):
+
+        @pl.when(core_ref[0] == core)
+        def _():
+            copy_half(out_ref, weight_ref, core)
 
 
 def half_weight(core, weight):
     ff, feat = weight.shape
-    lane = feat // (NX * NYH * NC)
-    pick = lambda k: pl.BlockSpec(
-        (ff, lane), lambda i, core_ref: (0, source_block(2 * i + k) * NC + core_ref[0])
-    )
+    step = 128
     return pl.pallas_call(
         half_kernel,
         out_shape=jax.ShapeDtypeStruct((ff, feat // NC), weight.dtype),
-        grid_spec=pltpu.PrefetchScalarGridSpec(
-            num_scalar_prefetch=1,
-            grid=(NX * NYH // 2,),
-            in_specs=[pick(0), pick(1)],
-            out_specs=pl.BlockSpec((ff, 2 * lane), lambda i, core_ref: (0, i)),
-        ),
+        grid=(ff // step,),
+        in_specs=[
+            pl.BlockSpec(memory_space=pltpu.SMEM),
+            pl.BlockSpec((step, feat), lambda i: (i, 0)),
+        ],
+        out_specs=pl.BlockSpec((step, feat // NC), lambda i: (i, 0)),
         name="half_weight",
-    )(core.reshape(1), weight, weight)
+    )(core.reshape(1), weight)
 
 
 def per_device(gate_pre, up_pre, down_weight, cotangent):
@@ -94,15 +99,15 @@
     hidden_peer = lax.ppermute(hidden_z, "c", SWAP)
 
     shard = jnp.concatenate([mine, from_core], axis=0)
-    w_half = half_weight(core, down_weight)
-    own = [None] * CHUNKS
-    theirs = [None] * CHUNKS
-    for k in range(CHUNKS):
-        piece = shard[:, k * width : (k + 1) * width]
-        if k:
-            piece, own[k - 1] = tie((piece, own[k - 1]))
-        own[k] = lax.all_gather(piece, "z", axis=0, tiled=True)
-        theirs[k] = lax.ppermute(own[k], "yl", SWAP)
+    main, rest = shard[:, : GATHERED * lane], shard[:, GATHERED * lane :]
+    rest = jnp.broadcast_to(rest[None], (NZ,) + rest.shape)
+    main, rest = tie((main, rest))
+    rest_all = lax.all_to_all(rest, "z", 0, 0).reshape(tok, -1)
+    main_all = lax.all_gather(main, "z", axis=0, tiled=True)
+    own = [main_all[:, :width], jnp.concatenate([main_all[:, width:], rest_all], axis=1)]
+    theirs = [lax.ppermute(rows_k, "yl", SWAP) for rows_k in own]
+    weight, main_all = tie((down_weight, main_all))
+    w_half = half_weight(core, weight)
 
     pair = jnp.stack([hidden_z, hidden_peer], axis=2)
     low, high = pair[:, 0], pair[:, 1]

time: 171 us -> 173 us (1.012)
  blocking collectives: 62.5 us -> 43.5 us
  waiting for transfers between devices: 15.1 us -> 26.8 us
  other arithmetic: 8.08 us -> 13.5 us
  starting transfers between devices: 33.2 us -> 36.5 us
  matrix products: 18.5 us -> 21.3 us
    all_gather x2 -> x1, blocking collectives: 62.5 us -> 43.5 us  [per_device(): main_all = lax.all_gather(main, 'z', axis=0, tiled=True)]
    all_to_all x0 -> x1, waiting for transfers between devices: none -> 11.8 us  [per_device(): rest_all = lax.all_to_all(rest, 'z', 0, 0).reshape(tok, -1)]
    concatenate x0 -> x3, other arithmetic: none -> 5.33 us  [the longest x2 4.44 us: per_device(): cot_k = jnp.concatenate([own[k], theirs[k]], axis=0)]
    all_to_all x0 -> x1, starting transfers between devices: none -> 4.76 us  [per_device(): rest_all = lax.all_to_all(rest, 'z', 0, 0).reshape(tok, -1)]
    concatenate x2 -> x0, local copies, waits for them, and re-layouts: 3.01 us -> none  [per_device(): cot_k = jnp.concatenate([own[k], theirs[k]], axis=0)]
  transfers between devices with their start and end apart: 10 -> 11, of which waited for: 2 -> 3; matrix products, arithmetic and copies ran while one was open for 18% -> 21% of each run, Pallas kernels for 4% -> 3%
where the time goes in v4:
time: 173 us; the launch traced here: 172 us
  blocking collectives  43.5 us (25%)
  starting transfers between devices  36.5 us (21%)
  waiting for transfers between devices  26.8 us (15%)
  matrix products  21.3 us (12%)
  between operations  14.3 us (8%)
  other arithmetic  13.5 us (8%)
  local copies, waits for them, and re-layouts  8.92 us (5%)
  Pallas kernels  7.22 us (4%)
    all_gather x1, blocking collectives, per_device(): main_all = lax.all_gather(main, 'z', axis=0, tiled=True)  43.5 us
    all_to_all x1, waiting for transfers between devices, per_device(): by_y = lax.all_to_all(jnp.concatenate(sums, axis=0), 'yh', 0, 0)  14.5 us
    all_to_all x1, waiting for transfers between devices, per_device(): rest_all = lax.all_to_all(rest, 'z', 0, 0).reshape(tok, -1)  11.8 us
    all_to_all x2, starting transfers between devices, per_device(): by_x = lax.all_to_all(term, 'x', 0, 0)  9.82 us
    dot_general x2, matrix products, per_device(): lax.dot_general(cot_k, w_half[:, k * width:(k + 1) * width], (((1,), (1,)...  8.03 us
    dot_general x2, matrix products, per_device(): lax.dot_general(cot_k, hidden_both, (((0,), (0,)), ((), ())), preferred_e...  7.32 us
    ppermute x2, starting transfers between devices, per_device(): theirs = [lax.ppermute(rows_k, 'yl', SWAP) for rows_k in own]  6.76 us
    all_to_all x1, starting transfers between devices, per_device(): by_y = lax.all_to_all(jnp.concatenate(sums, axis=0), 'yh', 0, 0)  6.1 us
  transfers between devices with their start and end apart: 11, of which 3 were waited for; matrix products, arithmetic and copies ran while one was open for 21% of the time, Pallas kernels for 3%

profile of v4, /device:TPU:2, one launch (start us, length us, event | category | flops | bytes accessed | tf_op | source)
XLA Modules:
  0.0 172.0 jit_solution(8305018717693775008)
XLA Ops:
  7.2 1.6 split_columns.1
  8.8 1.9 %collective-permute-start = (bf16[12,2048]{1,0:T(8,128)(2,1)}, bf16[12,2048]{1,0:T(8,128)(2,1)S(1)}, u32[]{:S(2)}, u32[]{:S(2)}) collective-permute-start(bf16[12,2048]{1,0:T(8,128)(2,1)} %get-tuple-element.22), channel_id=1, source_target_pairs={{0,24},{24,0},{1,25},{25,1},{2,26},{26,2},{3,27},{27,3},{4,28},{28... | collective-permute-start | bytes 147464 | tf_op jit(solution)/shard_map/ppermute | solution.py:87
  10.7 1.3 fusion.15
  12.3 5.9 %convolution_convert_fusion = bf16[288,4096]{1,0:T(8,128)(2,1)} fusion(bf16[288,640]{1,0:T(8,128)(2,1)S(1)} %reshape.80, bf16[640,4096]{1,0:T(8,128)(2,1)} %weight_ref), kind=kOutput, calls=%fused_computation | convolution fusion | flops 1511129088 | bytes 7970816 | tf_op jit(solution)/shard_map/dot_general | solution.py:96
  19.8 2.4 %collective-permute-start.3 = (bf16[12,2,12,640]{3,2,0,1:T(8,128)(2,1)S(1)}, bf16[12,2,12,640]{3,2,0,1:T(8,128)(2,1)S(1)}, u32[]{:S(2)}, u32[]{:S(2)}) collective-permute-start(bf16[12,2,12,640]{3,2,0,1:T(8,128)(2,1)S(1)} %bitcast.33), channel_id=1, source_target_pairs={{0,24},{24,0},{1,25},{25,1},{2,26},{26,2},{3,27},{27,3},{4,28},{28... | collective-permute-start | bytes 1105928 | tf_op jit(solution)/shard_map/ppermute | solution.py:99
  22.2 43.5 %all_gather.3 = bf16[288,1792]{1,0:T(8,128)(2,1)S(1)} all-gather(bf16[24,1792]{1,0:T(8,128)(2,1)S(1)} %fusion.19), channel_id=1, replica_groups=mesh['x'=4,'yh'=4,'c'=2,'yl'=2,'z'=12] {'z'}, dimensions={0}, use_global_device_ids=true | all-gather | bytes 1118208 | tf_op jit(solution)/shard_map/all_gather | solution.py:106
  65.7 3.6 %collective-permute-start.2 = (bf16[288,1024]{1,0:T(8,128)(2,1)S(1)}, bf16[288,1024]{1,0:T(8,128)(2,1)}, u32[]{:S(2)}, u32[]{:S(2)}) collective-permute-start(bf16[288,1024]{1,0:T(8,128)(2,1)S(1)} %slice.50), channel_id=1, source_target_pairs={{0,12},{12,0},{1,13},{13,1},{2,14},{14,2},{3,15},{15,3},{4,16},{16... | collective-permute-start | bytes 1769480 | tf_op jit(solution)/shard_map/ppermute | solution.py:108
  69.3 4.8 %all-to-all-start = ((bf16[12,24,256]{2,1,0:T(8,128)(2,1)}), bf16[12,24,256]{2,1,0:T(8,128)(2,1)S(1)}, u32[]{:S(2)}, u32[]{:S(2)}) async-start(bf16[12,24,256]{2,1,0:T(8,128)(2,1)} %broadcast_in_dim.2), calls=%async_computation.1 | async-start | bytes 294912 | tf_op jit(solution)/shard_map/all_to_all | solution.py:105
  74.8 1.0 reshape.81
  75.8 11.8 %all-to-all-done = bf16[12,24,256]{2,1,0:T(8,128)(2,1)S(1)} async-done(((bf16[12,24,256]{2,1,0:T(8,128)(2,1)}), bf16[12,24,256]{2,1,0:T(8,128)(2,1)S(1)}, u32[]{:S(2)}, u32[]{:S(2)}) %all-to-all-start) | async-done | bytes 147488 | tf_op jit(solution)/shard_map/all_to_all | solution.py:105
  88.5 3.2 %collective-permute-start.4 = (bf16[288,1024]{1,0:T(8,128)(2,1)}, bf16[288,1024]{1,0:T(8,128)(2,1)}, u32[]{:S(2)}, u32[]{:S(2)}) collective-permute-start(bf16[288,1024]{1,0:T(8,128)(2,1)} %pad_maximum_fusion.5), channel_id=1, source_target_pairs={{0,12},{12,0},{1,13},{13,1},{2,14},{14,2},{3,15},{15,3},{4,16},{16... | collective-permute-start | bytes 1769480 | tf_op jit(solution)/shard_map/ppermute | solution.py:108
  91.7 3.8 %multiply_convert_fusion.1 = bf16[1024,640]{1,0:T(8,128)(2,1)} fusion(bf16[576,640]{1,0:T(8,128)(2,1)} %reshape.81, bf16[288,1024]{1,0:T(8,128)(2,1)} %collective-permute-done.2, bf16[288,1024]{1,0:T(8,128)(2,1)S(1)} %slice.50), kind=kOutput, calls=%fused_computation.2 | convolution fusion | flops 758644736 | bytes 3227648 | tf_op jit(solution)/shard_map/dot_general | solution.py:122
  95.5 2.2 %pad_maximum_fusion = bf16[576,1024]{1,0:T(8,128)(2,1)} fusion(bf16[288,1024]{1,0:T(8,128)(2,1)} %collective-permute-done.2, bf16[288,1024]{1,0:T(8,128)(2,1)S(1)} %slice.50), kind=kLoop, calls=%fused_computation.7 | loop fusion | flops 2359296 | bytes 2359296 | tf_op jit(solution)/shard_map/concatenate | solution.py:121
  97.7 4.9 %all-to-all-start.1 = ((bf16[4,256,640]{2,1,0:T(8,128)(2,1)}), bf16[4,256,640]{2,1,0:T(8,128)(2,1)S(1)}, u32[]{:S(2)}, u32[]{:S(2)}) async-start(bf16[4,256,640]{2,1,0:T(8,128)(2,1)} %bitcast.42), calls=%async_computation.2 | async-start | bytes 2621440 | tf_op jit(solution)/shard_map/all_to_all | solution.py:127
  102.6 5.6 %half_weight.1 = bf16[640,2048]{1,0:T(8,128)(2,1)} custom-call(s32[1]{0:T(128)} %bitcast.1.core_ref, bf16[640,4096]{1,0:T(8,128)(2,1)} %weight_ref), custom_call_target="tpu_custom_call" | custom-call | tf_op jit(solution)/shard_map/half_weight/pallas_call | solution.py:64
  108.2 4.0 %fusion.1 = f32[576,640]{1,0:T(8,128)} fusion(bf16[576,1024]{1,0:T(8,128)(2,1)} %pad_maximum_fusion, bf16[640,2048]{1,0:T(8,128)(2,1)} %half_weight.1), kind=kOutput, calls=%fused_computation.5 | convolution fusion | flops 754974720 | bytes 3964928 | tf_op jit(solution)/shard_map/dot_general | solution.py:128
  112.2 2.3 %pad_maximum_fusion.1 = bf16[576,1024]{1,0:T(8,128)(2,1)} fusion(bf16[288,1024]{1,0:T(8,128)(2,1)} %collective-permute-done.4, bf16[288,256]{1,0:T(8,128)(2,1)S(1)} %bitcast.39, bf16[288,768]{1,0:T(8,128)(2,1)S(1)} %slice.54), kind=kLoop, calls=%fused_computation.8 | loop fusion | flops 3538944 | bytes 2359296 | tf_op jit(solution)/shard_map/concatenate | solution.py:121
  114.5 3.5 %multiply_convert_fusion = bf16[1024,640]{1,0:T(8,128)(2,1)} fusion(bf16[576,640]{1,0:T(8,128)(2,1)S(1)} %copy-done.4, bf16[288,1024]{1,0:T(8,128)(2,1)} %collective-permute-done.4, bf16[288,256]{1,0:T(8,128)(2,1)S(1)} %bitcast.40, bf16[288,768]{1,0:T(8,128)(2,1)S(1)} %slice.54), kind=kOutput, calls=%fused_computation.1 | convolution fusion | flops 759824384 | bytes 3227648 | tf_op jit(solution)/shard_map/dot_general | solution.py:122
  118.0 4.9 %all-to-all-start.2 = ((bf16[4,256,640]{2,1,0:T(8,128)(2,1)}), bf16[4,256,640]{2,1,0:T(8,128)(2,1)}, u32[]{:S(2)}, u32[]{:S(2)}) async-start(bf16[4,256,640]{2,1,0:T(8,128)(2,1)} %bitcast.41), calls=%async_computation.3 | async-start | bytes 2621440 | tf_op jit(solution)/shard_map/all_to_all | solution.py:127
  122.9 4.1 %convolution_add_fusion = f32[576,640]{1,0:T(8,128)} fusion(f32[576,640]{1,0:T(8,128)} %fusion.1, bf16[576,1024]{1,0:T(8,128)(2,1)S(1)} %copy-done.3, bf16[640,2048]{1,0:T(8,128)(2,1)} %half_weight.1), kind=kOutput, calls=%fused_computation.3 | convolution fusion | flops 755343360 | bytes 5439488 | tf_op jit(solution)/shard_map/dot_general | solution.py:128
  127.0 1.4 reshape.85
  128.4 1.5 fusion.20
  129.8 1.3 reshape_squeeze.7
  131.1 1.9 %collective-permute-start.5 = (f32[288,640]{1,0:T(8,128)S(1)}, f32[288,640]{1,0:T(8,128)}, u32[]{:S(2)}, u32[]{:S(2)}) collective-permute-start(f32[288,640]{1,0:T(8,128)S(1)} %reshape_squeeze.7), channel_id=1, source_target_pairs={{0,24},{24,0},{1,25},{25,1},{2,26},{26,2},{3,27},{27,3},{4,28},{28... | collective-permute-start | bytes 2211848 | tf_op jit(solution)/shard_map/ppermute | solution.py:140
  133.8 1.6 reduce_sum.37
  135.5 0.9 pad_maximum_fusion.4
  136.4 6.1 %all-to-all-start.3 = ((bf16[4,128,640]{2,1,0:T(8,128)(2,1)}), bf16[4,128,640]{2,1,0:T(8,128)(2,1)S(1)}, u32[]{:S(2)}, u32[]{:S(2)}) async-start(bf16[4,128,640]{2,1,0:T(8,128)(2,1)} %pad_maximum_fusion.4), calls=%async_computation.4 | async-start | bytes 1310720 | tf_op jit(solution)/shard_map/all_to_all | solution.py:135
  142.6 1.3 add.31
  144.0 1.0 constant_dynamic-slice_fusion
  144.9 2.8 %collective-permute-start.1 = (bf16[12,4096]{1,0:T(8,128)(2,1)S(1)}, bf16[12,4096]{1,0:T(8,128)(2,1)S(1)}, u32[]{:S(2)}, u32[]{:S(2)}) collective-permute-start(bf16[12,4096]{1,0:T(8,128)(2,1)S(1)} %constant_dynamic-slice_fusion), channel_id=1, source_target_pairs={{0,12},{12,0},{1,13},{13,1},{2,14},{14,2},{3,15},{15,3},{4,16},{16... | collective-permute-start | bytes 294920 | tf_op jit(solution)/shard_map/ppermute | solution.py:152
  147.7 1.2 fusion.14
  149.0 14.5 %all-to-all-done.3 = bf16[4,128,640]{2,1,0:T(8,128)(2,1)S(1)} async-done(((bf16[4,128,640]{2,1,0:T(8,128)(2,1)}), bf16[4,128,640]{2,1,0:T(8,128)(2,1)S(1)}, u32[]{:S(2)}, u32[]{:S(2)}) %all-to-all-start.3) | async-done | bytes 655392 | tf_op jit(solution)/shard_map/all_to_all | solution.py:135
  (44 shorter events, 6.0 us)
Async XLA Ops:
  7.2 136.8 %reduce-scatter.2.cloned.1.call-start = ((), (), s32[]{:S(2)}) async-start(), calls=%async_computation.5 | async-start | bytes 2555904 | tf_op jit(solution)/shard_map/reduce_scatter | solution.py:98
  8.8 3.4 %collective-permute-start = (bf16[12,2048]{1,0:T(8,128)(2,1)}, bf16[12,2048]{1,0:T(8,128)(2,1)S(1)}, u32[]{:S(2)}, u32[]{:S(2)}) collective-permute-start(bf16[12,2048]{1,0:T(8,128)(2,1)} %get-tuple-element.22), channel_id=1, source_target_pairs={{0,24},{24,0},{1,25},{25,1},{2,26},{26,2},{3,27},{27,3},{4,28},{28... | collective-permute-start | bytes 147464 | tf_op jit(solution)/shard_map/ppermute | solution.py:87
  18.2 0.8 copy-start.6
  19.8 54.3 %collective-permute-start.3 = (bf16[12,2,12,640]{3,2,0,1:T(8,128)(2,1)S(1)}, bf16[12,2,12,640]{3,2,0,1:T(8,128)(2,1)S(1)}, u32[]{:S(2)}, u32[]{:S(2)}) collective-permute-start(bf16[12,2,12,640]{3,2,0,1:T(8,128)(2,1)S(1)} %bitcast.33), channel_id=1, source_target_pairs={{0,24},{24,0},{1,25},{25,1},{2,26},{26,2},{3,27},{27,3},{4,28},{28... | collective-permute-start | bytes 1105928 | tf_op jit(solution)/shard_map/ppermute | solution.py:99
  65.7 25.9 %collective-permute-start.2 = (bf16[288,1024]{1,0:T(8,128)(2,1)S(1)}, bf16[288,1024]{1,0:T(8,128)(2,1)}, u32[]{:S(2)}, u32[]{:S(2)}) collective-permute-start(bf16[288,1024]{1,0:T(8,128)(2,1)S(1)} %slice.50), channel_id=1, source_target_pairs={{0,12},{12,0},{1,13},{13,1},{2,14},{14,2},{3,15},{15,3},{4,16},{16... | collective-permute-start | bytes 1769480 | tf_op jit(solution)/shard_map/ppermute | solution.py:108
  69.3 18.3 %all-to-all-start = ((bf16[12,24,256]{2,1,0:T(8,128)(2,1)}), bf16[12,24,256]{2,1,0:T(8,128)(2,1)S(1)}, u32[]{:S(2)}, u32[]{:S(2)}) async-start(bf16[12,24,256]{2,1,0:T(8,128)(2,1)} %broadcast_in_dim.2), calls=%async_computation.1 | async-start | bytes 294912 | tf_op jit(solution)/shard_map/all_to_all | solution.py:105
  88.5 23.7 %collective-permute-start.4 = (bf16[288,1024]{1,0:T(8,128)(2,1)}, bf16[288,1024]{1,0:T(8,128)(2,1)}, u32[]{:S(2)}, u32[]{:S(2)}) collective-permute-start(bf16[288,1024]{1,0:T(8,128)(2,1)} %pad_maximum_fusion.5), channel_id=1, source_target_pairs={{0,12},{12,0},{1,13},{13,1},{2,14},{14,2},{3,15},{15,3},{4,16},{16... | collective-permute-start | bytes 1769480 | tf_op jit(solution)/shard_map/ppermute | solution.py:108
  97.7 20.3 %all-to-all-start.1 = ((bf16[4,256,640]{2,1,0:T(8,128)(2,1)}), bf16[4,256,640]{2,1,0:T(8,128)(2,1)S(1)}, u32[]{:S(2)}, u32[]{:S(2)}) async-start(bf16[4,256,640]{2,1,0:T(8,128)(2,1)} %bitcast.42), calls=%async_computation.2 | async-start | bytes 2621440 | tf_op jit(solution)/shard_map/all_to_all | solution.py:127
  112.2 2.3 %copy-start.4 = (bf16[576,640]{1,0:T(8,128)(2,1)S(1)}, bf16[576,640]{1,0:T(8,128)(2,1)}, u32[]{:S(2)}) copy-start(bf16[576,640]{1,0:T(8,128)(2,1)} %reshape.81) | copy-start | bytes 2211844
  117.9 4.9 %copy-start.3 = (bf16[576,1024]{1,0:T(8,128)(2,1)S(1)}, bf16[576,1024]{1,0:T(8,128)(2,1)}, u32[]{:S(2)}) copy-start(bf16[576,1024]{1,0:T(8,128)(2,1)} %pad_maximum_fusion.1) | copy-start | bytes 3538948
  118.0 15.9 %all-to-all-start.2 = ((bf16[4,256,640]{2,1,0:T(8,128)(2,1)}), bf16[4,256,640]{2,1,0:T(8,128)(2,1)}, u32[]{:S(2)}, u32[]{:S(2)}) async-start(bf16[4,256,640]{2,1,0:T(8,128)(2,1)} %bitcast.41), calls=%async_computation.3 | async-start | bytes 2621440 | tf_op jit(solution)/shard_map/all_to_all | solution.py:127
  131.1 11.5 %collective-permute-start.5 = (f32[288,640]{1,0:T(8,128)S(1)}, f32[288,640]{1,0:T(8,128)}, u32[]{:S(2)}, u32[]{:S(2)}) collective-permute-start(f32[288,640]{1,0:T(8,128)S(1)} %reshape_squeeze.7), channel_id=1, source_target_pairs={{0,24},{24,0},{1,25},{25,1},{2,26},{26,2},{3,27},{27,3},{4,28},{28... | collective-permute-start | bytes 2211848 | tf_op jit(solution)/shard_map/ppermute | solution.py:140
  135.5 7.0 %copy-start = (f32[2,12,1,12,640]{4,3,2,1,0:T(8,128)S(1)}, f32[2,12,1,12,640]{4,3,2,1,0:T(8,128)}, u32[]{:S(2)}) copy-start(f32[2,12,1,12,640]{4,3,2,1,0:T(8,128)} %get-tuple-element.45) | copy-start | bytes 2211844
  136.4 27.1 %all-to-all-start.3 = ((bf16[4,128,640]{2,1,0:T(8,128)(2,1)}), bf16[4,128,640]{2,1,0:T(8,128)(2,1)S(1)}, u32[]{:S(2)}, u32[]{:S(2)}) async-start(bf16[4,128,640]{2,1,0:T(8,128)(2,1)} %pad_maximum_fusion.4), calls=%async_computation.4 | async-start | bytes 1310720 | tf_op jit(solution)/shard_map/all_to_all | solution.py:135
  142.6 5.1 %copy-start.1 = (bf16[288,640]{1,0:T(8,128)(2,1)S(1)}, bf16[288,640]{1,0:T(8,128)(2,1)}, u32[]{:S(2)}) copy-start(bf16[288,640]{1,0:T(8,128)(2,1)} %param.5) | copy-start | bytes 1105924
  142.6 5.1 %copy-start.2 = (bf16[288,640]{1,0:T(8,128)(2,1)S(1)}, bf16[288,640]{1,0:T(8,128)(2,1)}, u32[]{:S(2)}) copy-start(bf16[288,640]{1,0:T(8,128)(2,1)} %param.4) | copy-start | bytes 1105924
  144.9 19.5 %collective-permute-start.1 = (bf16[12,4096]{1,0:T(8,128)(2,1)S(1)}, bf16[12,4096]{1,0:T(8,128)(2,1)S(1)}, u32[]{:S(2)}, u32[]{:S(2)}) collective-permute-start(bf16[12,4096]{1,0:T(8,128)(2,1)S(1)} %constant_dynamic-slice_fusion), channel_id=1, source_target_pairs={{0,12},{12,0},{1,13},{13,1},{2,14},{14,2},{3,15},{15,3},{4,16},{16... | collective-permute-start | bytes 294920 | tf_op jit(solution)/shard_map/ppermute | solution.py:152
  147.7 16.7 %copy-start.5 = (bf16[24,4096]{1,0:T(8,128)(2,1)S(1)}, bf16[24,4096]{1,0:T(8,128)(2,1)}, u32[]{:S(2)}) copy-start(bf16[24,4096]{1,0:T(8,128)(2,1)} %reduce-scatter.2.cloned.1.call-done) | copy-start | bytes 589828
Sparse Core Ops, SparseCore 0:
  18.4 71.8 reduce-scatter.1

commit v5 on v4

v5 whole, which is shorter than its diff:
```python
import functools

import jax
import jax.numpy as jnp
from jax import lax
from jax.experimental import pallas as pl
from jax.experimental.pallas import tpu as pltpu
from jax.sharding import Mesh, PartitionSpec as P

NX, NYH, NC, NYL, NZ = 4, 4, 2, 2, 12
GATHERED = 14
BF, F32 = jnp.bfloat16, jnp.float32
SWAP = [(0, 1), (1, 0)]
tie = lax.optimization_barrier


def copy_half(out_ref, ref, half):
    lane = out_ref.shape[1] // (NX * NYH)
    for slot in range(NX * NYH):
        at = (slot * NC + half) * lane
        out_ref[:, slot * lane : (slot + 1) * lane] = ref[:, at : at + lane]


def split_kernel(core_ref, cot_ref, mine_ref, other_ref):
    for core in range(NC):

        @pl.when(core_ref[0] == core)
        def _():
            copy_half(mine_ref, cot_ref, core)
            copy_half(other_ref, cot_ref, 1 - core)


def split_columns(core, cot):
    rows, feat = cot.shape
    shape = jax.ShapeDtypeStruct((rows, feat // NC), cot.dtype)
    return pl.pallas_call(
        split_kernel,
        out_shape=(shape, shape),
        in_specs=[
            pl.BlockSpec(memory_space=pltpu.SMEM),
            pl.BlockSpec(memory_space=pltpu.VMEM),
        ],
        out_specs=(pl.BlockSpec(memory_space=pltpu.VMEM),) * 2,
        name="split_columns",
    )(core.reshape(1), cot)


def half_kernel(core_ref, weight_ref, out_ref):
    for core in range(NC):

        @pl.when(core_ref[0] == core)
        def _():
            copy_half(out_ref, weight_ref, core)


def half_weight(core, weight):
    ff, feat = weight.shape
    step = 128
    return pl.pallas_call(
        half_kernel,
        out_shape=jax.ShapeDtypeStruct((ff, feat // NC), weight.dtype),
        grid=(ff // step,),
        in_specs=[
            pl.BlockSpec(memory_space=pltpu.SMEM),
            pl.BlockSpec((step, feat), lambda i: (i, 0)),
        ],
        out_specs=pl.BlockSpec((step, feat // NC), lambda i: (i, 0)),
        name="half_weight",
    )(core.reshape(1), weight)


def grad_kernel(scale, *refs):
    main_near, rest_near, main_far, rest_far, hidden_near, hidden_far, out_ref = refs

    def product(near, far):
        turned = (((0,), (0,)), ((), ()))
        acc = lax.dot_general(near[...], hidden_near[...], turned, preferred_element_type=F32)
        acc += lax.dot_general(far[...], hidden_far[...], turned, preferred_element_type=F32)
        out_ref[...] = (acc * scale).astype(out_ref.dtype)

    last = pl.program_id(0) == pl.num_programs(0) - 1

    @pl.when(jnp.logical_not(last))
    def _():
        product(main_near, main_far)

    @pl.when(last)
    def _():
        product(rest_near, rest_far)


def weight_term(scale, main_near, rest_near, main_far, rest_far, hidden_near, hidden_far):
    tok, ff = hidden_near.shape
    width = rest_near.shape[1]
    blocks = main_near.shape[1] // width
    main = pl.BlockSpec((tok, width), lambda i: (0, jnp.minimum(i, blocks - 1)))
    rest = pl.BlockSpec((tok, width), lambda i: (0, 0))
    whole = pl.BlockSpec((tok, ff), lambda i: (0, 0))
    return pl.pallas_call(
        functools.partial(grad_kernel, scale),
        out_shape=jax.ShapeDtypeStruct(((blocks + 1) * width, ff), BF),
        grid=(blocks + 1,),
        in_specs=[main, rest, main, rest, whole, whole],
        out_specs=pl.BlockSpec((width, ff), lambda i: (i, 0)),
        name="weight_term",
    )(main_near, rest_near, main_far, rest_far, hidden_near, hidden_far)


def per_device(gate_pre, up_pre, down_weight, cotangent):
    tok, ff = gate_pre.shape
    rows, feat = cotangent.shape
    half = feat // NC
    lane = half // (NX * NYH)
    core, yl = lax.axis_index("c"), lax.axis_index("yl")
    first = yl == 0
    part = tok // NYL
    across = (((1,), (1,)), ((), ()))

    mine, other = split_columns(core, cotangent)
    from_core = lax.ppermute(other, "c", SWAP)
    gate_wide = gate_pre.astype(F32)
    up_wide = up_pre.astype(F32)
    sig = jax.nn.sigmoid(gate_wide)
    act = gate_wide * sig
    hidden = (act * up_wide).astype(BF)
    hidden, from_core = tie((hidden, from_core))
    hidden_peer = lax.ppermute(hidden, "c", SWAP)

    shard = jnp.concatenate([mine, from_core], axis=0)
    main, rest = shard[:, : GATHERED * lane], shard[:, GATHERED * lane :]
    main_all = lax.all_gather(main, "z", axis=0, tiled=True)
    main_all, rest = tie((main_all, rest))
    main_far = lax.ppermute(main_all, "yl", SWAP)

    rest_all = lax.all_gather(rest, "z", axis=0, tiled=True)
    rest_all, hidden, hidden_peer = tie((rest_all, hidden, hidden_peer))
    rest_far = lax.ppermute(rest_all, "yl", SWAP)
    hidden_z = hidden.reshape(NYL, NZ, rows, ff).transpose(1, 0, 2, 3).reshape(tok, ff)
    partial = jnp.dot(hidden_z, down_weight, preferred_element_type=F32).astype(BF)
    partial, hidden, hidden_peer = tie((partial, hidden, hidden_peer))
    out_z = lax.psum_scatter(partial, "z", scatter_dimension=0, tiled=True)

    def gathered_order(at):
        both = [lax.dynamic_slice_in_dim(h, at * part, part, 0) for h in (hidden, hidden_peer)]
        return jnp.stack([h.reshape(NZ, rows, ff) for h in both], axis=1).reshape(tok, ff)

    hidden_near, hidden_far = gathered_order(yl), gathered_order(1 - yl)
    main_far, rest_far, hidden_near, hidden_far = tie(
        (main_far, rest_far, hidden_near, hidden_far)
    )

    scale = 1.0 / (NX * NYH * NC)
    term = weight_term(scale, main_all, rest_all, main_far, rest_far, hidden_near, hidden_far)
    term = term.reshape(NX, NYH * lane, ff)
    term, main_all, main_far, gate_pre, up_pre, weight = tie(
        (term, main_all, main_far, gate_pre, up_pre, down_weight)
    )
    by_x = lax.all_to_all(term, "x", 0, 0)

    w_half = half_weight(core, weight)
    back_near, back_far = [
        lax.dot_general(
            jnp.concatenate(c, axis=1), w_half, across, preferred_element_type=F32
        ).reshape(NZ, NC, rows, ff)
        for c in ((main_all, rest_all), (main_far, rest_far))
    ]

    def rows_of(which):
        ordered = [back_near[:, which], back_far[:, which]]
        low, high = [b.reshape(part, ff) for b in ordered]
        return jnp.concatenate([jnp.where(first, low, high), jnp.where(first, high, low)], axis=0)

    back = rows_of(0) + lax.ppermute(rows_of(1), "c", SWAP)
    gate_wide = gate_pre.astype(F32)
    up_wide = up_pre.astype(F32)
    sig = jax.nn.sigmoid(gate_wide)
    act = gate_wide * sig
    gate_grad = (back * up_wide * sig * (1.0 + gate_wide * (1.0 - sig))).astype(BF)
    up_grad = (back * act).astype(BF)

    sum_x = by_x.astype(F32).sum(0).astype(BF).reshape(NYH, lane, ff)
    by_y = lax.all_to_all(sum_x, "yh", 0, 0)
    weight_grad = by_y.astype(F32).sum(0).astype(BF).T

    keep = lax.dynamic_slice_in_dim(out_z, yl * rows, rows, 0)
    give = lax.dynamic_slice_in_dim(out_z, (1 - yl) * rows, rows, 0)
    got = lax.ppermute(give, "yl", SWAP)
    output = (keep.astype(F32) + got.astype(F32)).astype(BF)
    return output, gate_grad, up_grad, weight_grad


def solution(mesh):
    fine = Mesh(
        mesh.devices.reshape(NX, NYH, NC, NYL, NZ), ("x", "yh", "c", "yl", "z")
    )
    dp, tensor = ("x", "yh", "c"), ("yl", "z")
    return jax.shard_map(
        per_device,
        mesh=fine,
        in_specs=(P(dp, tensor), P(dp, tensor), P(tensor, None), P(dp + tensor, None)),
        out_specs=(P(dp + tensor, None), P(dp, tensor), P(dp, tensor), P(tensor, dp)),
        check_vma=False,
    )
```

time: 173 us -> 180 us (1.040)
  blocking collectives: 43.5 us -> 61 us
  starting transfers between devices: 36.5 us -> 26.7 us
  matrix products: 21.3 us -> 12.4 us
  Pallas kernels: 7.22 us -> 15.7 us
  local copies, waits for them, and re-layouts: 8.92 us -> 13.8 us
  waiting for transfers between devices: 26.8 us -> 22.6 us
    all_gather x0 -> x1, blocking collectives: none -> 22.1 us  [per_device(): rest_all = lax.all_gather(rest, 'z', axis=0, tiled=True)]
    all_to_all x2 -> x1, waiting for transfers between devices: 26.3 us -> 13.6 us  [per_device(): by_y = lax.all_to_all(sum_x, 'yh', 0, 0)]
    dot_general x5 -> x3, matrix products: 21.3 us -> 12.4 us  [the longest x2 6.43 us: per_device(): lax.dot_general(jnp.concatenate(c, axis=1), w_half, across, preferred_ele...]
    ppermute x4, waiting for transfers between devices: 0.01 us -> 8.84 us  [the longest x1 8.83 us: per_device(): rest_far = lax.ppermute(rest_all, 'yl', SWAP)]
    pallas_call x0 -> x1, Pallas kernels: none -> 8.47 us  [weight_term(): pl.pallas_call(functools.partial(grad_kernel, scale), out_shape=jax.Shape...]
    all_to_all x2 -> x1, starting transfers between devices: 9.82 us -> 4.82 us  [per_device(): by_x = lax.all_to_all(term, 'x', 0, 0)]
    all_gather x1, blocking collectives: 43.5 us -> 39 us  [per_device(): main_all = lax.all_gather(main, 'z', axis=0, tiled=True)]
    concatenate x4 -> x1, other arithmetic: 6.25 us -> 1.91 us  [rows_of(): jnp.concatenate([jnp.where(first, low, high), jnp.where(first, high, low)...]
  transfers between devices with their start and end apart: 11 -> 9, of which waited for: 3 -> 3; matrix products, arithmetic and copies ran while one was open for 21% -> 16% of each run, Pallas kernels for 3% -> 8%
where the time goes in v5:
time: 180 us; the launch traced here: 179 us
  blocking collectives  61 us (34%)
  starting transfers between devices  26.7 us (15%)
  waiting for transfers between devices  22.6 us (13%)
  Pallas kernels  15.7 us (9%)
  between operations  14.3 us (8%)
  local copies, waits for them, and re-layouts  13.8 us (8%)
  matrix products  12.4 us (7%)
  other arithmetic  12.3 us (7%)
    all_gather x1, blocking collectives, per_device(): main_all = lax.all_gather(main, 'z', axis=0, tiled=True)  39 us
    all_gather x1, blocking collectives, per_device(): rest_all = lax.all_gather(rest, 'z', axis=0, tiled=True)  22.1 us
    all_to_all x1, waiting for transfers between devices, per_device(): by_y = lax.all_to_all(sum_x, 'yh', 0, 0)  13.6 us
    ppermute x1, waiting for transfers between devices, per_device(): rest_far = lax.ppermute(rest_all, 'yl', SWAP)  8.83 us
    pallas_call x1, Pallas kernels, weight_term(): pl.pallas_call(functools.partial(grad_kernel, scale), out_shape=jax.Shape...  8.47 us
    all_to_all x1, starting transfers between devices, per_device(): by_y = lax.all_to_all(sum_x, 'yh', 0, 0)  7.29 us
    dot_general x2, matrix products, per_device(): lax.dot_general(jnp.concatenate(c, axis=1), w_half, across, preferred_ele...  6.43 us
    dot_general x1, matrix products, per_device(): jnp.dot(hidden_z, down_weight, preferred_element_type=F32).astype(BF)  5.95 us
  transfers between devices with their start and end apart: 9, of which 3 were waited for; matrix products, arithmetic and copies ran while one was open for 16% of the time, Pallas kernels for 8%

profile of v5, /device:TPU:2, one launch (start us, length us, event | category | flops | bytes accessed | tf_op | source)
XLA Modules:
  0.0 178.8 jit_solution(5597761851843716173)
XLA Ops:
  7.2 1.6 split_columns.1
  8.8 1.9 %collective-permute-start = (bf16[12,2048]{1,0:T(8,128)(2,1)}, bf16[12,2048]{1,0:T(8,128)(2,1)S(1)}, u32[]{:S(2)}, u32[]{:S(2)}) collective-permute-start(bf16[12,2048]{1,0:T(8,128)(2,1)} %get-tuple-element.27), channel_id=1, source_target_pairs={{0,24},{24,0},{1,25},{25,1},{2,26},{26,2},{3,27},{27,3},{4,28},{28... | collective-permute-start | bytes 147464 | tf_op jit(solution)/shard_map/ppermute | solution.py:120
  10.7 1.3 fusion.20
  13.7 2.3 %collective-permute-start.1 = (bf16[288,640]{1,0:T(8,128)(2,1)S(1)}, bf16[288,640]{1,0:T(8,128)(2,1)}, u32[]{:S(2)}, u32[]{:S(2)}) collective-permute-start(bf16[288,640]{1,0:T(8,128)(2,1)S(1)} %fusion.20), channel_id=1, source_target_pairs={{0,24},{24,0},{1,25},{25,1},{2,26},{26,2},{3,27},{27,3},{4,28},{28... | collective-permute-start | bytes 1105928 | tf_op jit(solution)/shard_map/ppermute | solution.py:127
  16.0 39.0 %all_gather.6.refs_0_ = bf16[288,1792]{1,0:T(8,128)(2,1)S(1)} all-gather(bf16[24,1792]{1,0:T(8,128)(2,1)S(1)} %fusion.21), channel_id=1, replica_groups=mesh['x'=4,'yh'=4,'c'=2,'yl'=2,'z'=12] {'z'}, dimensions={0}, use_global_device_ids=true | all-gather | bytes 1118208 | tf_op jit(solution)/shard_map/all_gather | solution.py:131
  55.0 22.1 %all_gather.7.refs_1_ = bf16[288,256]{1,0:T(8,128)(2,1)} all-gather(bf16[24,256]{1,0:T(8,128)(2,1)S(1)} %pad_maximum_fusion.3), channel_id=1, replica_groups=mesh['x'=4,'yh'=4,'c'=2,'yl'=2,'z'=12] {'z'}, dimensions={0}, use_global_device_ids=true | all-gather | bytes 159744 | tf_op jit(solution)/shard_map/all_gather | solution.py:135
  77.3 6.0 %convolution_convert_fusion = bf16[288,4096]{1,0:T(8,128)(2,1)} fusion(bf16[288,640]{1,0:T(8,128)(2,1)S(1)} %reshape.46, bf16[640,4096]{1,0:T(8,128)(2,1)} %weight_ref), kind=kOutput, calls=%fused_computation | convolution fusion | flops 1511129088 | bytes 7970816 | tf_op jit(solution)/shard_map/dot_general | solution.py:139
  83.3 3.5 %collective-permute-start.3 = (bf16[288,1792]{1,0:T(8,128)(2,1)S(1)}, bf16[288,1792]{1,0:T(8,128)(2,1)S(1)}, u32[]{:S(2)}, u32[]{:S(2)}) collective-permute-start(bf16[288,1792]{1,0:T(8,128)(2,1)S(1)} %all_gather.6.refs_0_), channel_id=1, source_target_pairs={{0,12},{12,0},{1,13},{13,1},{2,14},{14,2},{3,15},{15,3},{4,16},{16... | collective-permute-start | bytes 3096584 | tf_op jit(solution)/shard_map/ppermute | solution.py:133
  86.8 2.4 %collective-permute-start.4 = (bf16[288,256]{1,0:T(8,128)(2,1)}, bf16[288,256]{1,0:T(8,128)(2,1)}, u32[]{:S(2)}, u32[]{:S(2)}) collective-permute-start(bf16[288,256]{1,0:T(8,128)(2,1)} %all_gather.7.refs_1_), channel_id=1, source_target_pairs={{0,12},{12,0},{1,13},{13,1},{2,14},{14,2},{3,15},{15,3},{4,16},{16... | collective-permute-start | bytes 442376 | tf_op jit(solution)/shard_map/ppermute | solution.py:137
  89.2 1.8 constant_dynamic-slice_fusion
  91.0 1.0 stack_reshape.12
  93.9 8.8 %collective-permute-done.4.refs_3_ = bf16[288,256]{1,0:T(8,128)(2,1)} collective-permute-done((bf16[288,256]{1,0:T(8,128)(2,1)}, bf16[288,256]{1,0:T(8,128)(2,1)}, u32[]{:S(2)}, u32[]{:S(2)}) %collective-permute-start.4) | collective-permute-done | bytes 147488 | tf_op jit(solution)/shard_map/ppermute | solution.py:137
  102.7 1.1 copy-done.3
  103.8 8.5 %weight_term.1 = bf16[2048,640]{1,0:T(8,128)(2,1)} custom-call(bf16[288,1792]{1,0:T(8,128)(2,1)} %copy-done, bf16[288,256]{1,0:T(8,128)(2,1)} %all_gather.7.refs_1_, bf16[288,1792]{1,0:T(8,128)(2,1)} %copy-done.3, bf16[288,256]{1,0:T(8,128)(2,1)} %collective-permute-done.4.refs_3_, bf16[288,640]{1,0:T(8,128)(2,1)} %reshape.47.refs_4_, ...), custom_call_target="tpu_custom_call" | custom-call | tf_op jit(solution)/shard_map/weight_term/pallas_call | solution.py:99
  112.3 4.8 %all-to-all-start = ((bf16[4,512,640]{2,1,0:T(8,128)(2,1)}), bf16[4,512,640]{2,1,0:T(8,128)(2,1)S(1)}, u32[]{:S(2)}, u32[]{:S(2)}) async-start(bf16[4,512,640]{2,1,0:T(8,128)(2,1)} %bitcast.9), calls=%async_computation.1 | async-start | bytes 5242880 | tf_op jit(solution)/shard_map/all_to_all | solution.py:158
  117.1 5.6 %half_weight.1 = bf16[640,2048]{1,0:T(8,128)(2,1)} custom-call(s32[1]{0:T(128)} %bitcast.core_ref, bf16[640,4096]{1,0:T(8,128)(2,1)} %weight_ref), custom_call_target="tpu_custom_call" | custom-call | tf_op jit(solution)/shard_map/half_weight/pallas_call | solution.py:59
  122.7 3.2 %fusion = f32[288,640]{1,0:T(8,128)S(1)} fusion(bf16[640,2048]{1,0:T(8,128)(2,1)} %half_weight.1, bf16[288,256]{1,0:T(8,128)(2,1)} %all_gather.7.refs_1_, bf16[288,1792]{1,0:T(8,128)(2,1)} %copy-done), kind=kOutput, calls=%fused_computation.1 | convolution fusion | flops 757334016 | bytes 4538368 | tf_op jit(solution)/shard_map/dot_general | solution.py:162
  126.0 1.1 reshape.50
  127.1 3.2 %fusion.4 = f32[288,640]{1,0:T(8,128)S(1)} fusion(bf16[640,2048]{1,0:T(8,128)(2,1)} %half_weight.1, bf16[288,256]{1,0:T(8,128)(2,1)} %collective-permute-done.4.refs_3_, bf16[288,1792]{1,0:T(8,128)(2,1)} %copy-done.3), kind=kOutput, calls=%fused_computation.5 | convolution fusion | flops 757334016 | bytes 4538368 | tf_op jit(solution)/shard_map/dot_general | solution.py:162
  130.3 1.0 reshape.51
  131.4 2.7 %slice_select_fusion.3 = (f32[12,1,12,640]{3,2,1,0:T(8,128)}, f32[12,1,12,640]{3,2,1,0:T(8,128)S(1)}, f32[12,1,12,640]{3,2,1,0:T(8,128)}, f32[12,1,12,640]{3,2,1,0:T(8,128)}) fusion(f32[12,2,12,640]{3,2,1,0:T(8,128)} %reshape.51, f32[12,2,12,640]{3,2,1,0:T(8,128)} %reshape.50, pred[]{:T(512)S(6)} %eq.3), kind=kLoop, calls=%fused_computation.34 | loop fusion | flops 368640 | bytes 2949121 | tf_op jit(solution)/shard_map/jit(_where)/select_n | solution.py:171
  134.1 1.1 select_n.58
  135.1 1.8 %select_n.56 = f32[144,640]{1,0:T(8,128)} reshape(f32[12,1,12,640]{3,2,1,0:T(8,128)} %get-tuple-element.55) | data formatting | bytes 737280 | tf_op jit(solution)/shard_map/jit(_where)/select_n | solution.py:171
  136.9 1.9 %pad_maximum_fusion = f32[288,640]{1,0:T(8,128)} fusion(f32[144,640]{1,0:T(8,128)S(1)} %select_n.58, f32[144,640]{1,0:T(8,128)} %select_n.56), kind=kLoop, calls=%fused_computation.27 | loop fusion | flops 184320 | bytes 1474560 | tf_op jit(solution)/shard_map/concatenate | solution.py:171
  138.9 1.9 %collective-permute-start.5 = (f32[288,640]{1,0:T(8,128)}, f32[288,640]{1,0:T(8,128)}, u32[]{:S(2)}, u32[]{:S(2)}) collective-permute-start(f32[288,640]{1,0:T(8,128)} %pad_maximum_fusion), channel_id=1, source_target_pairs={{0,24},{24,0},{1,25},{25,1},{2,26},{26,2},{3,27},{27,3},{4,28},{28... | collective-permute-start | bytes 2211848 | tf_op jit(solution)/shard_map/ppermute | solution.py:173
  140.8 1.4 reduce_sum.24
  142.2 7.3 %all-to-all-start.1 = ((bf16[4,128,640]{2,1,0:T(8,128)(2,1)}), bf16[4,128,640]{2,1,0:T(8,128)(2,1)S(1)}, u32[]{:S(2)}, u32[]{:S(2)}) async-start(bf16[4,128,640]{2,1,0:T(8,128)(2,1)} %bitcast.3), calls=%async_computation.2 | async-start | bytes 1310720 | tf_op jit(solution)/shard_map/all_to_all | solution.py:182
  149.5 1.1 select_n.52
  150.6 1.0 constant_dynamic-slice_fusion.4
  151.6 2.6 %collective-permute-start.2 = (bf16[12,4096]{1,0:T(8,128)(2,1)S(1)}, bf16[12,4096]{1,0:T(8,128)(2,1)S(1)}, u32[]{:S(2)}, u32[]{:S(2)}) collective-permute-start(bf16[12,4096]{1,0:T(8,128)(2,1)S(1)} %constant_dynamic-slice_fusion.4), channel_id=1, source_target_pairs={{0,12},{12,0},{1,13},{13,1},{2,14},{14,2},{3,15},{15,3},{4,16},{16... | collective-permute-start | bytes 294920 | tf_op jit(solution)/shard_map/ppermute | solution.py:187
  154.3 2.4 %fusion.19 = (bf16[288,640]{1,0:T(8,128)(2,1)}, bf16[288,640]{1,0:T(8,128)(2,1)}) fusion(bf16[288,640]{1,0:T(8,128)(2,1)S(1)} %copy-done.2, f32[288,640]{1,0:T(8,128)} %collective-permute-done.5, f32[144,640]{1,0:T(8,128)S(1)} %select_n.54, f32[144,640]{1,0:T(8,128)S(1)} %select_n.52, bf16[288,640]{1,0:T(8,128)(2,1)S(1)} %copy-done.1), kind=kLoop, calls=%fused_computation.25 | loop fusion | flops 3133440 | bytes 2949120 | tf_op jit(solution)/shard_map/convert_element_type | solution.py:179
  156.7 13.6 %all-to-all-done.1 = bf16[4,128,640]{2,1,0:T(8,128)(2,1)S(1)} async-done(((bf16[4,128,640]{2,1,0:T(8,128)(2,1)}), bf16[4,128,640]{2,1,0:T(8,128)(2,1)S(1)}, u32[]{:S(2)}, u32[]{:S(2)}) %all-to-all-start.1) | async-done | bytes 655392 | tf_op jit(solution)/shard_map/all_to_all | solution.py:182
  (34 shorter events, 5.6 us)
Async XLA Ops:
  7.2 143.4 %reduce-scatter.2.cloned.1.call-start = ((), (), s32[]{:S(2)}) async-start(), calls=%async_computation.3 | async-start | bytes 2555904 | tf_op jit(solution)/shard_map/reduce_scatter | solution.py:141
  8.8 3.3 %collective-permute-start = (bf16[12,2048]{1,0:T(8,128)(2,1)}, bf16[12,2048]{1,0:T(8,128)(2,1)S(1)}, u32[]{:S(2)}, u32[]{:S(2)}) collective-permute-start(bf16[12,2048]{1,0:T(8,128)(2,1)} %get-tuple-element.27), channel_id=1, source_target_pairs={{0,24},{24,0},{1,25},{25,1},{2,26},{26,2},{3,27},{27,3},{4,28},{28... | collective-permute-start | bytes 147464 | tf_op jit(solution)/shard_map/ppermute | solution.py:120
  13.7 63.4 %collective-permute-start.1 = (bf16[288,640]{1,0:T(8,128)(2,1)S(1)}, bf16[288,640]{1,0:T(8,128)(2,1)}, u32[]{:S(2)}, u32[]{:S(2)}) collective-permute-start(bf16[288,640]{1,0:T(8,128)(2,1)S(1)} %fusion.20), channel_id=1, source_target_pairs={{0,24},{24,0},{1,25},{25,1},{2,26},{26,2},{3,27},{27,3},{4,28},{28... | collective-permute-start | bytes 1105928 | tf_op jit(solution)/shard_map/ppermute | solution.py:127
  55.0 28.3 %copy-start = (bf16[288,1792]{1,0:T(8,128)(2,1)}, bf16[288,1792]{1,0:T(8,128)(2,1)S(1)}, u32[]{:S(2)}) copy-start(bf16[288,1792]{1,0:T(8,128)(2,1)S(1)} %all_gather.6.refs_0_) | copy-start | bytes 3096580
  83.3 19.4 %collective-permute-start.3 = (bf16[288,1792]{1,0:T(8,128)(2,1)S(1)}, bf16[288,1792]{1,0:T(8,128)(2,1)S(1)}, u32[]{:S(2)}, u32[]{:S(2)}) collective-permute-start(bf16[288,1792]{1,0:T(8,128)(2,1)S(1)} %all_gather.6.refs_0_), channel_id=1, source_target_pairs={{0,12},{12,0},{1,13},{13,1},{2,14},{14,2},{3,15},{15,3},{4,16},{16... | collective-permute-start | bytes 3096584 | tf_op jit(solution)/shard_map/ppermute | solution.py:133
  86.8 15.9 %collective-permute-start.4 = (bf16[288,256]{1,0:T(8,128)(2,1)}, bf16[288,256]{1,0:T(8,128)(2,1)}, u32[]{:S(2)}, u32[]{:S(2)}) collective-permute-start(bf16[288,256]{1,0:T(8,128)(2,1)} %all_gather.7.refs_1_), channel_id=1, source_target_pairs={{0,12},{12,0},{1,13},{13,1},{2,14},{14,2},{3,15},{15,3},{4,16},{16... | collective-permute-start | bytes 442376 | tf_op jit(solution)/shard_map/ppermute | solution.py:137
  102.7 1.1 copy-start.3
  112.3 28.5 %all-to-all-start = ((bf16[4,512,640]{2,1,0:T(8,128)(2,1)}), bf16[4,512,640]{2,1,0:T(8,128)(2,1)S(1)}, u32[]{:S(2)}, u32[]{:S(2)}) async-start(bf16[4,512,640]{2,1,0:T(8,128)(2,1)} %bitcast.9), calls=%async_computation.1 | async-start | bytes 5242880 | tf_op jit(solution)/shard_map/all_to_all | solution.py:158
  138.9 15.4 %collective-permute-start.5 = (f32[288,640]{1,0:T(8,128)}, f32[288,640]{1,0:T(8,128)}, u32[]{:S(2)}, u32[]{:S(2)}) collective-permute-start(f32[288,640]{1,0:T(8,128)} %pad_maximum_fusion), channel_id=1, source_target_pairs={{0,24},{24,0},{1,25},{25,1},{2,26},{26,2},{3,27},{27,3},{4,28},{28... | collective-permute-start | bytes 2211848 | tf_op jit(solution)/shard_map/ppermute | solution.py:173
  142.2 12.1 %copy-start.1 = (bf16[288,640]{1,0:T(8,128)(2,1)S(1)}, bf16[288,640]{1,0:T(8,128)(2,1)}, u32[]{:S(2)}) copy-start(bf16[288,640]{1,0:T(8,128)(2,1)} %param.5) | copy-start | bytes 1105924
  142.2 12.1 %copy-start.2 = (bf16[288,640]{1,0:T(8,128)(2,1)S(1)}, bf16[288,640]{1,0:T(8,128)(2,1)}, u32[]{:S(2)}) copy-start(bf16[288,640]{1,0:T(8,128)(2,1)} %param.4) | copy-start | bytes 1105924
  142.2 28.1 %all-to-all-start.1 = ((bf16[4,128,640]{2,1,0:T(8,128)(2,1)}), bf16[4,128,640]{2,1,0:T(8,128)(2,1)S(1)}, u32[]{:S(2)}, u32[]{:S(2)}) async-start(bf16[4,128,640]{2,1,0:T(8,128)(2,1)} %bitcast.3), calls=%async_computation.2 | async-start | bytes 1310720 | tf_op jit(solution)/shard_map/all_to_all | solution.py:182
  150.6 20.6 %copy-start.4 = (bf16[24,4096]{1,0:T(8,128)(2,1)S(1)}, bf16[24,4096]{1,0:T(8,128)(2,1)}, u32[]{:S(2)}) copy-start(bf16[24,4096]{1,0:T(8,128)(2,1)} %reduce-scatter.2.cloned.1.call-done) | copy-start | bytes 589828
  151.6 19.6 %collective-permute-start.2 = (bf16[12,4096]{1,0:T(8,128)(2,1)S(1)}, bf16[12,4096]{1,0:T(8,128)(2,1)S(1)}, u32[]{:S(2)}, u32[]{:S(2)}) collective-permute-start(bf16[12,4096]{1,0:T(8,128)(2,1)S(1)} %constant_dynamic-slice_fusion.4), channel_id=1, source_target_pairs={{0,12},{12,0},{1,13},{13,1},{2,14},{14,2},{3,15},{15,3},{4,16},{16... | collective-permute-start | bytes 294920 | tf_op jit(solution)/shard_map/ppermute | solution.py:187
Sparse Core Ops, SparseCore 0:
  83.4 58.6 reduce-scatter.1

commit v6 on v1

v6 whole, which is shorter than its diff:
```python
import jax
import jax.numpy as jnp
from jax import lax
from jax.experimental import pallas as pl
from jax.experimental.pallas import tpu as pltpu
from jax.sharding import Mesh, PartitionSpec as P

NX, NYH, NC, NYL, NZ = 4, 4, 2, 2, 12
NB = NX * NYH
GATHERED = 14
BF, F32 = jnp.bfloat16, jnp.float32
SWAP = [(0, 1), (1, 0)]
DIAGONAL = [(0, 3), (1, 2), (2, 1), (3, 0)]
tie = lax.optimization_barrier


def quarter(ref, core, yl):
    lane = ref.shape[1] // (NB * NC)
    half = lane // NYL
    pieces = []
    for pair in range(NB):
        at = (pair * NC + core) * lane
        pieces.append(ref[:, at : at + lane][:, yl * half : (yl + 1) * half])
    return jnp.concatenate(pieces, axis=1)


def split_kernel(place_ref, cot_ref, *out_refs):
    for core in range(NC):
        for yl in range(NYL):

            @pl.when(place_ref[0] == core * NYL + yl)
            def _():
                wanted = ((core, yl), (1 - core, yl), (core, 1 - yl), (1 - core, 1 - yl))
                for out_ref, (c, y) in zip(out_refs, wanted):
                    out_ref[...] = quarter(cot_ref, c, y)


def split_columns(place, cot):
    rows, feat = cot.shape
    vmem = pl.BlockSpec(memory_space=pltpu.VMEM)
    return pl.pallas_call(
        split_kernel,
        out_shape=[jax.ShapeDtypeStruct((rows, feat // 4), cot.dtype)] * 4,
        in_specs=[pl.BlockSpec(memory_space=pltpu.SMEM), vmem],
        out_specs=[vmem] * 4,
        name="split_columns",
    )(place, cot)


def weight_kernel(place_ref, weight_ref, near_ref, far_ref):
    for core in range(NC):
        for yl in range(NYL):

            @pl.when(place_ref[0] == core * NYL + yl)
            def _():
                near_ref[...] = quarter(weight_ref, core, yl)
                far_ref[...] = quarter(weight_ref, core, 1 - yl)


def weight_quarters(place, weight):
    ff, feat = weight.shape
    step = 128
    return pl.pallas_call(
        weight_kernel,
        out_shape=[jax.ShapeDtypeStruct((ff, feat // 4), weight.dtype)] * 2,
        grid=(ff // step,),
        in_specs=[
            pl.BlockSpec(memory_space=pltpu.SMEM),
            pl.BlockSpec((step, feat), lambda i: (i, 0)),
        ],
        out_specs=[pl.BlockSpec((step, feat // 4), lambda i: (i, 0))] * 2,
        name="weight_quarters",
    )(place, weight)


def per_device(gate_pre, up_pre, down_weight, cotangent):
    tok, ff = gate_pre.shape
    rows, feat = cotangent.shape
    block = feat // (NB * NC)
    half = block // NYL
    both = NYL * rows
    core, yl = lax.axis_index("c"), lax.axis_index("yl")
    first = yl == 0
    place = (core * NYL + yl).reshape(1)
    across = (((1,), (1,)), ((), ()))

    mine, to_core, to_yl, to_diag = split_columns(place, cotangent)
    from_core = lax.ppermute(to_core, "c", SWAP)
    from_yl = lax.ppermute(to_yl, "yl", SWAP)
    from_diag = lax.ppermute(to_diag, ("c", "yl"), DIAGONAL)

    gate_wide = gate_pre.astype(F32)
    up_wide = up_pre.astype(F32)
    sig = jax.nn.sigmoid(gate_wide)
    act = gate_wide * sig
    hidden = (act * up_wide).astype(BF)
    hidden_z = hidden.reshape(NYL, NZ, rows, ff).transpose(1, 0, 2, 3).reshape(tok, ff)
    hidden_z, from_core, from_yl, from_diag = tie((hidden_z, from_core, from_yl, from_diag))
    hidden_core = lax.ppermute(hidden_z, "c", SWAP)
    hidden_yl = lax.ppermute(hidden_z, "yl", SWAP)
    hidden_diag = lax.ppermute(hidden_z, ("c", "yl"), DIAGONAL)
    partial = jnp.dot(hidden_z, down_weight, preferred_element_type=F32).astype(BF)

    shard = jnp.concatenate(
        [
            jnp.where(first, mine, from_yl),
            jnp.where(first, from_yl, mine),
            jnp.where(first, from_core, from_diag),
            jnp.where(first, from_diag, from_core),
        ],
        axis=0,
    )
    main, rest = shard[:, : GATHERED * half], shard[:, GATHERED * half :]
    rest = jnp.broadcast_to(rest[None], (NZ,) + rest.shape)
    main, rest, partial = tie((main, rest, partial))
    out_z = lax.psum_scatter(partial, "z", scatter_dimension=0, tiled=True)
    rest_all = lax.all_to_all(rest, "z", 0, 0).reshape(NC * tok, -1)
    main_all = lax.all_gather(main, "z", axis=0, tiled=True)
    near = jnp.concatenate([main_all, rest_all], axis=1)
    near, hidden_core, hidden_yl, hidden_diag = tie((near, hidden_core, hidden_yl, hidden_diag))

    def stacked(a, b):
        return jnp.stack([a.reshape(NZ, both, ff), b.reshape(NZ, both, ff)], axis=1)

    hidden_all = jnp.concatenate(
        [stacked(hidden_z, hidden_core), stacked(hidden_yl, hidden_diag)], axis=-1
    ).reshape(NC * tok, NYL * ff)

    grad_acc = lax.dot_general(
        near, hidden_all, (((0,), (0,)), ((), ())), preferred_element_type=F32
    )
    term = (grad_acc / (NX * NYH * NC)).astype(BF).reshape(NX, NYH * half, NYL * ff)
    term, near, gate_pre, up_pre, weight = tie((term, near, gate_pre, up_pre, down_weight))
    by_x = lax.all_to_all(term, "x", 0, 0)

    far = lax.ppermute(near, "yl", SWAP)
    weight_near, weight_far = weight_quarters(place, weight)
    back = lax.dot_general(near, weight_near, across, preferred_element_type=F32)
    back = back + lax.dot_general(far, weight_far, across, preferred_element_type=F32)
    back = back.reshape(NZ, NC, both, ff)
    back_z = back[:, 0] + lax.ppermute(back[:, 1], "c", SWAP)
    back = back_z.reshape(NZ, NYL, rows, ff).transpose(1, 0, 2, 3).reshape(tok, ff)
    gate_wide = gate_pre.astype(F32)
    up_wide = up_pre.astype(F32)
    sig = jax.nn.sigmoid(gate_wide)
    act = gate_wide * sig
    gate_grad = (back * up_wide * sig * (1.0 + gate_wide * (1.0 - sig))).astype(BF)
    up_grad = (back * act).astype(BF)

    sum_x = by_x.astype(F32).sum(0).astype(BF).reshape(NYH, half, NYL, ff)
    own, other = sum_x[:, :, 0], sum_x[:, :, 1]
    sum_x = jnp.stack([jnp.where(first, own, other), jnp.where(first, other, own)], axis=1)
    by_y = lax.all_to_all(sum_x.reshape(NYH * NYL, half, ff), ("yh", "yl"), 0, 0)
    by_y = by_y.reshape(NYH, NYL * half, ff)
    weight_grad = by_y.astype(F32).sum(0).astype(BF).T

    keep = lax.dynamic_slice_in_dim(out_z, yl * rows, rows, 0)
    give = lax.dynamic_slice_in_dim(out_z, (1 - yl) * rows, rows, 0)
    got = lax.ppermute(give, "yl", SWAP)
    output = (keep.astype(F32) + got.astype(F32)).astype(BF)
    return output, gate_grad, up_grad, weight_grad


def solution(mesh):
    fine = Mesh(
        mesh.devices.reshape(NX, NYH, NC, NYL, NZ), ("x", "yh", "c", "yl", "z")
    )
    dp, tensor = ("x", "yh", "c"), ("yl", "z")
    return jax.shard_map(
        per_device,
        mesh=fine,
        in_specs=(P(dp, tensor), P(dp, tensor), P(tensor, None), P(dp + tensor, None)),
        out_specs=(P(dp + tensor, None), P(dp, tensor), P(dp, tensor), P(tensor, dp)),
        check_vma=False,
    )
```

time: 199 us -> 176 us (0.88)
  the two profiles are of different devices: /device:TPU:2 before, /device:TPU:1 now
where the time goes in v6:
time: 176 us; the launch traced here: 175 us
  starting transfers between devices  53.4 us (30%)
  blocking collectives  40.1 us (23%)
  waiting for transfers between devices  29.1 us (17%)
  matrix products  15.1 us (9%)
  between operations  14.4 us (8%)
  local copies, waits for them, and re-layouts  7.59 us (4%)
  other arithmetic  7.5 us (4%)
  Pallas kernels  7.46 us (4%)
    all_gather x1, blocking collectives, per_device(): main_all = lax.all_gather(main, 'z', axis=0, tiled=True)  40.1 us
    ppermute x1, waiting for transfers between devices, per_device(): far = lax.ppermute(near, 'yl', SWAP)  16.2 us
    all_to_all x1, waiting for transfers between devices, per_device(): lax.all_to_all(sum_x.reshape(NYH * NYL, half, ff), ('yh', 'yl'), 0, 0)  12.5 us
    ppermute x1, starting transfers between devices, per_device(): from_core = lax.ppermute(to_core, 'c', SWAP)  12.4 us
    all_to_all x1, starting transfers between devices, per_device(): rest_all = lax.all_to_all(rest, 'z', 0, 0).reshape(NC * tok, -1)  6.95 us
    all_to_all x1, starting transfers between devices, per_device(): lax.all_to_all(sum_x.reshape(NYH * NYL, half, ff), ('yh', 'yl'), 0, 0)  6.03 us
    dot_general x1, matrix products, per_device(): jnp.dot(hidden_z, down_weight, preferred_element_type=F32).astype(BF)  5.95 us
    pallas_call x1, Pallas kernels, weight_quarters(): pl.pallas_call(weight_kernel, out_shape=[jax.ShapeDtypeStruct((ff, feat /...  5.8 us
  transfers between devices with their start and end apart: 13, of which 3 were waited for; matrix products, arithmetic and copies ran while one was open for 12% of the time, Pallas kernels for 3%

profile of v6, /device:TPU:1, one launch (start us, length us, event | category | flops | bytes accessed | tf_op | source)
XLA Modules:
  0.0 174.5 jit_solution(10795858357060648268)
XLA Ops:
  7.2 1.7 split_columns.1
  8.9 12.4 %collective-permute-start = (bf16[12,1024]{1,0:T(8,128)(2,1)}, bf16[12,1024]{1,0:T(8,128)(2,1)S(1)}, u32[]{:S(2)}, u32[]{:S(2)}) collective-permute-start(bf16[12,1024]{1,0:T(8,128)(2,1)} %get-tuple-element.27), channel_id=1, source_target_pairs={{0,24},{24,0},{1,25},{25,1},{2,26},{26,2},{3,27},{27,3},{4,28},{28... | collective-permute-start | bytes 73736 | tf_op jit(solution)/shard_map/ppermute | solution.py:88
  21.3 1.9 %collective-permute-start.1 = (bf16[12,1024]{1,0:T(8,128)(2,1)}, bf16[12,1024]{1,0:T(8,128)(2,1)S(1)}, u32[]{:S(2)}, u32[]{:S(2)}) collective-permute-start(bf16[12,1024]{1,0:T(8,128)(2,1)} %get-tuple-element.28), channel_id=1, source_target_pairs={{0,12},{12,0},{1,13},{13,1},{2,14},{14,2},{3,15},{15,3},{4,16},{16... | collective-permute-start | bytes 73736 | tf_op jit(solution)/shard_map/ppermute | solution.py:89
  23.2 3.5 %collective-permute-start.2 = (bf16[12,1024]{1,0:T(8,128)(2,1)}, bf16[12,1024]{1,0:T(8,128)(2,1)S(1)}, u32[]{:S(2)}, u32[]{:S(2)}) collective-permute-start(bf16[12,1024]{1,0:T(8,128)(2,1)} %get-tuple-element.29), channel_id=1, source_target_pairs={{0,36},{12,24},{24,12},{36,0},{1,37},{13,25},{25,13},{37,1},{2,38}... | collective-permute-start | bytes 73736 | tf_op jit(solution)/shard_map/ppermute | solution.py:90
  26.8 1.3 fusion.13
  29.0 6.0 %convolution_convert_fusion = bf16[288,4096]{1,0:T(8,128)(2,1)} fusion(bf16[288,640]{1,0:T(8,128)(2,1)S(1)} %reshape.85, bf16[640,4096]{1,0:T(8,128)(2,1)} %weight_ref), kind=kOutput, calls=%fused_computation | convolution fusion | flops 1511129088 | bytes 7970816 | tf_op jit(solution)/shard_map/dot_general | solution.py:102
  35.7 3.3 %collective-permute-start.6 = (bf16[288,640]{1,0:T(8,128)(2,1)S(1)}, bf16[288,640]{1,0:T(8,128)(2,1)S(1)}, u32[]{:S(2)}, u32[]{:S(2)}) collective-permute-start(bf16[288,640]{1,0:T(8,128)(2,1)S(1)} %reshape.85), channel_id=1, source_target_pairs={{0,36},{12,24},{24,12},{36,0},{1,37},{13,25},{25,13},{37,1},{2,38}... | collective-permute-start | bytes 1105928 | tf_op jit(solution)/shard_map/ppermute | solution.py:101
  39.0 2.0 %collective-permute-start.5 = (bf16[288,640]{1,0:T(8,128)(2,1)S(1)}, bf16[288,640]{1,0:T(8,128)(2,1)S(1)}, u32[]{:S(2)}, u32[]{:S(2)}) collective-permute-start(bf16[288,640]{1,0:T(8,128)(2,1)S(1)} %reshape.85), channel_id=1, source_target_pairs={{0,12},{12,0},{1,13},{13,1},{2,14},{14,2},{3,15},{15,3},{4,16},{16... | collective-permute-start | bytes 1105928 | tf_op jit(solution)/shard_map/ppermute | solution.py:100
  41.1 2.5 %collective-permute-start.4 = (bf16[288,640]{1,0:T(8,128)(2,1)S(1)}, bf16[288,640]{1,0:T(8,128)(2,1)S(1)}, u32[]{:S(2)}, u32[]{:S(2)}) collective-permute-start(bf16[288,640]{1,0:T(8,128)(2,1)S(1)} %reshape.85), channel_id=1, source_target_pairs={{0,24},{24,0},{1,25},{25,1},{2,26},{26,2},{3,27},{27,3},{4,28},{28... | collective-permute-start | bytes 1105928 | tf_op jit(solution)/shard_map/ppermute | solution.py:99
  43.5 6.9 %all-to-all-start = ((bf16[12,48,128]{2,1,0:T(8,128)(2,1)}), bf16[12,48,128]{2,1,0:T(8,128)(2,1)S(1)}, u32[]{:S(2)}, u32[]{:S(2)}) async-start(bf16[12,48,128]{2,1,0:T(8,128)(2,1)} %broadcast_in_dim.2), calls=%async_computation.1 | async-start | bytes 294912 | tf_op jit(solution)/shard_map/all_to_all | solution.py:117
  50.5 40.1 %all_gather.3 = bf16[576,896]{1,0:T(8,128)(2,1)S(1)} all-gather(bf16[48,896]{1,0:T(8,128)(2,1)S(1)} %slice-done), channel_id=1, replica_groups=mesh['x'=4,'yh'=4,'c'=2,'yl'=2,'z'=12] {'z'}, dimensions={0}, use_global_device_ids=true | all-gather | bytes 1118208 | tf_op jit(solution)/shard_map/all_gather | solution.py:118
  90.9 1.0 copy-done.3
  91.9 3.8 %multiply_convert_fusion = bf16[1024,1280]{1,0:T(8,128)(2,1)} fusion(bf16[576,1024]{1,0:T(8,128)(2,1)S(1)} %pad_maximum_fusion, bf16[576,1280]{1,0:T(8,128)(2,1)S(1)} %bitcast.54), kind=kOutput, calls=%fused_computation.1 | convolution fusion | flops 1512570880 | bytes 5275648 | tf_op jit(solution)/shard_map/dot_general | solution.py:129
  95.7 3.7 %all-to-all-start.1 = ((bf16[4,256,1280]{2,1,0:T(8,128)(2,1)}), bf16[4,256,1280]{2,1,0:T(8,128)(2,1)S(1)}, u32[]{:S(2)}, u32[]{:S(2)}) async-start(bf16[4,256,1280]{2,1,0:T(8,128)(2,1)} %bitcast.49), calls=%async_computation.2 | async-start | bytes 5242880 | tf_op jit(solution)/shard_map/all_to_all | solution.py:134
  99.3 1.9 %collective-permute-start.7 = (bf16[576,1024]{1,0:T(8,128)(2,1)}, bf16[576,1024]{1,0:T(8,128)(2,1)}, u32[]{:S(2)}, u32[]{:S(2)}) collective-permute-start(bf16[576,1024]{1,0:T(8,128)(2,1)} %copy-done.3), channel_id=1, source_target_pairs={{0,12},{12,0},{1,13},{13,1},{2,14},{14,2},{3,15},{15,3},{4,16},{16... | collective-permute-start | bytes 3538952 | tf_op jit(solution)/shard_map/ppermute | solution.py:136
  101.3 5.8 %weight_quarters.1 = (bf16[640,1024]{1,0:T(8,128)(2,1)}, bf16[640,1024]{1,0:T(8,128)(2,1)}) custom-call(s32[1]{0:T(128)} %bitcast.place_ref, bf16[640,4096]{1,0:T(8,128)(2,1)} %weight_ref), custom_call_target="tpu_custom_call" | custom-call | tf_op jit(solution)/shard_map/weight_quarters/pallas_call | solution.py:63
  107.1 2.9 %fusion.14 = f32[576,640]{1,0:T(8,128)S(1)} fusion(bf16[576,1024]{1,0:T(8,128)(2,1)} %copy-done.3, bf16[640,1024]{1,0:T(8,128)(2,1)} %get-tuple-element.43), kind=kOutput, calls=%fused_computation.40 | convolution fusion | flops 754974720 | bytes 3964928 | tf_op jit(solution)/shard_map/dot_general | solution.py:138
  110.0 16.2 %collective-permute-done.7 = bf16[576,1024]{1,0:T(8,128)(2,1)} collective-permute-done((bf16[576,1024]{1,0:T(8,128)(2,1)}, bf16[576,1024]{1,0:T(8,128)(2,1)}, u32[]{:S(2)}, u32[]{:S(2)}) %collective-permute-start.7) | collective-permute-done | bytes 1179680 | tf_op jit(solution)/shard_map/ppermute | solution.py:136
  126.2 2.4 %convolution_add_fusion = f32[576,640]{1,0:T(8,128)S(1)} fusion(f32[576,640]{1,0:T(8,128)S(1)} %fusion.14, bf16[576,1024]{1,0:T(8,128)(2,1)} %collective-permute-done.7, bf16[640,1024]{1,0:T(8,128)(2,1)S(1)} %copy-done.7), kind=kOutput, calls=%fused_computation.3 | convolution fusion | flops 755343360 | bytes 5439488 | tf_op jit(solution)/shard_map/dot_general | solution.py:139
  128.6 1.0 slice_bitcast_fusion
  130.0 5.6 %collective-permute-start.8 = (f32[12,24,640]{2,1,0:T(8,128)}, f32[12,24,640]{2,1,0:T(8,128)}, u32[]{:S(2)}, u32[]{:S(2)}) collective-permute-start(f32[12,24,640]{2,1,0:T(8,128)} %slice_bitcast_fusion), channel_id=1, source_target_pairs={{0,24},{24,0},{1,25},{25,1},{2,26},{26,2},{3,27},{27,3},{4,28},{28... | collective-permute-start | bytes 2211848 | tf_op jit(solution)/shard_map/ppermute | solution.py:141
  135.7 0.8 reduce_sum.24
  136.6 1.5 broadcast_select_fusion.1
  138.3 0.9 copy.39
  139.2 6.0 %all-to-all-start.2 = ((bf16[8,64,640]{2,1,0:T(8,128)(2,1)}), bf16[8,64,640]{2,1,0:T(8,128)(2,1)S(1)}, u32[]{:S(2)}, u32[]{:S(2)}) async-start(bf16[8,64,640]{2,1,0:T(8,128)(2,1)} %bitcast.17), calls=%async_computation.3 | async-start | bytes 1310720 | tf_op jit(solution)/shard_map/all_to_all | solution.py:153
  145.3 1.4 fusion.12
  147.0 0.8 copy-done.1
  147.9 1.2 fusion.11
  149.1 1.0 constant_dynamic-slice_fusion
  150.1 3.4 %collective-permute-start.3 = (bf16[12,4096]{1,0:T(8,128)(2,1)S(1)}, bf16[12,4096]{1,0:T(8,128)(2,1)S(1)}, u32[]{:S(2)}, u32[]{:S(2)}) collective-permute-start(bf16[12,4096]{1,0:T(8,128)(2,1)S(1)} %constant_dynamic-slice_fusion), channel_id=1, source_target_pairs={{0,12},{12,0},{1,13},{13,1},{2,14},{14,2},{3,15},{15,3},{4,16},{16... | collective-permute-start | bytes 294920 | tf_op jit(solution)/shard_map/ppermute | solution.py:159
  153.5 12.5 %all-to-all-done.2 = bf16[8,64,640]{2,1,0:T(8,128)(2,1)S(1)} async-done(((bf16[8,64,640]{2,1,0:T(8,128)(2,1)}), bf16[8,64,640]{2,1,0:T(8,128)(2,1)S(1)}, u32[]{:S(2)}, u32[]{:S(2)}) %all-to-all-start.2) | async-done | bytes 655392 | tf_op jit(solution)/shard_map/all_to_all | solution.py:153
  166.2 0.8 copy.40
  (47 shorter events, 3.6 us)
Async XLA Ops:
  7.2 142.0 %reduce-scatter.2.cloned.1.call-start = ((), (), s32[]{:S(2)}) async-start(), calls=%async_computation.4 | async-start | bytes 2555904 | tf_op jit(solution)/shard_map/reduce_scatter | solution.py:116
  8.9 19.5 %collective-permute-start = (bf16[12,1024]{1,0:T(8,128)(2,1)}, bf16[12,1024]{1,0:T(8,128)(2,1)S(1)}, u32[]{:S(2)}, u32[]{:S(2)}) collective-permute-start(bf16[12,1024]{1,0:T(8,128)(2,1)} %get-tuple-element.27), channel_id=1, source_target_pairs={{0,24},{24,0},{1,25},{25,1},{2,26},{26,2},{3,27},{27,3},{4,28},{28... | collective-permute-start | bytes 73736 | tf_op jit(solution)/shard_map/ppermute | solution.py:88
  21.3 7.1 %collective-permute-start.1 = (bf16[12,1024]{1,0:T(8,128)(2,1)}, bf16[12,1024]{1,0:T(8,128)(2,1)S(1)}, u32[]{:S(2)}, u32[]{:S(2)}) collective-permute-start(bf16[12,1024]{1,0:T(8,128)(2,1)} %get-tuple-element.28), channel_id=1, source_target_pairs={{0,12},{12,0},{1,13},{13,1},{2,14},{14,2},{3,15},{15,3},{4,16},{16... | collective-permute-start | bytes 73736 | tf_op jit(solution)/shard_map/ppermute | solution.py:89
  23.2 5.4 %collective-permute-start.2 = (bf16[12,1024]{1,0:T(8,128)(2,1)}, bf16[12,1024]{1,0:T(8,128)(2,1)S(1)}, u32[]{:S(2)}, u32[]{:S(2)}) collective-permute-start(bf16[12,1024]{1,0:T(8,128)(2,1)} %get-tuple-element.29), channel_id=1, source_target_pairs={{0,36},{12,24},{24,12},{36,0},{1,37},{13,25},{25,13},{37,1},{2,38}... | collective-permute-start | bytes 73736 | tf_op jit(solution)/shard_map/ppermute | solution.py:90
  28.1 0.8 copy-start.6
  29.0 6.0 %copy-start.5 = (bf16[48,1024]{1,0:T(8,128)(2,1)}, bf16[48,1024]{1,0:T(8,128)(2,1)S(1)}, u32[]{:S(2)}) copy-start(bf16[48,1024]{1,0:T(8,128)(2,1)S(1)} %pad_maximum_fusion.2) | copy-start | bytes 294916
  34.9 15.6 %slice-start = ((bf16[48,1024]{1,0:T(8,128)(2,1)}), bf16[48,896]{1,0:T(8,128)(2,1)S(1)}, s32[]{:S(2)}) async-start(bf16[48,1024]{1,0:T(8,128)(2,1)} %copy-done.5), calls=%async_computation.5 | async-start | bytes 172032 | tf_op jit(solution)/shard_map/slice | solution.py:113
  35.7 55.1 %collective-permute-start.6 = (bf16[288,640]{1,0:T(8,128)(2,1)S(1)}, bf16[288,640]{1,0:T(8,128)(2,1)S(1)}, u32[]{:S(2)}, u32[]{:S(2)}) collective-permute-start(bf16[288,640]{1,0:T(8,128)(2,1)S(1)} %reshape.85), channel_id=1, source_target_pairs={{0,36},{12,24},{24,12},{36,0},{1,37},{13,25},{25,13},{37,1},{2,38}... | collective-permute-start | bytes 1105928 | tf_op jit(solution)/shard_map/ppermute | solution.py:101
  39.0 51.8 %collective-permute-start.5 = (bf16[288,640]{1,0:T(8,128)(2,1)S(1)}, bf16[288,640]{1,0:T(8,128)(2,1)S(1)}, u32[]{:S(2)}, u32[]{:S(2)}) collective-permute-start(bf16[288,640]{1,0:T(8,128)(2,1)S(1)} %reshape.85), channel_id=1, source_target_pairs={{0,12},{12,0},{1,13},{13,1},{2,14},{14,2},{3,15},{15,3},{4,16},{16... | collective-permute-start | bytes 1105928 | tf_op jit(solution)/shard_map/ppermute | solution.py:100
  41.1 49.7 %collective-permute-start.4 = (bf16[288,640]{1,0:T(8,128)(2,1)S(1)}, bf16[288,640]{1,0:T(8,128)(2,1)S(1)}, u32[]{:S(2)}, u32[]{:S(2)}) collective-permute-start(bf16[288,640]{1,0:T(8,128)(2,1)S(1)} %reshape.85), channel_id=1, source_target_pairs={{0,24},{24,0},{1,25},{25,1},{2,26},{26,2},{3,27},{27,3},{4,28},{28... | collective-permute-start | bytes 1105928 | tf_op jit(solution)/shard_map/ppermute | solution.py:99
  43.5 47.1 %all-to-all-start = ((bf16[12,48,128]{2,1,0:T(8,128)(2,1)}), bf16[12,48,128]{2,1,0:T(8,128)(2,1)S(1)}, u32[]{:S(2)}, u32[]{:S(2)}) async-start(bf16[12,48,128]{2,1,0:T(8,128)(2,1)} %broadcast_in_dim.2), calls=%async_computation.1 | async-start | bytes 294912 | tf_op jit(solution)/shard_map/all_to_all | solution.py:117
  90.8 1.1 copy-start.3
  95.7 40.0 %all-to-all-start.1 = ((bf16[4,256,1280]{2,1,0:T(8,128)(2,1)}), bf16[4,256,1280]{2,1,0:T(8,128)(2,1)S(1)}, u32[]{:S(2)}, u32[]{:S(2)}) async-start(bf16[4,256,1280]{2,1,0:T(8,128)(2,1)} %bitcast.49), calls=%async_computation.2 | async-start | bytes 5242880 | tf_op jit(solution)/shard_map/all_to_all | solution.py:134
  99.3 26.9 %collective-permute-start.7 = (bf16[576,1024]{1,0:T(8,128)(2,1)}, bf16[576,1024]{1,0:T(8,128)(2,1)}, u32[]{:S(2)}, u32[]{:S(2)}) collective-permute-start(bf16[576,1024]{1,0:T(8,128)(2,1)} %copy-done.3), channel_id=1, source_target_pairs={{0,12},{12,0},{1,13},{13,1},{2,14},{14,2},{3,15},{15,3},{4,16},{16... | collective-permute-start | bytes 3538952 | tf_op jit(solution)/shard_map/ppermute | solution.py:136
  107.1 19.1 %copy-start.7 = (bf16[640,1024]{1,0:T(8,128)(2,1)S(1)}, bf16[640,1024]{1,0:T(8,128)(2,1)}, u32[]{:S(2)}) copy-start(bf16[640,1024]{1,0:T(8,128)(2,1)} %get-tuple-element.44) | copy-start | bytes 3932164
  128.6 1.4 copy-start
  130.0 15.3 %collective-permute-start.8 = (f32[12,24,640]{2,1,0:T(8,128)}, f32[12,24,640]{2,1,0:T(8,128)}, u32[]{:S(2)}, u32[]{:S(2)}) collective-permute-start(f32[12,24,640]{2,1,0:T(8,128)} %slice_bitcast_fusion), channel_id=1, source_target_pairs={{0,24},{24,0},{1,25},{25,1},{2,26},{26,2},{3,27},{27,3},{4,28},{28... | collective-permute-start | bytes 2211848 | tf_op jit(solution)/shard_map/ppermute | solution.py:141
  139.2 26.8 %all-to-all-start.2 = ((bf16[8,64,640]{2,1,0:T(8,128)(2,1)}), bf16[8,64,640]{2,1,0:T(8,128)(2,1)S(1)}, u32[]{:S(2)}, u32[]{:S(2)}) async-start(bf16[8,64,640]{2,1,0:T(8,128)(2,1)} %bitcast.17), calls=%async_computation.3 | async-start | bytes 1310720 | tf_op jit(solution)/shard_map/all_to_all | solution.py:153
  146.8 1.0 copy-start.1
  146.8 1.1 copy-start.2
  149.1 17.8 %copy-start.4 = (bf16[24,4096]{1,0:T(8,128)(2,1)S(1)}, bf16[24,4096]{1,0:T(8,128)(2,1)}, u32[]{:S(2)}) copy-start(bf16[24,4096]{1,0:T(8,128)(2,1)} %reduce-scatter.2.cloned.1.call-done) | copy-start | bytes 589828
  150.1 16.8 %collective-permute-start.3 = (bf16[12,4096]{1,0:T(8,128)(2,1)S(1)}, bf16[12,4096]{1,0:T(8,128)(2,1)S(1)}, u32[]{:S(2)}, u32[]{:S(2)}) collective-permute-start(bf16[12,4096]{1,0:T(8,128)(2,1)S(1)} %constant_dynamic-slice_fusion), channel_id=1, source_target_pairs={{0,12},{12,0},{1,13},{13,1},{2,14},{14,2},{3,15},{15,3},{4,16},{16... | collective-permute-start | bytes 294920 | tf_op jit(solution)/shard_map/ppermute | solution.py:159
Sparse Core Ops, SparseCore 0:
  35.8 62.2 reduce-scatter.1

commit v7 on v6

--- a/solution.py
+++ b/solution.py
@@ -5,9 +5,9 @@
 from jax.experimental.pallas import tpu as pltpu
 from jax.sharding import Mesh, PartitionSpec as P
 
-NX, NYH, NC, NYL, NZ = 4, 4, 2, 2, 12
+NX, NYH, NC, NYL, NZH, NZL = 4, 4, 2, 2, 6, 2
+NZ = NZH * NZL
 NB = NX * NYH
-GATHERED = 14
 BF, F32 = jnp.bfloat16, jnp.float32
 SWAP = [(0, 1), (1, 0)]
 DIAGONAL = [(0, 3), (1, 2), (2, 1), (3, 0)]
@@ -97,9 +97,6 @@
     hidden_z = hidden.reshape(NYL, NZ, rows, ff).transpose(1, 0, 2, 3).reshape(tok, ff)
     hidden_z, from_core, from_yl, from_diag = tie((hidden_z, from_core, from_yl, from_diag))
     hidden_core = lax.ppermute(hidden_z, "c", SWAP)
-    hidden_yl = lax.ppermute(hidden_z, "yl", SWAP)
-    hidden_diag = lax.ppermute(hidden_z, ("c", "yl"), DIAGONAL)
-    partial = jnp.dot(hidden_z, down_weight, preferred_element_type=F32).astype(BF)
 
     shard = jnp.concatenate(
         [
@@ -110,21 +107,21 @@
         ],
         axis=0,
     )
-    main, rest = shard[:, : GATHERED * half], shard[:, GATHERED * half :]
-    rest = jnp.broadcast_to(rest[None], (NZ,) + rest.shape)
-    main, rest, partial = tie((main, rest, partial))
-    out_z = lax.psum_scatter(partial, "z", scatter_dimension=0, tiled=True)
-    rest_all = lax.all_to_all(rest, "z", 0, 0).reshape(NC * tok, -1)
-    main_all = lax.all_gather(main, "z", axis=0, tiled=True)
-    near = jnp.concatenate([main_all, rest_all], axis=1)
-    near, hidden_core, hidden_yl, hidden_diag = tie((near, hidden_core, hidden_yl, hidden_diag))
+    hidden_near = jnp.stack([h.reshape(NZ, both, ff) for h in (hidden_z, hidden_core)], axis=1)
+    shard, hidden_near, hidden_z = tie((shard, hidden_near, hidden_z))
+    hidden_far = lax.ppermute(hidden_near.reshape(NC * tok, ff), "yl", SWAP)
+    mine_z = lax.all_gather(shard, "zh", axis=0, tiled=True)
+    mine_z, hidden_z, hidden_far = tie((mine_z, hidden_z, hidden_far))
+    other_z = lax.ppermute(mine_z, "zl", SWAP)
 
-    def stacked(a, b):
-        return jnp.stack([a.reshape(NZ, both, ff), b.reshape(NZ, both, ff)], axis=1)
-
-    hidden_all = jnp.concatenate(
-        [stacked(hidden_z, hidden_core), stacked(hidden_yl, hidden_diag)], axis=-1
-    ).reshape(NC * tok, NYL * ff)
+    partial = jnp.dot(hidden_z, down_weight, preferred_element_type=F32).astype(BF)
+    out_z = lax.psum_scatter(partial, ("zh", "zl"), scatter_dimension=0, tiled=True)
+    _, other_z, hidden_near, hidden_far = tie((partial, other_z, hidden_near, hidden_far))
+    even = lax.axis_index("zl") == 0
+    ours, theirs = [rows_z.reshape(NZH, NC * both, -1) for rows_z in (mine_z, other_z)]
+    near = jnp.stack([jnp.where(even, ours, theirs), jnp.where(even, theirs, ours)], axis=1)
+    near = near.reshape(NC * tok, -1)
+    hidden_all = jnp.concatenate([hidden_near.reshape(NC * tok, ff), hidden_far], axis=1)
 
     grad_acc = lax.dot_general(
         near, hidden_all, (((0,), (0,)), ((), ())), preferred_element_type=F32
@@ -136,6 +133,10 @@
     far = lax.ppermute(near, "yl", SWAP)
     weight_near, weight_far = weight_quarters(place, weight)
     back = lax.dot_general(near, weight_near, across, preferred_element_type=F32)
+    sum_x = by_x.astype(F32).sum(0).astype(BF).reshape(NYH, half, NYL, ff)
+    own, other = sum_x[:, :, 0], sum_x[:, :, 1]
+    sum_x = jnp.stack([jnp.where(first, own, other), jnp.where(first, other, own)], axis=1)
+    sum_x, far, back = tie((sum_x, far, back))
     back = back + lax.dot_general(far, weight_far, across, preferred_element_type=F32)
     back = back.reshape(NZ, NC, both, ff)
     back_z = back[:, 0] + lax.ppermute(back[:, 1], "c", SWAP)
@@ -147,9 +148,6 @@
     gate_grad = (back * up_wide * sig * (1.0 + gate_wide * (1.0 - sig))).astype(BF)
     up_grad = (back * act).astype(BF)
 
-    sum_x = by_x.astype(F32).sum(0).astype(BF).reshape(NYH, half, NYL, ff)
-    own, other = sum_x[:, :, 0], sum_x[:, :, 1]
-    sum_x = jnp.stack([jnp.where(first, own, other), jnp.where(first, other, own)], axis=1)
     by_y = lax.all_to_all(sum_x.reshape(NYH * NYL, half, ff), ("yh", "yl"), 0, 0)
     by_y = by_y.reshape(NYH, NYL * half, ff)
     weight_grad = by_y.astype(F32).sum(0).astype(BF).T
@@ -163,9 +161,9 @@
 
 def solution(mesh):
     fine = Mesh(
-        mesh.devices.reshape(NX, NYH, NC, NYL, NZ), ("x", "yh", "c", "yl", "z")
+        mesh.devices.reshape(NX, NYH, NC, NYL, NZH, NZL), ("x", "yh", "c", "yl", "zh", "zl")
     )
-    dp, tensor = ("x", "yh", "c"), ("yl", "z")
+    dp, tensor = ("x", "yh", "c"), ("yl", "zh", "zl")
     return jax.shard_map(
         per_device,
         mesh=fine,

time: 176 us -> 156 us (0.89)
  blocking collectives: 40.1 us -> 20.2 us
  local copies, waits for them, and re-layouts: 7.59 us -> 5.55 us
    all_gather x1, blocking collectives: 40.1 us -> 20.2 us  [per_device(): mine_z = lax.all_gather(shard, 'zh', axis=0, tiled=True)]
    ppermute x1, waiting for transfers between devices: 16.2 us -> 0.01 us  [per_device(): far = lax.ppermute(near, 'yl', SWAP)]
    all_to_all x1, waiting for transfers between devices: 0.01 us -> 12.2 us  [per_device(): by_x = lax.all_to_all(term, 'x', 0, 0)]
    all_to_all x1 -> x0, starting transfers between devices: 6.95 us -> none  [per_device(): rest_all = lax.all_to_all(rest, 'z', 0, 0).reshape(NC * tok, -1)]
    ppermute x2, waiting for transfers between devices: 0.01 us -> 4.01 us  [the longest x1 4.01 us: per_device(): other_z = lax.ppermute(mine_z, 'zl', SWAP)]
    ppermute x1, starting transfers between devices: 1.92 us -> 5.22 us  [per_device(): far = lax.ppermute(near, 'yl', SWAP)]
    ppermute x1, starting transfers between devices: 5.64 us -> 7.49 us  [per_device(): back_z = back[:, 0] + lax.ppermute(back[:, 1], 'c', SWAP)]
  transfers between devices with their start and end apart: 13 -> 12, of which waited for: 3 -> 5; matrix products, arithmetic and copies ran while one was open for 12% -> 17% of each run, Pallas kernels for 3% -> 4%
where the time goes in v7:
time: 156 us
  starting transfers between devices  53.6 us (34%)
  waiting for transfers between devices  30.6 us (20%)
  blocking collectives  20.2 us (13%)
  matrix products  16.2 us (10%)
  between operations  14.4 us (9%)
  Pallas kernels  7.61 us (5%)
  other arithmetic  7.42 us (5%)
  local copies, waits for them, and re-layouts  5.55 us (4%)
    all_gather x1, blocking collectives, per_device(): mine_z = lax.all_gather(shard, 'zh', axis=0, tiled=True)  20.2 us
    all_to_all x1, waiting for transfers between devices, per_device(): lax.all_to_all(sum_x.reshape(NYH * NYL, half, ff), ('yh', 'yl'), 0, 0)  12.7 us
    ppermute x1, starting transfers between devices, per_device(): from_core = lax.ppermute(to_core, 'c', SWAP)  12.4 us
    all_to_all x1, waiting for transfers between devices, per_device(): by_x = lax.all_to_all(term, 'x', 0, 0)  12.2 us
    ppermute x1, starting transfers between devices, per_device(): back_z = back[:, 0] + lax.ppermute(back[:, 1], 'c', SWAP)  7.49 us
    all_to_all x1, starting transfers between devices, per_device(): lax.all_to_all(sum_x.reshape(NYH * NYL, half, ff), ('yh', 'yl'), 0, 0)  6.83 us
    pallas_call x1, Pallas kernels, weight_quarters(): pl.pallas_call(weight_kernel, out_shape=[jax.ShapeDtypeStruct((ff, feat /...  5.95 us
    dot_general x1, matrix products, per_device(): jnp.dot(hidden_z, down_weight, preferred_element_type=F32).astype(BF)  5.92 us
  transfers between devices with their start and end apart: 12, of which 5 were waited for; matrix products, arithmetic and copies ran while one was open for 17% of the time, Pallas kernels for 4%

profile of v7, /device:TPU:1, one launch (start us, length us, event | category | flops | bytes accessed | tf_op | source)
XLA Modules:
  0.0 155.6 jit_solution(1878355063186230669)
XLA Ops:
  7.2 1.7 %split_columns.1 = (bf16[12,1024]{1,0:T(8,128)(2,1)}, bf16[12,1024]{1,0:T(8,128)(2,1)}, bf16[12,1024]{1,0:T(8,128)(2,1)}, bf16[12,1024]{1,0:T(8,128)(2,1)}) custom-call(s32[1]{0:T(128)} %bitcast.place_ref, bf16[12,4096]{1,0:T(8,128)(2,1)} %cot_ref.1), custom_call_target="tpu_custom_call" | custom-call | tf_op jit(solution)/shard_map/split_columns/pallas_call | solution.py:41
  8.9 12.4 %collective-permute-start = (bf16[12,1024]{1,0:T(8,128)(2,1)}, bf16[12,1024]{1,0:T(8,128)(2,1)S(1)}, u32[]{:S(2)}, u32[]{:S(2)}) collective-permute-start(bf16[12,1024]{1,0:T(8,128)(2,1)} %get-tuple-element.32), channel_id=1, source_target_pairs={{0,24},{24,0},{1,25},{25,1},{2,26},{26,2},{3,27},{27,3},{4,28},{28... | collective-permute-start | bytes 73736 | tf_op jit(solution)/shard_map/ppermute | solution.py:88
  21.3 1.9 %collective-permute-start.1 = (bf16[12,1024]{1,0:T(8,128)(2,1)}, bf16[12,1024]{1,0:T(8,128)(2,1)S(1)}, u32[]{:S(2)}, u32[]{:S(2)}) collective-permute-start(bf16[12,1024]{1,0:T(8,128)(2,1)} %get-tuple-element.33), channel_id=1, source_target_pairs={{0,12},{12,0},{1,13},{13,1},{2,14},{14,2},{3,15},{15,3},{4,16},{16... | collective-permute-start | bytes 73736 | tf_op jit(solution)/shard_map/ppermute | solution.py:89
  23.2 3.5 %collective-permute-start.2 = (bf16[12,1024]{1,0:T(8,128)(2,1)}, bf16[12,1024]{1,0:T(8,128)(2,1)S(1)}, u32[]{:S(2)}, u32[]{:S(2)}) collective-permute-start(bf16[12,1024]{1,0:T(8,128)(2,1)} %get-tuple-element.34), channel_id=1, source_target_pairs={{0,36},{12,24},{24,12},{36,0},{1,37},{13,25},{25,13},{37,1},{2,38}... | collective-permute-start | bytes 73736 | tf_op jit(solution)/shard_map/ppermute | solution.py:90
  26.8 1.3 fusion.16
  28.7 2.1 %collective-permute-start.3 = (bf16[288,640]{1,0:T(8,128)(2,1)S(1)}, bf16[288,640]{1,0:T(8,128)(2,1)S(1)}, u32[]{:S(2)}, u32[]{:S(2)}) collective-permute-start(bf16[288,640]{1,0:T(8,128)(2,1)S(1)} %reshape.127), channel_id=1, source_target_pairs={{0,24},{24,0},{1,25},{25,1},{2,26},{26,2},{3,27},{27,3},{4,28},{28... | collective-permute-start | bytes 1105928 | tf_op jit(solution)/shard_map/ppermute | solution.py:99
  30.9 1.4 collective-permute-done.3
  32.4 3.4 %collective-permute-start.4 = (bf16[576,640]{1,0:T(8,128)(2,1)S(1)}, bf16[576,640]{1,0:T(8,128)(2,1)S(1)}, u32[]{:S(2)}, u32[]{:S(2)}) collective-permute-start(bf16[576,640]{1,0:T(8,128)(2,1)S(1)} %bitcast.62), channel_id=1, source_target_pairs={{0,12},{12,0},{1,13},{13,1},{2,14},{14,2},{3,15},{15,3},{4,16},{16... | collective-permute-start | bytes 2211848 | tf_op jit(solution)/shard_map/ppermute | solution.py:112
  35.7 20.2 %all_gather.3 = bf16[288,1024]{1,0:T(8,128)(2,1)S(1)} all-gather(bf16[48,1024]{1,0:T(8,128)(2,1)S(1)} %pad_maximum_fusion.3), channel_id=1, replica_groups=mesh['x'=4,'yh'=4,'c'=2,'yl'=2,'zh'=6,'zl'=2] {'zh'}, dimensions={0}, use_global_device_ids=true | all-gather | bytes 688128 | tf_op jit(solution)/shard_map/all_gather | solution.py:113
  56.0 3.1 %collective-permute-start.6 = (bf16[288,1024]{1,0:T(8,128)(2,1)S(1)}, bf16[288,1024]{1,0:T(8,128)(2,1)S(1)}, u32[]{:S(2)}, u32[]{:S(2)}) collective-permute-start(bf16[288,1024]{1,0:T(8,128)(2,1)S(1)} %all_gather.3), channel_id=1, source_target_pairs={{0,1},{1,0},{2,3},{3,2},{4,5},{5,4},{6,7},{7,6},{8,9},{9,8},{10,11... | collective-permute-start | bytes 1769480 | tf_op jit(solution)/shard_map/ppermute | solution.py:115
  59.1 5.9 %convolution_convert_fusion = bf16[288,4096]{1,0:T(8,128)(2,1)} fusion(bf16[288,640]{1,0:T(8,128)(2,1)S(1)} %reshape.127, bf16[640,4096]{1,0:T(8,128)(2,1)} %weight_ref), kind=kOutput, calls=%fused_computation | convolution fusion | flops 1511129088 | bytes 7970816 | tf_op jit(solution)/shard_map/dot_general | solution.py:117
  65.1 4.0 %collective-permute-done.6 = bf16[288,1024]{1,0:T(8,128)(2,1)S(1)} collective-permute-done((bf16[288,1024]{1,0:T(8,128)(2,1)S(1)}, bf16[288,1024]{1,0:T(8,128)(2,1)S(1)}, u32[]{:S(2)}, u32[]{:S(2)}) %collective-permute-start.6) | collective-permute-done | bytes 589856 | tf_op jit(solution)/shard_map/ppermute | solution.py:115
  69.3 3.8 %multiply_convert_fusion = bf16[1024,1280]{1,0:T(8,128)(2,1)} fusion(bf16[576,1024]{1,0:T(8,128)(2,1)S(1)} %bitcast.59, bf16[576,640]{1,0:T(8,128)(2,1)S(1)} %collective-permute-done.4, bf16[576,640]{1,0:T(8,128)(2,1)S(1)} %bitcast.63), kind=kOutput, calls=%fused_computation.1 | convolution fusion | flops 1515520000 | bytes 5275648 | tf_op jit(solution)/shard_map/dot_general | solution.py:126
  73.1 4.1 %all-to-all-start = ((bf16[4,256,1280]{2,1,0:T(8,128)(2,1)}), bf16[4,256,1280]{2,1,0:T(8,128)(2,1)S(1)}, u32[]{:S(2)}, u32[]{:S(2)}) async-start(bf16[4,256,1280]{2,1,0:T(8,128)(2,1)} %bitcast.51), calls=%async_computation.1 | async-start | bytes 5242880 | tf_op jit(solution)/shard_map/all_to_all | solution.py:131
  77.2 5.2 %collective-permute-start.7 = (bf16[576,1024]{1,0:T(8,128)(2,1)}, bf16[576,1024]{1,0:T(8,128)(2,1)}, u32[]{:S(2)}, u32[]{:S(2)}) collective-permute-start(bf16[576,1024]{1,0:T(8,128)(2,1)} %bitcast.60), channel_id=1, source_target_pairs={{0,12},{12,0},{1,13},{13,1},{2,14},{14,2},{3,15},{15,3},{4,16},{16... | collective-permute-start | bytes 3538952 | tf_op jit(solution)/shard_map/ppermute | solution.py:133
  82.4 5.9 %weight_quarters.1 = (bf16[640,1024]{1,0:T(8,128)(2,1)}, bf16[640,1024]{1,0:T(8,128)(2,1)}) custom-call(s32[1]{0:T(128)} %bitcast.place_ref, bf16[640,4096]{1,0:T(8,128)(2,1)} %weight_ref), custom_call_target="tpu_custom_call" | custom-call | tf_op jit(solution)/shard_map/weight_quarters/pallas_call | solution.py:63
  88.4 4.0 %fusion.18 = f32[576,640]{1,0:T(8,128)} fusion(bf16[576,1024]{1,0:T(8,128)(2,1)} %bitcast.61, bf16[640,1024]{1,0:T(8,128)(2,1)} %get-tuple-element.51), kind=kOutput, calls=%fused_computation.44 | convolution fusion | flops 754974720 | bytes 3964928 | tf_op jit(solution)/shard_map/dot_general | solution.py:135
  92.3 12.2 %all-to-all-done = bf16[4,256,1280]{2,1,0:T(8,128)(2,1)S(1)} async-done(((bf16[4,256,1280]{2,1,0:T(8,128)(2,1)}), bf16[4,256,1280]{2,1,0:T(8,128)(2,1)S(1)}, u32[]{:S(2)}, u32[]{:S(2)}) %all-to-all-start) | async-done | bytes 2621472 | tf_op jit(solution)/shard_map/all_to_all | solution.py:131
  104.5 0.8 reduce_sum.24
  105.5 1.5 broadcast_select_fusion.1
  107.2 1.1 copy-done.6
  108.3 2.5 %fusion.19 = f32[576,640]{1,0:T(8,128)S(1)} fusion(bf16[576,1024]{1,0:T(8,128)(2,1)} %collective-permute-done.7, bf16[640,1024]{1,0:T(8,128)(2,1)S(1)} %copy-done.6), kind=kOutput, calls=%fused_computation.45 | convolution fusion | flops 754974720 | bytes 3964928 | tf_op jit(solution)/shard_map/dot_general | solution.py:140
  111.1 7.5 %collective-permute-start.8 = (f32[12,24,640]{2,1,0:T(8,128)S(1)}, f32[12,24,640]{2,1,0:T(8,128)}, u32[]{:S(2)}, u32[]{:S(2)}) collective-permute-start(f32[12,24,640]{2,1,0:T(8,128)S(1)} %slice_bitcast_fusion), channel_id=1, source_target_pairs={{0,24},{24,0},{1,25},{25,1},{2,26},{26,2},{3,27},{27,3},{4,28},{28... | collective-permute-start | bytes 2211848 | tf_op jit(solution)/shard_map/ppermute | solution.py:142
  118.6 0.9 copy.39
  119.5 6.8 %all-to-all-start.1 = ((bf16[8,64,640]{2,1,0:T(8,128)(2,1)}), bf16[8,64,640]{2,1,0:T(8,128)(2,1)S(1)}, u32[]{:S(2)}, u32[]{:S(2)}) async-start(bf16[8,64,640]{2,1,0:T(8,128)(2,1)} %bitcast.18), calls=%async_computation.2 | async-start | bytes 1310720 | tf_op jit(solution)/shard_map/all_to_all | solution.py:151
  126.3 1.2 fusion.15
  127.8 0.8 copy-done.1
  128.7 1.2 fusion.14
  130.0 1.0 constant_dynamic-slice_fusion
  131.0 3.4 %collective-permute-start.5 = (bf16[12,4096]{1,0:T(8,128)(2,1)S(1)}, bf16[12,4096]{1,0:T(8,128)(2,1)S(1)}, u32[]{:S(2)}, u32[]{:S(2)}) collective-permute-start(bf16[12,4096]{1,0:T(8,128)(2,1)S(1)} %constant_dynamic-slice_fusion), channel_id=1, source_target_pairs={{0,12},{12,0},{1,13},{13,1},{2,14},{14,2},{3,15},{15,3},{4,16},{16... | collective-permute-start | bytes 294920 | tf_op jit(solution)/shard_map/ppermute | solution.py:157
  134.4 12.7 %all-to-all-done.1 = bf16[8,64,640]{2,1,0:T(8,128)(2,1)S(1)} async-done(((bf16[8,64,640]{2,1,0:T(8,128)(2,1)}), bf16[8,64,640]{2,1,0:T(8,128)(2,1)S(1)}, u32[]{:S(2)}, u32[]{:S(2)}) %all-to-all-start.1) | async-done | bytes 655392 | tf_op jit(solution)/shard_map/all_to_all | solution.py:151
  147.2 0.8 copy.40
  (41 shorter events, 2.6 us)
Async XLA Ops:
  7.2 122.8 %reduce-scatter.2.cloned.1.call-start = ((), (), s32[]{:S(2)}) async-start(), calls=%async_computation.3 | async-start | bytes 2555904 | tf_op jit(solution)/shard_map/reduce_scatter | solution.py:118
  8.9 19.5 %collective-permute-start = (bf16[12,1024]{1,0:T(8,128)(2,1)}, bf16[12,1024]{1,0:T(8,128)(2,1)S(1)}, u32[]{:S(2)}, u32[]{:S(2)}) collective-permute-start(bf16[12,1024]{1,0:T(8,128)(2,1)} %get-tuple-element.32), channel_id=1, source_target_pairs={{0,24},{24,0},{1,25},{25,1},{2,26},{26,2},{3,27},{27,3},{4,28},{28... | collective-permute-start | bytes 73736 | tf_op jit(solution)/shard_map/ppermute | solution.py:88
  21.3 7.1 %collective-permute-start.1 = (bf16[12,1024]{1,0:T(8,128)(2,1)}, bf16[12,1024]{1,0:T(8,128)(2,1)S(1)}, u32[]{:S(2)}, u32[]{:S(2)}) collective-permute-start(bf16[12,1024]{1,0:T(8,128)(2,1)} %get-tuple-element.33), channel_id=1, source_target_pairs={{0,12},{12,0},{1,13},{13,1},{2,14},{14,2},{3,15},{15,3},{4,16},{16... | collective-permute-start | bytes 73736 | tf_op jit(solution)/shard_map/ppermute | solution.py:89
  23.2 5.4 %collective-permute-start.2 = (bf16[12,1024]{1,0:T(8,128)(2,1)}, bf16[12,1024]{1,0:T(8,128)(2,1)S(1)}, u32[]{:S(2)}, u32[]{:S(2)}) collective-permute-start(bf16[12,1024]{1,0:T(8,128)(2,1)} %get-tuple-element.34), channel_id=1, source_target_pairs={{0,36},{12,24},{24,12},{36,0},{1,37},{13,25},{25,13},{37,1},{2,38}... | collective-permute-start | bytes 73736 | tf_op jit(solution)/shard_map/ppermute | solution.py:90
  28.1 2.7 %copy-start.5 = (bf16[12,1024]{1,0:T(8,128)(2,1)S(1)}, bf16[12,1024]{1,0:T(8,128)(2,1)}, u32[]{:S(2)}) copy-start(bf16[12,1024]{1,0:T(8,128)(2,1)} %get-tuple-element.31) | copy-start | bytes 73732
  28.7 3.6 %collective-permute-start.3 = (bf16[288,640]{1,0:T(8,128)(2,1)S(1)}, bf16[288,640]{1,0:T(8,128)(2,1)S(1)}, u32[]{:S(2)}, u32[]{:S(2)}) collective-permute-start(bf16[288,640]{1,0:T(8,128)(2,1)S(1)} %reshape.127), channel_id=1, source_target_pairs={{0,24},{24,0},{1,25},{25,1},{2,26},{26,2},{3,27},{27,3},{4,28},{28... | collective-permute-start | bytes 1105928 | tf_op jit(solution)/shard_map/ppermute | solution.py:99
  32.4 23.6 %collective-permute-start.4 = (bf16[576,640]{1,0:T(8,128)(2,1)S(1)}, bf16[576,640]{1,0:T(8,128)(2,1)S(1)}, u32[]{:S(2)}, u32[]{:S(2)}) collective-permute-start(bf16[576,640]{1,0:T(8,128)(2,1)S(1)} %bitcast.62), channel_id=1, source_target_pairs={{0,12},{12,0},{1,13},{13,1},{2,14},{14,2},{3,15},{15,3},{4,16},{16... | collective-permute-start | bytes 2211848 | tf_op jit(solution)/shard_map/ppermute | solution.py:112
  56.0 13.1 %collective-permute-start.6 = (bf16[288,1024]{1,0:T(8,128)(2,1)S(1)}, bf16[288,1024]{1,0:T(8,128)(2,1)S(1)}, u32[]{:S(2)}, u32[]{:S(2)}) collective-permute-start(bf16[288,1024]{1,0:T(8,128)(2,1)S(1)} %all_gather.3), channel_id=1, source_target_pairs={{0,1},{1,0},{2,3},{3,2},{4,5},{5,4},{6,7},{7,6},{8,9},{9,8},{10,11... | collective-permute-start | bytes 1769480 | tf_op jit(solution)/shard_map/ppermute | solution.py:115
  69.3 3.8 %copy-start.3 = (bf16[6,2,48,1024]{3,2,1,0:T(8,128)(2,1)}, bf16[6,2,48,1024]{3,2,1,0:T(8,128)(2,1)S(1)}, u32[]{:S(2)}) copy-start(bf16[6,2,48,1024]{3,2,1,0:T(8,128)(2,1)S(1)} %pad_maximum_fusion) | copy-start | bytes 3538948
  73.1 31.4 %all-to-all-start = ((bf16[4,256,1280]{2,1,0:T(8,128)(2,1)}), bf16[4,256,1280]{2,1,0:T(8,128)(2,1)S(1)}, u32[]{:S(2)}, u32[]{:S(2)}) async-start(bf16[4,256,1280]{2,1,0:T(8,128)(2,1)} %bitcast.51), calls=%async_computation.1 | async-start | bytes 5242880 | tf_op jit(solution)/shard_map/all_to_all | solution.py:131
  77.2 30.0 %collective-permute-start.7 = (bf16[576,1024]{1,0:T(8,128)(2,1)}, bf16[576,1024]{1,0:T(8,128)(2,1)}, u32[]{:S(2)}, u32[]{:S(2)}) collective-permute-start(bf16[576,1024]{1,0:T(8,128)(2,1)} %bitcast.60), channel_id=1, source_target_pairs={{0,12},{12,0},{1,13},{13,1},{2,14},{14,2},{3,15},{15,3},{4,16},{16... | collective-permute-start | bytes 3538952 | tf_op jit(solution)/shard_map/ppermute | solution.py:133
  107.0 1.3 copy-start.6
  108.3 2.5 %copy-start = (f32[576,640]{1,0:T(8,128)S(1)}, f32[576,640]{1,0:T(8,128)}, u32[]{:S(2)}) copy-start(f32[576,640]{1,0:T(8,128)} %fusion.18) | copy-start | bytes 4423684
  111.1 15.2 %collective-permute-start.8 = (f32[12,24,640]{2,1,0:T(8,128)S(1)}, f32[12,24,640]{2,1,0:T(8,128)}, u32[]{:S(2)}, u32[]{:S(2)}) collective-permute-start(f32[12,24,640]{2,1,0:T(8,128)S(1)} %slice_bitcast_fusion), channel_id=1, source_target_pairs={{0,24},{24,0},{1,25},{25,1},{2,26},{26,2},{3,27},{27,3},{4,28},{28... | collective-permute-start | bytes 2211848 | tf_op jit(solution)/shard_map/ppermute | solution.py:142
  119.5 27.6 %all-to-all-start.1 = ((bf16[8,64,640]{2,1,0:T(8,128)(2,1)}), bf16[8,64,640]{2,1,0:T(8,128)(2,1)S(1)}, u32[]{:S(2)}, u32[]{:S(2)}) async-start(bf16[8,64,640]{2,1,0:T(8,128)(2,1)} %bitcast.18), calls=%async_computation.2 | async-start | bytes 1310720 | tf_op jit(solution)/shard_map/all_to_all | solution.py:151
  127.6 1.0 copy-start.1
  127.6 1.1 copy-start.2
  130.0 18.1 %copy-start.4 = (bf16[24,4096]{1,0:T(8,128)(2,1)S(1)}, bf16[24,4096]{1,0:T(8,128)(2,1)}, u32[]{:S(2)}) copy-start(bf16[24,4096]{1,0:T(8,128)(2,1)} %reduce-scatter.2.cloned.1.call-done) | copy-start | bytes 589828
  131.0 17.0 %collective-permute-start.5 = (bf16[12,4096]{1,0:T(8,128)(2,1)S(1)}, bf16[12,4096]{1,0:T(8,128)(2,1)S(1)}, u32[]{:S(2)}, u32[]{:S(2)}) collective-permute-start(bf16[12,4096]{1,0:T(8,128)(2,1)S(1)} %constant_dynamic-slice_fusion), channel_id=1, source_target_pairs={{0,12},{12,0},{1,13},{13,1},{2,14},{14,2},{3,15},{15,3},{4,16},{16... | collective-permute-start | bytes 294920 | tf_op jit(solution)/shard_map/ppermute | solution.py:157
Sparse Core Ops, SparseCore 0:
  65.2 57.4 reduce-scatter.1

commit v8 on v7

--- a/solution.py
+++ b/solution.py
@@ -113,32 +113,41 @@
     mine_z = lax.all_gather(shard, "zh", axis=0, tiled=True)
     mine_z, hidden_z, hidden_far = tie((mine_z, hidden_z, hidden_far))
     other_z = lax.ppermute(mine_z, "zl", SWAP)
+    mine_far = lax.ppermute(mine_z, "yl", SWAP)
 
     partial = jnp.dot(hidden_z, down_weight, preferred_element_type=F32).astype(BF)
     out_z = lax.psum_scatter(partial, ("zh", "zl"), scatter_dimension=0, tiled=True)
-    _, other_z, hidden_near, hidden_far = tie((partial, other_z, hidden_near, hidden_far))
+    _, mine_far, other_z, hidden_near, hidden_far = tie(
+        (partial, mine_far, other_z, hidden_near, hidden_far)
+    )
     even = lax.axis_index("zl") == 0
-    ours, theirs = [rows_z.reshape(NZH, NC * both, -1) for rows_z in (mine_z, other_z)]
-    near = jnp.stack([jnp.where(even, ours, theirs), jnp.where(even, theirs, ours)], axis=1)
-    near = near.reshape(NC * tok, -1)
+
+    def by_place(ours, theirs):
+        ours, theirs = [rows_z.reshape(NZH, NC * both, -1) for rows_z in (ours, theirs)]
+        pair = [jnp.where(even, ours, theirs), jnp.where(even, theirs, ours)]
+        return jnp.stack(pair, axis=1).reshape(NC * tok, -1)
+
+    near = by_place(mine_z, other_z)
     hidden_all = jnp.concatenate([hidden_near.reshape(NC * tok, ff), hidden_far], axis=1)
 
     grad_acc = lax.dot_general(
         near, hidden_all, (((0,), (0,)), ((), ())), preferred_element_type=F32
     )
     term = (grad_acc / (NX * NYH * NC)).astype(BF).reshape(NX, NYH * half, NYL * ff)
-    term, near, gate_pre, up_pre, weight = tie((term, near, gate_pre, up_pre, down_weight))
+    term, near, other_z, mine_far, gate_pre, up_pre, weight = tie(
+        (term, near, other_z, mine_far, gate_pre, up_pre, down_weight)
+    )
     by_x = lax.all_to_all(term, "x", 0, 0)
 
-    far = lax.ppermute(near, "yl", SWAP)
+    far = by_place(mine_far, lax.ppermute(other_z, "yl", SWAP))
     weight_near, weight_far = weight_quarters(place, weight)
     back = lax.dot_general(near, weight_near, across, preferred_element_type=F32)
+    back = back + lax.dot_general(far, weight_far, across, preferred_element_type=F32)
+    back = back.reshape(NZ, NC, both, ff)
+    by_x, back = tie((by_x, back))
     sum_x = by_x.astype(F32).sum(0).astype(BF).reshape(NYH, half, NYL, ff)
     own, other = sum_x[:, :, 0], sum_x[:, :, 1]
     sum_x = jnp.stack([jnp.where(first, own, other), jnp.where(first, other, own)], axis=1)
-    sum_x, far, back = tie((sum_x, far, back))
-    back = back + lax.dot_general(far, weight_far, across, preferred_element_type=F32)
-    back = back.reshape(NZ, NC, both, ff)
     back_z = back[:, 0] + lax.ppermute(back[:, 1], "c", SWAP)
     back = back_z.reshape(NZ, NYL, rows, ff).transpose(1, 0, 2, 3).reshape(tok, ff)
     gate_wide = gate_pre.astype(F32)

time: 156 us -> 160 us (1.026)
  local copies, waits for them, and re-layouts: 5.55 us -> 9.61 us
  waiting for transfers between devices: 30.6 us -> 27.7 us
  starting transfers between devices: 53.6 us -> 55.8 us
    ppermute x1, waiting for transfers between devices: 4.01 us -> 0.84 us  [per_device(): other_z = lax.ppermute(mine_z, 'zl', SWAP)]
    ppermute x1 -> x2, waiting for transfers between devices: 0.01 us -> 2.47 us  [the longest x1 2.47 us: per_device(): mine_far = lax.ppermute(mine_z, 'yl', SWAP)]
    unnamed x17 -> x21, local copies, waits for them, and re-layouts: 2.97 us -> 5.04 us
    squeeze x1, local copies, waits for them, and re-layouts: 0.05 us -> 2.07 us  [per_device(): back_z = back[:, 0] + lax.ppermute(back[:, 1], 'c', SWAP)]
    all_to_all x1, waiting for transfers between devices: 12.2 us -> 10.2 us  [per_device(): by_x = lax.all_to_all(term, 'x', 0, 0)]
    ppermute x1 -> x2, starting transfers between devices: 5.22 us -> 6.35 us  [the longest x1 3.19 us: per_device(): far = by_place(mine_far, lax.ppermute(other_z, 'yl', SWAP))]
  transfers between devices with their start and end apart: 12 -> 13, of which waited for: 5 -> 6; matrix products, arithmetic and copies ran while one was open for 17% -> 18% of each run, Pallas kernels for 4% -> 4%
where the time goes in v8:
time: 160 us; the launch traced here: 159 us
  starting transfers between devices  55.8 us (35%)
  waiting for transfers between devices  27.7 us (17%)
  blocking collectives  20.2 us (13%)
  matrix products  14.8 us (9%)
  between operations  14.4 us (9%)
  local copies, waits for them, and re-layouts  9.61 us (6%)
  other arithmetic  8.77 us (5%)
  Pallas kernels  7.53 us (5%)
    all_gather x1, blocking collectives, per_device(): mine_z = lax.all_gather(shard, 'zh', axis=0, tiled=True)  20.2 us
    all_to_all x1, waiting for transfers between devices, per_device(): lax.all_to_all(sum_x.reshape(NYH * NYL, half, ff), ('yh', 'yl'), 0, 0)  12.5 us
    ppermute x1, starting transfers between devices, per_device(): from_core = lax.ppermute(to_core, 'c', SWAP)  12.4 us
    all_to_all x1, waiting for transfers between devices, per_device(): by_x = lax.all_to_all(term, 'x', 0, 0)  10.2 us
    ppermute x1, starting transfers between devices, per_device(): back_z = back[:, 0] + lax.ppermute(back[:, 1], 'c', SWAP)  8.14 us
    all_to_all x1, starting transfers between devices, per_device(): lax.all_to_all(sum_x.reshape(NYH * NYL, half, ff), ('yh', 'yl'), 0, 0)  6.83 us
    dot_general x1, matrix products, per_device(): jnp.dot(hidden_z, down_weight, preferred_element_type=F32).astype(BF)  5.92 us
    pallas_call x1, Pallas kernels, weight_quarters(): pl.pallas_call(weight_kernel, out_shape=[jax.ShapeDtypeStruct((ff, feat /...  5.86 us
  transfers between devices with their start and end apart: 13, of which 6 were waited for; matrix products, arithmetic and copies ran while one was open for 18% of the time, Pallas kernels for 4%

profile of v8, /device:TPU:1, one launch (start us, length us, event | category | flops | bytes accessed | tf_op | source)
XLA Modules:
  0.0 158.8 jit_solution(3952295334704322589)
XLA Ops:
  7.2 1.7 %split_columns.1 = (bf16[12,1024]{1,0:T(8,128)(2,1)}, bf16[12,1024]{1,0:T(8,128)(2,1)}, bf16[12,1024]{1,0:T(8,128)(2,1)}, bf16[12,1024]{1,0:T(8,128)(2,1)}) custom-call(s32[1]{0:T(128)} %bitcast.place_ref, bf16[12,4096]{1,0:T(8,128)(2,1)} %cot_ref.1), custom_call_target="tpu_custom_call" | custom-call | tf_op jit(solution)/shard_map/split_columns/pallas_call | solution.py:41
  8.9 12.4 %collective-permute-start = (bf16[12,1024]{1,0:T(8,128)(2,1)}, bf16[12,1024]{1,0:T(8,128)(2,1)S(1)}, u32[]{:S(2)}, u32[]{:S(2)}) collective-permute-start(bf16[12,1024]{1,0:T(8,128)(2,1)} %get-tuple-element.34), channel_id=1, source_target_pairs={{0,24},{24,0},{1,25},{25,1},{2,26},{26,2},{3,27},{27,3},{4,28},{28... | collective-permute-start | bytes 73736 | tf_op jit(solution)/shard_map/ppermute | solution.py:88
  21.3 1.9 %collective-permute-start.1 = (bf16[12,1024]{1,0:T(8,128)(2,1)}, bf16[12,1024]{1,0:T(8,128)(2,1)S(1)}, u32[]{:S(2)}, u32[]{:S(2)}) collective-permute-start(bf16[12,1024]{1,0:T(8,128)(2,1)} %get-tuple-element.35), channel_id=1, source_target_pairs={{0,12},{12,0},{1,13},{13,1},{2,14},{14,2},{3,15},{15,3},{4,16},{16... | collective-permute-start | bytes 73736 | tf_op jit(solution)/shard_map/ppermute | solution.py:89
  23.2 3.5 %collective-permute-start.2 = (bf16[12,1024]{1,0:T(8,128)(2,1)}, bf16[12,1024]{1,0:T(8,128)(2,1)S(1)}, u32[]{:S(2)}, u32[]{:S(2)}) collective-permute-start(bf16[12,1024]{1,0:T(8,128)(2,1)} %get-tuple-element.36), channel_id=1, source_target_pairs={{0,36},{12,24},{24,12},{36,0},{1,37},{13,25},{25,13},{37,1},{2,38}... | collective-permute-start | bytes 73736 | tf_op jit(solution)/shard_map/ppermute | solution.py:90
  26.8 1.3 fusion.16
  28.7 2.1 %collective-permute-start.3 = (bf16[288,640]{1,0:T(8,128)(2,1)S(1)}, bf16[288,640]{1,0:T(8,128)(2,1)S(1)}, u32[]{:S(2)}, u32[]{:S(2)}) collective-permute-start(bf16[288,640]{1,0:T(8,128)(2,1)S(1)} %reshape.170), channel_id=1, source_target_pairs={{0,24},{24,0},{1,25},{25,1},{2,26},{26,2},{3,27},{27,3},{4,28},{28... | collective-permute-start | bytes 1105928 | tf_op jit(solution)/shard_map/ppermute | solution.py:99
  30.9 1.4 collective-permute-done.3
  32.4 3.4 %collective-permute-start.4 = (bf16[576,640]{1,0:T(8,128)(2,1)S(1)}, bf16[576,640]{1,0:T(8,128)(2,1)S(1)}, u32[]{:S(2)}, u32[]{:S(2)}) collective-permute-start(bf16[576,640]{1,0:T(8,128)(2,1)S(1)} %bitcast.67), channel_id=1, source_target_pairs={{0,12},{12,0},{1,13},{13,1},{2,14},{14,2},{3,15},{15,3},{4,16},{16... | collective-permute-start | bytes 2211848 | tf_op jit(solution)/shard_map/ppermute | solution.py:112
  35.7 20.2 %all_gather.3 = bf16[288,1024]{1,0:T(8,128)(2,1)S(1)} all-gather(bf16[48,1024]{1,0:T(8,128)(2,1)S(1)} %pad_maximum_fusion.4), channel_id=1, replica_groups=mesh['x'=4,'yh'=4,'c'=2,'yl'=2,'zh'=6,'zl'=2] {'zh'}, dimensions={0}, use_global_device_ids=true | all-gather | bytes 688128 | tf_op jit(solution)/shard_map/all_gather | solution.py:113
  56.8 3.1 %collective-permute-start.7 = (bf16[288,1024]{1,0:T(8,128)(2,1)S(1)}, bf16[288,1024]{1,0:T(8,128)(2,1)S(1)}, u32[]{:S(2)}, u32[]{:S(2)}) collective-permute-start(bf16[288,1024]{1,0:T(8,128)(2,1)S(1)} %all_gather.3), channel_id=1, source_target_pairs={{0,1},{1,0},{2,3},{3,2},{4,5},{5,4},{6,7},{7,6},{8,9},{9,8},{10,11... | collective-permute-start | bytes 1769480 | tf_op jit(solution)/shard_map/ppermute | solution.py:115
  60.0 3.2 %collective-permute-start.6 = (bf16[288,1024]{1,0:T(8,128)(2,1)S(1)}, bf16[288,1024]{1,0:T(8,128)(2,1)S(1)}, u32[]{:S(2)}, u32[]{:S(2)}) collective-permute-start(bf16[288,1024]{1,0:T(8,128)(2,1)S(1)} %all_gather.3), channel_id=1, source_target_pairs={{0,12},{12,0},{1,13},{13,1},{2,14},{14,2},{3,15},{15,3},{4,16},{16... | collective-permute-start | bytes 1769480 | tf_op jit(solution)/shard_map/ppermute | solution.py:116
  63.1 5.9 %convolution_convert_fusion = bf16[288,4096]{1,0:T(8,128)(2,1)} fusion(bf16[288,640]{1,0:T(8,128)(2,1)S(1)} %reshape.170, bf16[640,4096]{1,0:T(8,128)(2,1)} %weight_ref), kind=kOutput, calls=%fused_computation | convolution fusion | flops 1511129088 | bytes 7970816 | tf_op jit(solution)/shard_map/dot_general | solution.py:118
  69.9 2.5 %collective-permute-done.6 = bf16[288,1024]{1,0:T(8,128)(2,1)S(1)} collective-permute-done((bf16[288,1024]{1,0:T(8,128)(2,1)S(1)}, bf16[288,1024]{1,0:T(8,128)(2,1)S(1)}, u32[]{:S(2)}, u32[]{:S(2)}) %collective-permute-start.6) | collective-permute-done | bytes 589856 | tf_op jit(solution)/shard_map/ppermute | solution.py:116
  72.6 1.1 copy-done.8
  73.8 3.8 %multiply_convert_fusion = bf16[1024,1280]{1,0:T(8,128)(2,1)} fusion(bf16[576,1024]{1,0:T(8,128)(2,1)S(1)} %bitcast.64, bf16[576,640]{1,0:T(8,128)(2,1)S(1)} %copy-done.8, bf16[576,640]{1,0:T(8,128)(2,1)S(1)} %bitcast.68), kind=kOutput, calls=%fused_computation.1 | convolution fusion | flops 1515520000 | bytes 5275648 | tf_op jit(solution)/shard_map/dot_general | solution.py:133
  77.6 4.5 %all-to-all-start = ((bf16[4,256,1280]{2,1,0:T(8,128)(2,1)}), bf16[4,256,1280]{2,1,0:T(8,128)(2,1)S(1)}, u32[]{:S(2)}, u32[]{:S(2)}) async-start(bf16[4,256,1280]{2,1,0:T(8,128)(2,1)} %bitcast.52), calls=%async_computation.1 | async-start | bytes 5242880 | tf_op jit(solution)/shard_map/all_to_all | solution.py:140
  82.1 3.2 %collective-permute-start.8 = (bf16[288,1024]{1,0:T(8,128)(2,1)}, bf16[288,1024]{1,0:T(8,128)(2,1)}, u32[]{:S(2)}, u32[]{:S(2)}) collective-permute-start(bf16[288,1024]{1,0:T(8,128)(2,1)} %copy-done.3), channel_id=1, source_target_pairs={{0,12},{12,0},{1,13},{13,1},{2,14},{14,2},{3,15},{15,3},{4,16},{16... | collective-permute-start | bytes 1769480 | tf_op jit(solution)/shard_map/ppermute | solution.py:142
  85.3 5.9 %weight_quarters.1 = (bf16[640,1024]{1,0:T(8,128)(2,1)}, bf16[640,1024]{1,0:T(8,128)(2,1)}) custom-call(s32[1]{0:T(128)} %bitcast.place_ref, bf16[640,4096]{1,0:T(8,128)(2,1)} %weight_ref), custom_call_target="tpu_custom_call" | custom-call | tf_op jit(solution)/shard_map/weight_quarters/pallas_call | solution.py:63
  91.2 2.8 %fusion.18 = f32[576,640]{1,0:T(8,128)S(1)} fusion(bf16[576,1024]{1,0:T(8,128)(2,1)} %bitcast.65, bf16[640,1024]{1,0:T(8,128)(2,1)} %get-tuple-element.54), kind=kOutput, calls=%fused_computation.48 | convolution fusion | flops 754974720 | bytes 3964928 | tf_op jit(solution)/shard_map/dot_general | solution.py:144
  94.0 1.2 broadcast_select_fusion.3
  95.3 1.2 copy-done.6
  96.5 2.3 %convolution_add_fusion = f32[576,640]{1,0:T(8,128)} fusion(f32[576,640]{1,0:T(8,128)S(1)} %fusion.18, bf16[576,1024]{1,0:T(8,128)(2,1)S(1)} %bitcast.66, bf16[640,1024]{1,0:T(8,128)(2,1)S(1)} %copy-done.6), kind=kOutput, calls=%fused_computation.5 | convolution fusion | flops 755343360 | bytes 5439488 | tf_op jit(solution)/shard_map/dot_general | solution.py:145
  98.8 10.2 %all-to-all-done = bf16[4,256,1280]{2,1,0:T(8,128)(2,1)S(1)} async-done(((bf16[4,256,1280]{2,1,0:T(8,128)(2,1)}), bf16[4,256,1280]{2,1,0:T(8,128)(2,1)S(1)}, u32[]{:S(2)}, u32[]{:S(2)}) %all-to-all-start) | async-done | bytes 2621472 | tf_op jit(solution)/shard_map/all_to_all | solution.py:140
  108.9 2.1 %slice_bitcast_fusion = f32[12,24,640]{2,1,0:T(8,128)} fusion(f32[12,2,24,640]{3,2,1,0:T(8,128)} %bitcast.59), kind=kLoop, calls=%fused_computation.27 | loop fusion | bytes 1474560 | tf_op jit(solution)/shard_map/squeeze | solution.py:151
  111.0 8.1 %collective-permute-start.9 = (f32[12,24,640]{2,1,0:T(8,128)}, f32[12,24,640]{2,1,0:T(8,128)}, u32[]{:S(2)}, u32[]{:S(2)}) collective-permute-start(f32[12,24,640]{2,1,0:T(8,128)} %slice_bitcast_fusion), channel_id=1, source_target_pairs={{0,24},{24,0},{1,25},{25,1},{2,26},{26,2},{3,27},{27,3},{4,28},{28... | collective-permute-start | bytes 2211848 | tf_op jit(solution)/shard_map/ppermute | solution.py:151
  120.1 1.5 broadcast_select_fusion.1
  122.7 6.8 %all-to-all-start.1 = ((bf16[8,64,640]{2,1,0:T(8,128)(2,1)}), bf16[8,64,640]{2,1,0:T(8,128)(2,1)S(1)}, u32[]{:S(2)}, u32[]{:S(2)}) async-start(bf16[8,64,640]{2,1,0:T(8,128)(2,1)} %bitcast.23), calls=%async_computation.2 | async-start | bytes 1310720 | tf_op jit(solution)/shard_map/all_to_all | solution.py:160
  129.5 1.4 fusion.15
  132.2 1.2 fusion.14
  133.4 1.0 constant_dynamic-slice_fusion
  134.4 3.4 %collective-permute-start.5 = (bf16[12,4096]{1,0:T(8,128)(2,1)S(1)}, bf16[12,4096]{1,0:T(8,128)(2,1)S(1)}, u32[]{:S(2)}, u32[]{:S(2)}) collective-permute-start(bf16[12,4096]{1,0:T(8,128)(2,1)S(1)} %constant_dynamic-slice_fusion), channel_id=1, source_target_pairs={{0,12},{12,0},{1,13},{13,1},{2,14},{14,2},{3,15},{15,3},{4,16},{16... | collective-permute-start | bytes 294920 | tf_op jit(solution)/shard_map/ppermute | solution.py:166
  137.8 12.5 %all-to-all-done.1 = bf16[8,64,640]{2,1,0:T(8,128)(2,1)S(1)} async-done(((bf16[8,64,640]{2,1,0:T(8,128)(2,1)}), bf16[8,64,640]{2,1,0:T(8,128)(2,1)S(1)}, u32[]{:S(2)}, u32[]{:S(2)}) %all-to-all-start.1) | async-done | bytes 655392 | tf_op jit(solution)/shard_map/all_to_all | solution.py:160
  (48 shorter events, 7.5 us)
Async XLA Ops:
  7.2 126.2 %reduce-scatter.2.cloned.1.call-start = ((), (), s32[]{:S(2)}) async-start(), calls=%async_computation.3 | async-start | bytes 2555904 | tf_op jit(solution)/shard_map/reduce_scatter | solution.py:119
  8.9 19.5 %collective-permute-start = (bf16[12,1024]{1,0:T(8,128)(2,1)}, bf16[12,1024]{1,0:T(8,128)(2,1)S(1)}, u32[]{:S(2)}, u32[]{:S(2)}) collective-permute-start(bf16[12,1024]{1,0:T(8,128)(2,1)} %get-tuple-element.34), channel_id=1, source_target_pairs={{0,24},{24,0},{1,25},{25,1},{2,26},{26,2},{3,27},{27,3},{4,28},{28... | collective-permute-start | bytes 73736 | tf_op jit(solution)/shard_map/ppermute | solution.py:88
  21.3 7.1 %collective-permute-start.1 = (bf16[12,1024]{1,0:T(8,128)(2,1)}, bf16[12,1024]{1,0:T(8,128)(2,1)S(1)}, u32[]{:S(2)}, u32[]{:S(2)}) collective-permute-start(bf16[12,1024]{1,0:T(8,128)(2,1)} %get-tuple-element.35), channel_id=1, source_target_pairs={{0,12},{12,0},{1,13},{13,1},{2,14},{14,2},{3,15},{15,3},{4,16},{16... | collective-permute-start | bytes 73736 | tf_op jit(solution)/shard_map/ppermute | solution.py:89
  23.2 5.4 %collective-permute-start.2 = (bf16[12,1024]{1,0:T(8,128)(2,1)}, bf16[12,1024]{1,0:T(8,128)(2,1)S(1)}, u32[]{:S(2)}, u32[]{:S(2)}) collective-permute-start(bf16[12,1024]{1,0:T(8,128)(2,1)} %get-tuple-element.36), channel_id=1, source_target_pairs={{0,36},{12,24},{24,12},{36,0},{1,37},{13,25},{25,13},{37,1},{2,38}... | collective-permute-start | bytes 73736 | tf_op jit(solution)/shard_map/ppermute | solution.py:90
  28.1 2.7 %copy-start.5 = (bf16[12,1024]{1,0:T(8,128)(2,1)S(1)}, bf16[12,1024]{1,0:T(8,128)(2,1)}, u32[]{:S(2)}) copy-start(bf16[12,1024]{1,0:T(8,128)(2,1)} %get-tuple-element.33) | copy-start | bytes 73732
  28.7 3.6 %collective-permute-start.3 = (bf16[288,640]{1,0:T(8,128)(2,1)S(1)}, bf16[288,640]{1,0:T(8,128)(2,1)S(1)}, u32[]{:S(2)}, u32[]{:S(2)}) collective-permute-start(bf16[288,640]{1,0:T(8,128)(2,1)S(1)} %reshape.170), channel_id=1, source_target_pairs={{0,24},{24,0},{1,25},{25,1},{2,26},{26,2},{3,27},{27,3},{4,28},{28... | collective-permute-start | bytes 1105928 | tf_op jit(solution)/shard_map/ppermute | solution.py:99
  32.4 23.6 %collective-permute-start.4 = (bf16[576,640]{1,0:T(8,128)(2,1)S(1)}, bf16[576,640]{1,0:T(8,128)(2,1)S(1)}, u32[]{:S(2)}, u32[]{:S(2)}) collective-permute-start(bf16[576,640]{1,0:T(8,128)(2,1)S(1)} %bitcast.67), channel_id=1, source_target_pairs={{0,12},{12,0},{1,13},{13,1},{2,14},{14,2},{3,15},{15,3},{4,16},{16... | collective-permute-start | bytes 2211848 | tf_op jit(solution)/shard_map/ppermute | solution.py:112
  56.0 0.9 copy-start.7
  56.8 13.1 %collective-permute-start.7 = (bf16[288,1024]{1,0:T(8,128)(2,1)S(1)}, bf16[288,1024]{1,0:T(8,128)(2,1)S(1)}, u32[]{:S(2)}, u32[]{:S(2)}) collective-permute-start(bf16[288,1024]{1,0:T(8,128)(2,1)S(1)} %all_gather.3), channel_id=1, source_target_pairs={{0,1},{1,0},{2,3},{3,2},{4,5},{5,4},{6,7},{7,6},{8,9},{9,8},{10,11... | collective-permute-start | bytes 1769480 | tf_op jit(solution)/shard_map/ppermute | solution.py:115
  60.0 12.4 %collective-permute-start.6 = (bf16[288,1024]{1,0:T(8,128)(2,1)S(1)}, bf16[288,1024]{1,0:T(8,128)(2,1)S(1)}, u32[]{:S(2)}, u32[]{:S(2)}) collective-permute-start(bf16[288,1024]{1,0:T(8,128)(2,1)S(1)} %all_gather.3), channel_id=1, source_target_pairs={{0,12},{12,0},{1,13},{13,1},{2,14},{14,2},{3,15},{15,3},{4,16},{16... | collective-permute-start | bytes 1769480 | tf_op jit(solution)/shard_map/ppermute | solution.py:116
  69.9 2.7 %copy-start.3 = (bf16[288,1024]{1,0:T(8,128)(2,1)}, bf16[288,1024]{1,0:T(8,128)(2,1)S(1)}, u32[]{:S(2)}) copy-start(bf16[288,1024]{1,0:T(8,128)(2,1)S(1)} %collective-permute-done.7) | copy-start | bytes 1769476
  72.5 1.3 copy-start.8
  72.6 4.9 %copy-start.2 = (bf16[6,2,48,1024]{3,2,1,0:T(8,128)(2,1)}, bf16[6,2,48,1024]{3,2,1,0:T(8,128)(2,1)S(1)}, u32[]{:S(2)}) copy-start(bf16[6,2,48,1024]{3,2,1,0:T(8,128)(2,1)S(1)} %pad_maximum_fusion) | copy-start | bytes 3538948
  77.6 31.4 %all-to-all-start = ((bf16[4,256,1280]{2,1,0:T(8,128)(2,1)}), bf16[4,256,1280]{2,1,0:T(8,128)(2,1)S(1)}, u32[]{:S(2)}, u32[]{:S(2)}) async-start(bf16[4,256,1280]{2,1,0:T(8,128)(2,1)} %bitcast.52), calls=%async_computation.1 | async-start | bytes 5242880 | tf_op jit(solution)/shard_map/all_to_all | solution.py:140
  82.1 11.9 %collective-permute-start.8 = (bf16[288,1024]{1,0:T(8,128)(2,1)}, bf16[288,1024]{1,0:T(8,128)(2,1)}, u32[]{:S(2)}, u32[]{:S(2)}) collective-permute-start(bf16[288,1024]{1,0:T(8,128)(2,1)} %copy-done.3), channel_id=1, source_target_pairs={{0,12},{12,0},{1,13},{13,1},{2,14},{14,2},{3,15},{15,3},{4,16},{16... | collective-permute-start | bytes 1769480 | tf_op jit(solution)/shard_map/ppermute | solution.py:142
  95.1 1.3 copy-start.6
  111.0 18.5 %collective-permute-start.9 = (f32[12,24,640]{2,1,0:T(8,128)}, f32[12,24,640]{2,1,0:T(8,128)}, u32[]{:S(2)}, u32[]{:S(2)}) collective-permute-start(f32[12,24,640]{2,1,0:T(8,128)} %slice_bitcast_fusion), channel_id=1, source_target_pairs={{0,24},{24,0},{1,25},{25,1},{2,26},{26,2},{3,27},{27,3},{4,28},{28... | collective-permute-start | bytes 2211848 | tf_op jit(solution)/shard_map/ppermute | solution.py:151
  122.7 27.6 %all-to-all-start.1 = ((bf16[8,64,640]{2,1,0:T(8,128)(2,1)}), bf16[8,64,640]{2,1,0:T(8,128)(2,1)S(1)}, u32[]{:S(2)}, u32[]{:S(2)}) async-start(bf16[8,64,640]{2,1,0:T(8,128)(2,1)} %bitcast.23), calls=%async_computation.2 | async-start | bytes 1310720 | tf_op jit(solution)/shard_map/all_to_all | solution.py:160
  131.1 1.0 copy-start
  131.1 1.1 copy-start.1
  133.4 17.8 %copy-start.4 = (bf16[24,4096]{1,0:T(8,128)(2,1)S(1)}, bf16[24,4096]{1,0:T(8,128)(2,1)}, u32[]{:S(2)}) copy-start(bf16[24,4096]{1,0:T(8,128)(2,1)} %reduce-scatter.2.cloned.1.call-done) | copy-start | bytes 589828
  134.4 16.8 %collective-permute-start.5 = (bf16[12,4096]{1,0:T(8,128)(2,1)S(1)}, bf16[12,4096]{1,0:T(8,128)(2,1)S(1)}, u32[]{:S(2)}, u32[]{:S(2)}) collective-permute-start(bf16[12,4096]{1,0:T(8,128)(2,1)S(1)} %constant_dynamic-slice_fusion), channel_id=1, source_target_pairs={{0,12},{12,0},{1,13},{13,1},{2,14},{14,2},{3,15},{15,3},{4,16},{16... | collective-permute-start | bytes 294920 | tf_op jit(solution)/shard_map/ppermute | solution.py:166
Sparse Core Ops, SparseCore 0:
  69.2 56.7 reduce-scatter.1

commit v9 on v7

--- a/solution.py
+++ b/solution.py
@@ -116,12 +116,16 @@
 
     partial = jnp.dot(hidden_z, down_weight, preferred_element_type=F32).astype(BF)
     out_z = lax.psum_scatter(partial, ("zh", "zl"), scatter_dimension=0, tiled=True)
-    _, other_z, hidden_near, hidden_far = tie((partial, other_z, hidden_near, hidden_far))
+    hidden_near = hidden_near.reshape(NC * tok, ff)
+    hidden_all = jnp.concatenate(
+        [jnp.where(first, hidden_near, hidden_far), jnp.where(first, hidden_far, hidden_near)],
+        axis=1,
+    )
+    _, other_z, hidden_all = tie((partial, other_z, hidden_all))
     even = lax.axis_index("zl") == 0
     ours, theirs = [rows_z.reshape(NZH, NC * both, -1) for rows_z in (mine_z, other_z)]
     near = jnp.stack([jnp.where(even, ours, theirs), jnp.where(even, theirs, ours)], axis=1)
     near = near.reshape(NC * tok, -1)
-    hidden_all = jnp.concatenate([hidden_near.reshape(NC * tok, ff), hidden_far], axis=1)
 
     grad_acc = lax.dot_general(
         near, hidden_all, (((0,), (0,)), ((), ())), preferred_element_type=F32
@@ -134,8 +138,7 @@
     weight_near, weight_far = weight_quarters(place, weight)
     back = lax.dot_general(near, weight_near, across, preferred_element_type=F32)
     sum_x = by_x.astype(F32).sum(0).astype(BF).reshape(NYH, half, NYL, ff)
-    own, other = sum_x[:, :, 0], sum_x[:, :, 1]
-    sum_x = jnp.stack([jnp.where(first, own, other), jnp.where(first, other, own)], axis=1)
+    sum_x = sum_x.transpose(0, 2, 1, 3).reshape(NYH * NYL, half, ff)
     sum_x, far, back = tie((sum_x, far, back))
     back = back + lax.dot_general(far, weight_far, across, preferred_element_type=F32)
     back = back.reshape(NZ, NC, both, ff)
@@ -148,7 +151,7 @@
     gate_grad = (back * up_wide * sig * (1.0 + gate_wide * (1.0 - sig))).astype(BF)
     up_grad = (back * act).astype(BF)
 
-    by_y = lax.all_to_all(sum_x.reshape(NYH * NYL, half, ff), ("yh", "yl"), 0, 0)
+    by_y = lax.all_to_all(sum_x, ("yh", "yl"), 0, 0)
     by_y = by_y.reshape(NYH, NYL * half, ff)
     weight_grad = by_y.astype(F32).sum(0).astype(BF).T
 

time: 156 us -> 154 us (0.987)
  transfers between devices with their start and end apart: 12 -> 12, of which waited for: 5 -> 5; matrix products, arithmetic and copies ran while one was open for 17% -> 16% of each run, Pallas kernels for 4% -> 4%
where the time goes in v9:
time: 154 us; the launch traced here: 153 us
  starting transfers between devices  53.6 us (35%)
  waiting for transfers between devices  30.3 us (20%)
  blocking collectives  20.2 us (13%)
  matrix products  16.2 us (11%)
  between operations  14.3 us (9%)
  Pallas kernels  7.61 us (5%)
  other arithmetic  6.16 us (4%)
  local copies, waits for them, and re-layouts  4.81 us (3%)
    all_gather x1, blocking collectives, per_device(): mine_z = lax.all_gather(shard, 'zh', axis=0, tiled=True)  20.2 us
    all_to_all x1, waiting for transfers between devices, per_device(): by_y = lax.all_to_all(sum_x, ('yh', 'yl'), 0, 0)  12.7 us
    ppermute x1, starting transfers between devices, per_device(): from_core = lax.ppermute(to_core, 'c', SWAP)  12.4 us
    all_to_all x1, waiting for transfers between devices, per_device(): by_x = lax.all_to_all(term, 'x', 0, 0)  12.2 us
    ppermute x1, starting transfers between devices, per_device(): back_z = back[:, 0] + lax.ppermute(back[:, 1], 'c', SWAP)  7.49 us
    all_to_all x1, starting transfers between devices, per_device(): by_y = lax.all_to_all(sum_x, ('yh', 'yl'), 0, 0)  6.83 us
    pallas_call x1, Pallas kernels, weight_quarters(): pl.pallas_call(weight_kernel, out_shape=[jax.ShapeDtypeStruct((ff, feat /...  5.95 us
    dot_general x1, matrix products, per_device(): jnp.dot(hidden_z, down_weight, preferred_element_type=F32).astype(BF)  5.92 us
  transfers between devices with their start and end apart: 12, of which 5 were waited for; matrix products, arithmetic and copies ran while one was open for 16% of the time, Pallas kernels for 4%

profile of v9, /device:TPU:1, one launch (start us, length us, event | category | flops | bytes accessed | tf_op | source)
XLA Modules:
  0.0 153.2 jit_solution(15124309085183547767)
XLA Ops:
  7.2 1.7 %split_columns.1 = (bf16[12,1024]{1,0:T(8,128)(2,1)}, bf16[12,1024]{1,0:T(8,128)(2,1)}, bf16[12,1024]{1,0:T(8,128)(2,1)}, bf16[12,1024]{1,0:T(8,128)(2,1)}) custom-call(s32[1]{0:T(128)} %bitcast.place_ref, bf16[12,4096]{1,0:T(8,128)(2,1)} %cot_ref.1), custom_call_target="tpu_custom_call" | custom-call | tf_op jit(solution)/shard_map/split_columns/pallas_call | solution.py:41
  8.9 12.4 %collective-permute-start = (bf16[12,1024]{1,0:T(8,128)(2,1)}, bf16[12,1024]{1,0:T(8,128)(2,1)S(1)}, u32[]{:S(2)}, u32[]{:S(2)}) collective-permute-start(bf16[12,1024]{1,0:T(8,128)(2,1)} %get-tuple-element.31), channel_id=1, source_target_pairs={{0,24},{24,0},{1,25},{25,1},{2,26},{26,2},{3,27},{27,3},{4,28},{28... | collective-permute-start | bytes 73736 | tf_op jit(solution)/shard_map/ppermute | solution.py:88
  21.3 1.9 %collective-permute-start.1 = (bf16[12,1024]{1,0:T(8,128)(2,1)}, bf16[12,1024]{1,0:T(8,128)(2,1)S(1)}, u32[]{:S(2)}, u32[]{:S(2)}) collective-permute-start(bf16[12,1024]{1,0:T(8,128)(2,1)} %get-tuple-element.32), channel_id=1, source_target_pairs={{0,12},{12,0},{1,13},{13,1},{2,14},{14,2},{3,15},{15,3},{4,16},{16... | collective-permute-start | bytes 73736 | tf_op jit(solution)/shard_map/ppermute | solution.py:89
  23.2 3.5 %collective-permute-start.2 = (bf16[12,1024]{1,0:T(8,128)(2,1)}, bf16[12,1024]{1,0:T(8,128)(2,1)S(1)}, u32[]{:S(2)}, u32[]{:S(2)}) collective-permute-start(bf16[12,1024]{1,0:T(8,128)(2,1)} %get-tuple-element.33), channel_id=1, source_target_pairs={{0,36},{12,24},{24,12},{36,0},{1,37},{13,25},{25,13},{37,1},{2,38}... | collective-permute-start | bytes 73736 | tf_op jit(solution)/shard_map/ppermute | solution.py:90
  26.8 1.3 fusion.13
  28.7 2.1 %collective-permute-start.3 = (bf16[288,640]{1,0:T(8,128)(2,1)S(1)}, bf16[288,640]{1,0:T(8,128)(2,1)S(1)}, u32[]{:S(2)}, u32[]{:S(2)}) collective-permute-start(bf16[288,640]{1,0:T(8,128)(2,1)S(1)} %reshape.87), channel_id=1, source_target_pairs={{0,24},{24,0},{1,25},{25,1},{2,26},{26,2},{3,27},{27,3},{4,28},{28... | collective-permute-start | bytes 1105928 | tf_op jit(solution)/shard_map/ppermute | solution.py:99
  30.9 1.4 collective-permute-done.3
  32.4 3.4 %collective-permute-start.4 = (bf16[576,640]{1,0:T(8,128)(2,1)S(1)}, bf16[576,640]{1,0:T(8,128)(2,1)S(1)}, u32[]{:S(2)}, u32[]{:S(2)}) collective-permute-start(bf16[576,640]{1,0:T(8,128)(2,1)S(1)} %bitcast.48), channel_id=1, source_target_pairs={{0,12},{12,0},{1,13},{13,1},{2,14},{14,2},{3,15},{15,3},{4,16},{16... | collective-permute-start | bytes 2211848 | tf_op jit(solution)/shard_map/ppermute | solution.py:112
  35.7 20.2 %all_gather.3 = bf16[288,1024]{1,0:T(8,128)(2,1)S(1)} all-gather(bf16[48,1024]{1,0:T(8,128)(2,1)S(1)} %pad_maximum_fusion.3), channel_id=1, replica_groups=mesh['x'=4,'yh'=4,'c'=2,'yl'=2,'zh'=6,'zl'=2] {'zh'}, dimensions={0}, use_global_device_ids=true | all-gather | bytes 688128 | tf_op jit(solution)/shard_map/all_gather | solution.py:113
  56.0 3.1 %collective-permute-start.6 = (bf16[288,1024]{1,0:T(8,128)(2,1)S(1)}, bf16[288,1024]{1,0:T(8,128)(2,1)S(1)}, u32[]{:S(2)}, u32[]{:S(2)}) collective-permute-start(bf16[288,1024]{1,0:T(8,128)(2,1)S(1)} %all_gather.3), channel_id=1, source_target_pairs={{0,1},{1,0},{2,3},{3,2},{4,5},{5,4},{6,7},{7,6},{8,9},{9,8},{10,11... | collective-permute-start | bytes 1769480 | tf_op jit(solution)/shard_map/ppermute | solution.py:115
  59.1 5.9 %convolution_convert_fusion = bf16[288,4096]{1,0:T(8,128)(2,1)} fusion(bf16[288,640]{1,0:T(8,128)(2,1)S(1)} %reshape.87, bf16[640,4096]{1,0:T(8,128)(2,1)} %weight_ref), kind=kOutput, calls=%fused_computation | convolution fusion | flops 1511129088 | bytes 7970816 | tf_op jit(solution)/shard_map/dot_general | solution.py:117
  65.4 3.7 %collective-permute-done.6 = bf16[288,1024]{1,0:T(8,128)(2,1)S(1)} collective-permute-done((bf16[288,1024]{1,0:T(8,128)(2,1)S(1)}, bf16[288,1024]{1,0:T(8,128)(2,1)S(1)}, u32[]{:S(2)}, u32[]{:S(2)}) %collective-permute-start.6) | collective-permute-done | bytes 589856 | tf_op jit(solution)/shard_map/ppermute | solution.py:115
  69.3 3.8 %multiply_convert_fusion = bf16[1024,1280]{1,0:T(8,128)(2,1)} fusion(bf16[576,1024]{1,0:T(8,128)(2,1)S(1)} %bitcast.56, bf16[576,1280]{1,0:T(8,128)(2,1)S(1)} %pad_maximum_fusion), kind=kOutput, calls=%fused_computation.1 | convolution fusion | flops 1512570880 | bytes 5275648 | tf_op jit(solution)/shard_map/dot_general | solution.py:130
  73.1 4.1 %all-to-all-start = ((bf16[4,256,1280]{2,1,0:T(8,128)(2,1)}), bf16[4,256,1280]{2,1,0:T(8,128)(2,1)S(1)}, u32[]{:S(2)}, u32[]{:S(2)}) async-start(bf16[4,256,1280]{2,1,0:T(8,128)(2,1)} %bitcast.49), calls=%async_computation.1 | async-start | bytes 5242880 | tf_op jit(solution)/shard_map/all_to_all | solution.py:135
  77.2 5.2 %collective-permute-start.7 = (bf16[576,1024]{1,0:T(8,128)(2,1)}, bf16[576,1024]{1,0:T(8,128)(2,1)}, u32[]{:S(2)}, u32[]{:S(2)}) collective-permute-start(bf16[576,1024]{1,0:T(8,128)(2,1)} %bitcast.57), channel_id=1, source_target_pairs={{0,12},{12,0},{1,13},{13,1},{2,14},{14,2},{3,15},{15,3},{4,16},{16... | collective-permute-start | bytes 3538952 | tf_op jit(solution)/shard_map/ppermute | solution.py:137
  82.4 6.0 %weight_quarters.1 = (bf16[640,1024]{1,0:T(8,128)(2,1)}, bf16[640,1024]{1,0:T(8,128)(2,1)}) custom-call(s32[1]{0:T(128)} %bitcast.place_ref, bf16[640,4096]{1,0:T(8,128)(2,1)} %weight_ref), custom_call_target="tpu_custom_call" | custom-call | tf_op jit(solution)/shard_map/weight_quarters/pallas_call | solution.py:63
  88.4 4.0 %fusion.14 = f32[576,640]{1,0:T(8,128)} fusion(bf16[576,1024]{1,0:T(8,128)(2,1)} %bitcast.58, bf16[640,1024]{1,0:T(8,128)(2,1)} %get-tuple-element.49), kind=kOutput, calls=%fused_computation.38 | convolution fusion | flops 754974720 | bytes 3964928 | tf_op jit(solution)/shard_map/dot_general | solution.py:139
  92.3 12.2 %all-to-all-done = bf16[4,256,1280]{2,1,0:T(8,128)(2,1)S(1)} async-done(((bf16[4,256,1280]{2,1,0:T(8,128)(2,1)}), bf16[4,256,1280]{2,1,0:T(8,128)(2,1)S(1)}, u32[]{:S(2)}, u32[]{:S(2)}) %all-to-all-start) | async-done | bytes 2621472 | tf_op jit(solution)/shard_map/all_to_all | solution.py:135
  104.5 0.8 reduce_sum.24
  105.5 1.0 copy.32
  106.4 0.4 copy-done.6
  106.9 2.5 %fusion.15 = f32[576,640]{1,0:T(8,128)S(1)} fusion(bf16[576,1024]{1,0:T(8,128)(2,1)} %collective-permute-done.7, bf16[640,1024]{1,0:T(8,128)(2,1)S(1)} %copy-done.6), kind=kOutput, calls=%fused_computation.39 | convolution fusion | flops 754974720 | bytes 3964928 | tf_op jit(solution)/shard_map/dot_general | solution.py:143
  109.6 7.5 %collective-permute-start.8 = (f32[12,24,640]{2,1,0:T(8,128)S(1)}, f32[12,24,640]{2,1,0:T(8,128)}, u32[]{:S(2)}, u32[]{:S(2)}) collective-permute-start(f32[12,24,640]{2,1,0:T(8,128)S(1)} %slice_bitcast_fusion), channel_id=1, source_target_pairs={{0,24},{24,0},{1,25},{25,1},{2,26},{26,2},{3,27},{27,3},{4,28},{28... | collective-permute-start | bytes 2211848 | tf_op jit(solution)/shard_map/ppermute | solution.py:145
  117.1 6.8 %all-to-all-start.1 = ((bf16[8,64,640]{2,1,0:T(8,128)(2,1)}), bf16[8,64,640]{2,1,0:T(8,128)(2,1)S(1)}, u32[]{:S(2)}, u32[]{:S(2)}) async-start(bf16[8,64,640]{2,1,0:T(8,128)(2,1)} %bitcast.14), calls=%async_computation.2 | async-start | bytes 1310720 | tf_op jit(solution)/shard_map/all_to_all | solution.py:154
  123.9 1.2 fusion.12
  125.4 0.8 copy-done.1
  126.3 1.2 fusion.11
  127.6 1.0 constant_dynamic-slice_fusion
  128.6 3.4 %collective-permute-start.5 = (bf16[12,4096]{1,0:T(8,128)(2,1)S(1)}, bf16[12,4096]{1,0:T(8,128)(2,1)S(1)}, u32[]{:S(2)}, u32[]{:S(2)}) collective-permute-start(bf16[12,4096]{1,0:T(8,128)(2,1)S(1)} %constant_dynamic-slice_fusion), channel_id=1, source_target_pairs={{0,12},{12,0},{1,13},{13,1},{2,14},{14,2},{3,15},{15,3},{4,16},{16... | collective-permute-start | bytes 294920 | tf_op jit(solution)/shard_map/ppermute | solution.py:160
  132.0 12.7 %all-to-all-done.1 = bf16[8,64,640]{2,1,0:T(8,128)(2,1)S(1)} async-done(((bf16[8,64,640]{2,1,0:T(8,128)(2,1)}), bf16[8,64,640]{2,1,0:T(8,128)(2,1)S(1)}, u32[]{:S(2)}, u32[]{:S(2)}) %all-to-all-start.1) | async-done | bytes 655392 | tf_op jit(solution)/shard_map/all_to_all | solution.py:154
  144.8 0.8 copy.36
  145.6 0.7 add_convert_fusion
  (39 shorter events, 2.0 us)
Async XLA Ops:
  7.2 120.4 %reduce-scatter.2.cloned.1.call-start = ((), (), s32[]{:S(2)}) async-start(), calls=%async_computation.3 | async-start | bytes 2555904 | tf_op jit(solution)/shard_map/reduce_scatter | solution.py:118
  8.9 19.5 %collective-permute-start = (bf16[12,1024]{1,0:T(8,128)(2,1)}, bf16[12,1024]{1,0:T(8,128)(2,1)S(1)}, u32[]{:S(2)}, u32[]{:S(2)}) collective-permute-start(bf16[12,1024]{1,0:T(8,128)(2,1)} %get-tuple-element.31), channel_id=1, source_target_pairs={{0,24},{24,0},{1,25},{25,1},{2,26},{26,2},{3,27},{27,3},{4,28},{28... | collective-permute-start | bytes 73736 | tf_op jit(solution)/shard_map/ppermute | solution.py:88
  21.3 7.1 %collective-permute-start.1 = (bf16[12,1024]{1,0:T(8,128)(2,1)}, bf16[12,1024]{1,0:T(8,128)(2,1)S(1)}, u32[]{:S(2)}, u32[]{:S(2)}) collective-permute-start(bf16[12,1024]{1,0:T(8,128)(2,1)} %get-tuple-element.32), channel_id=1, source_target_pairs={{0,12},{12,0},{1,13},{13,1},{2,14},{14,2},{3,15},{15,3},{4,16},{16... | collective-permute-start | bytes 73736 | tf_op jit(solution)/shard_map/ppermute | solution.py:89
  23.2 5.4 %collective-permute-start.2 = (bf16[12,1024]{1,0:T(8,128)(2,1)}, bf16[12,1024]{1,0:T(8,128)(2,1)S(1)}, u32[]{:S(2)}, u32[]{:S(2)}) collective-permute-start(bf16[12,1024]{1,0:T(8,128)(2,1)} %get-tuple-element.33), channel_id=1, source_target_pairs={{0,36},{12,24},{24,12},{36,0},{1,37},{13,25},{25,13},{37,1},{2,38}... | collective-permute-start | bytes 73736 | tf_op jit(solution)/shard_map/ppermute | solution.py:90
  28.1 2.7 %copy-start.5 = (bf16[12,1024]{1,0:T(8,128)(2,1)S(1)}, bf16[12,1024]{1,0:T(8,128)(2,1)}, u32[]{:S(2)}) copy-start(bf16[12,1024]{1,0:T(8,128)(2,1)} %get-tuple-element.30) | copy-start | bytes 73732
  28.7 3.6 %collective-permute-start.3 = (bf16[288,640]{1,0:T(8,128)(2,1)S(1)}, bf16[288,640]{1,0:T(8,128)(2,1)S(1)}, u32[]{:S(2)}, u32[]{:S(2)}) collective-permute-start(bf16[288,640]{1,0:T(8,128)(2,1)S(1)} %reshape.87), channel_id=1, source_target_pairs={{0,24},{24,0},{1,25},{25,1},{2,26},{26,2},{3,27},{27,3},{4,28},{28... | collective-permute-start | bytes 1105928 | tf_op jit(solution)/shard_map/ppermute | solution.py:99
  32.4 23.6 %collective-permute-start.4 = (bf16[576,640]{1,0:T(8,128)(2,1)S(1)}, bf16[576,640]{1,0:T(8,128)(2,1)S(1)}, u32[]{:S(2)}, u32[]{:S(2)}) collective-permute-start(bf16[576,640]{1,0:T(8,128)(2,1)S(1)} %bitcast.48), channel_id=1, source_target_pairs={{0,12},{12,0},{1,13},{13,1},{2,14},{14,2},{3,15},{15,3},{4,16},{16... | collective-permute-start | bytes 2211848 | tf_op jit(solution)/shard_map/ppermute | solution.py:112
  56.0 13.1 %collective-permute-start.6 = (bf16[288,1024]{1,0:T(8,128)(2,1)S(1)}, bf16[288,1024]{1,0:T(8,128)(2,1)S(1)}, u32[]{:S(2)}, u32[]{:S(2)}) collective-permute-start(bf16[288,1024]{1,0:T(8,128)(2,1)S(1)} %all_gather.3), channel_id=1, source_target_pairs={{0,1},{1,0},{2,3},{3,2},{4,5},{5,4},{6,7},{7,6},{8,9},{9,8},{10,11... | collective-permute-start | bytes 1769480 | tf_op jit(solution)/shard_map/ppermute | solution.py:115
  69.3 3.8 %copy-start.3 = (bf16[6,2,48,1024]{3,2,1,0:T(8,128)(2,1)}, bf16[6,2,48,1024]{3,2,1,0:T(8,128)(2,1)S(1)}, u32[]{:S(2)}) copy-start(bf16[6,2,48,1024]{3,2,1,0:T(8,128)(2,1)S(1)} %pad_maximum_fusion.1) | copy-start | bytes 3538948
  73.1 31.4 %all-to-all-start = ((bf16[4,256,1280]{2,1,0:T(8,128)(2,1)}), bf16[4,256,1280]{2,1,0:T(8,128)(2,1)S(1)}, u32[]{:S(2)}, u32[]{:S(2)}) async-start(bf16[4,256,1280]{2,1,0:T(8,128)(2,1)} %bitcast.49), calls=%async_computation.1 | async-start | bytes 5242880 | tf_op jit(solution)/shard_map/all_to_all | solution.py:135
  77.2 29.2 %collective-permute-start.7 = (bf16[576,1024]{1,0:T(8,128)(2,1)}, bf16[576,1024]{1,0:T(8,128)(2,1)}, u32[]{:S(2)}, u32[]{:S(2)}) collective-permute-start(bf16[576,1024]{1,0:T(8,128)(2,1)} %bitcast.57), channel_id=1, source_target_pairs={{0,12},{12,0},{1,13},{13,1},{2,14},{14,2},{3,15},{15,3},{4,16},{16... | collective-permute-start | bytes 3538952 | tf_op jit(solution)/shard_map/ppermute | solution.py:137
  105.3 1.6 %copy-start.6 = (bf16[640,1024]{1,0:T(8,128)(2,1)S(1)}, bf16[640,1024]{1,0:T(8,128)(2,1)}, u32[]{:S(2)}) copy-start(bf16[640,1024]{1,0:T(8,128)(2,1)} %get-tuple-element.52) | copy-start | bytes 3932164
  106.9 2.5 %copy-start = (f32[576,640]{1,0:T(8,128)S(1)}, f32[576,640]{1,0:T(8,128)}, u32[]{:S(2)}) copy-start(f32[576,640]{1,0:T(8,128)} %fusion.14) | copy-start | bytes 4423684
  109.6 14.3 %collective-permute-start.8 = (f32[12,24,640]{2,1,0:T(8,128)S(1)}, f32[12,24,640]{2,1,0:T(8,128)}, u32[]{:S(2)}, u32[]{:S(2)}) collective-permute-start(f32[12,24,640]{2,1,0:T(8,128)S(1)} %slice_bitcast_fusion), channel_id=1, source_target_pairs={{0,24},{24,0},{1,25},{25,1},{2,26},{26,2},{3,27},{27,3},{4,28},{28... | collective-permute-start | bytes 2211848 | tf_op jit(solution)/shard_map/ppermute | solution.py:145
  117.1 27.6 %all-to-all-start.1 = ((bf16[8,64,640]{2,1,0:T(8,128)(2,1)}), bf16[8,64,640]{2,1,0:T(8,128)(2,1)S(1)}, u32[]{:S(2)}, u32[]{:S(2)}) async-start(bf16[8,64,640]{2,1,0:T(8,128)(2,1)} %bitcast.14), calls=%async_computation.2 | async-start | bytes 1310720 | tf_op jit(solution)/shard_map/all_to_all | solution.py:154
  125.2 1.0 copy-start.1
  125.2 1.1 copy-start.2
  127.6 18.1 %copy-start.4 = (bf16[24,4096]{1,0:T(8,128)(2,1)S(1)}, bf16[24,4096]{1,0:T(8,128)(2,1)}, u32[]{:S(2)}) copy-start(bf16[24,4096]{1,0:T(8,128)(2,1)} %reduce-scatter.2.cloned.1.call-done) | copy-start | bytes 589828
  128.6 17.0 %collective-permute-start.5 = (bf16[12,4096]{1,0:T(8,128)(2,1)S(1)}, bf16[12,4096]{1,0:T(8,128)(2,1)S(1)}, u32[]{:S(2)}, u32[]{:S(2)}) collective-permute-start(bf16[12,4096]{1,0:T(8,128)(2,1)S(1)} %constant_dynamic-slice_fusion), channel_id=1, source_target_pairs={{0,12},{12,0},{1,13},{13,1},{2,14},{14,2},{3,15},{15,3},{4,16},{16... | collective-permute-start | bytes 294920 | tf_op jit(solution)/shard_map/ppermute | solution.py:160
Sparse Core Ops, SparseCore 0:
  65.2 57.4 reduce-scatter.1

commit v10 on v9

--- a/solution.py
+++ b/solution.py
@@ -10,7 +10,6 @@
 NB = NX * NYH
 BF, F32 = jnp.bfloat16, jnp.float32
 SWAP = [(0, 1), (1, 0)]
-DIAGONAL = [(0, 3), (1, 2), (2, 1), (3, 0)]
 tie = lax.optimization_barrier
 
 
@@ -85,9 +84,7 @@
     across = (((1,), (1,)), ((), ()))
 
     mine, to_core, to_yl, to_diag = split_columns(place, cotangent)
-    from_core = lax.ppermute(to_core, "c", SWAP)
-    from_yl = lax.ppermute(to_yl, "yl", SWAP)
-    from_diag = lax.ppermute(to_diag, ("c", "yl"), DIAGONAL)
+    from_core = lax.ppermute(jnp.concatenate([to_core, to_diag], axis=0), "c", SWAP)
 
     gate_wide = gate_pre.astype(F32)
     up_wide = up_pre.astype(F32)
@@ -95,18 +92,13 @@
     act = gate_wide * sig
     hidden = (act * up_wide).astype(BF)
     hidden_z = hidden.reshape(NYL, NZ, rows, ff).transpose(1, 0, 2, 3).reshape(tok, ff)
-    hidden_z, from_core, from_yl, from_diag = tie((hidden_z, from_core, from_yl, from_diag))
     hidden_core = lax.ppermute(hidden_z, "c", SWAP)
+    hidden_z, from_core = tie((hidden_z, from_core))
+    mine_both = jnp.concatenate([mine, from_core[:rows]], axis=0)
+    from_yl = lax.ppermute(jnp.concatenate([to_yl, from_core[rows:]], axis=0), "yl", SWAP)
 
-    shard = jnp.concatenate(
-        [
-            jnp.where(first, mine, from_yl),
-            jnp.where(first, from_yl, mine),
-            jnp.where(first, from_core, from_diag),
-            jnp.where(first, from_diag, from_core),
-        ],
-        axis=0,
-    )
+    low, high = jnp.where(first, mine_both, from_yl), jnp.where(first, from_yl, mine_both)
+    shard = jnp.concatenate([low[:rows], high[:rows], low[rows:], high[rows:]], axis=0)
     hidden_near = jnp.stack([h.reshape(NZ, both, ff) for h in (hidden_z, hidden_core)], axis=1)
     shard, hidden_near, hidden_z = tie((shard, hidden_near, hidden_z))
     hidden_far = lax.ppermute(hidden_near.reshape(NC * tok, ff), "yl", SWAP)

time: 154 us -> 152 us (0.987)
  starting transfers between devices: 53.6 us -> 51.5 us
    ppermute x3 -> x2, starting transfers between devices: 17.9 us -> 14.4 us  [the longest x1 12.4 us: per_device(): lax.ppermute(jnp.concatenate([to_core, to_diag], axis=0), 'c', SWAP)]
  transfers between devices with their start and end apart: 12 -> 11, of which waited for: 5 -> 5; matrix products, arithmetic and copies ran while one was open for 16% -> 17% of each run, Pallas kernels for 4% -> 4%
where the time goes in v10:
time: 152 us; the launch traced here: 151 us
  starting transfers between devices  51.5 us (34%)
  waiting for transfers between devices  29 us (19%)
  blocking collectives  19.8 us (13%)
  matrix products  16.2 us (11%)
  between operations  14.3 us (9%)
  Pallas kernels  7.61 us (5%)
  other arithmetic  6.98 us (5%)
  local copies, waits for them, and re-layouts  5.32 us (4%)
    all_gather x1, blocking collectives, per_device(): mine_z = lax.all_gather(shard, 'zh', axis=0, tiled=True)  19.8 us
    all_to_all x1, waiting for transfers between devices, per_device(): by_y = lax.all_to_all(sum_x, ('yh', 'yl'), 0, 0)  12.7 us
    ppermute x1, starting transfers between devices, per_device(): lax.ppermute(jnp.concatenate([to_core, to_diag], axis=0), 'c', SWAP)  12.4 us
    all_to_all x1, waiting for transfers between devices, per_device(): by_x = lax.all_to_all(term, 'x', 0, 0)  12.1 us
    ppermute x1, starting transfers between devices, per_device(): back_z = back[:, 0] + lax.ppermute(back[:, 1], 'c', SWAP)  8.38 us
    all_to_all x1, starting transfers between devices, per_device(): by_y = lax.all_to_all(sum_x, ('yh', 'yl'), 0, 0)  8.07 us
    pallas_call x1, Pallas kernels, weight_quarters(): pl.pallas_call(weight_kernel, out_shape=[jax.ShapeDtypeStruct((ff, feat /...  5.95 us
    dot_general x1, matrix products, per_device(): jnp.dot(hidden_z, down_weight, preferred_element_type=F32).astype(BF)  5.92 us
  transfers between devices with their start and end apart: 11, of which 5 were waited for; matrix products, arithmetic and copies ran while one was open for 17% of the time, Pallas kernels for 4%

profile of v10, /device:TPU:1, one launch (start us, length us, event | category | flops | bytes accessed | tf_op | source)
XLA Modules:
  0.0 150.7 jit_solution(8212462687705678250)
XLA Ops:
  7.2 1.7 %split_columns.1 = (bf16[12,1024]{1,0:T(8,128)(2,1)}, bf16[12,1024]{1,0:T(8,128)(2,1)}, bf16[12,1024]{1,0:T(8,128)(2,1)}, bf16[12,1024]{1,0:T(8,128)(2,1)}) custom-call(s32[1]{0:T(128)} %bitcast.place_ref, bf16[12,4096]{1,0:T(8,128)(2,1)} %cot_ref.1), custom_call_target="tpu_custom_call" | custom-call | tf_op jit(solution)/shard_map/split_columns/pallas_call | solution.py:40
  8.9 0.8 pad_maximum_fusion.4
  9.7 12.4 %collective-permute-start = (bf16[24,1024]{1,0:T(8,128)(2,1)S(1)}, bf16[24,1024]{1,0:T(8,128)(2,1)S(1)}, u32[]{:S(2)}, u32[]{:S(2)}) collective-permute-start(bf16[24,1024]{1,0:T(8,128)(2,1)S(1)} %pad_maximum_fusion.4), channel_id=1, source_target_pairs={{0,24},{24,0},{1,25},{25,1},{2,26},{26,2},{3,27},{27,3},{4,28},{28... | collective-permute-start | bytes 147464 | tf_op jit(solution)/shard_map/ppermute | solution.py:87
  22.1 1.3 fusion.13
  23.8 0.5 copy-done.5
  24.2 1.9 %collective-permute-start.1 = (bf16[24,1024]{1,0:T(8,128)(2,1)S(1)}, bf16[24,1024]{1,0:T(8,128)(2,1)S(1)}, u32[]{:S(2)}, u32[]{:S(2)}) collective-permute-start(bf16[24,1024]{1,0:T(8,128)(2,1)S(1)} %pad_maximum_fusion.6), channel_id=1, source_target_pairs={{0,12},{12,0},{1,13},{13,1},{2,14},{14,2},{3,15},{15,3},{4,16},{16... | collective-permute-start | bytes 147464 | tf_op jit(solution)/shard_map/ppermute | solution.py:98
  26.2 1.9 %collective-permute-start.2 = (bf16[288,640]{1,0:T(8,128)(2,1)S(1)}, bf16[288,640]{1,0:T(8,128)(2,1)S(1)}, u32[]{:S(2)}, u32[]{:S(2)}) collective-permute-start(bf16[288,640]{1,0:T(8,128)(2,1)S(1)} %reshape.87), channel_id=1, source_target_pairs={{0,24},{24,0},{1,25},{25,1},{2,26},{26,2},{3,27},{27,3},{4,28},{28... | collective-permute-start | bytes 1105928 | tf_op jit(solution)/shard_map/ppermute | solution.py:95
  28.1 1.4 collective-permute-done.1
  29.8 3.4 %collective-permute-start.3 = (bf16[576,640]{1,0:T(8,128)(2,1)S(1)}, bf16[576,640]{1,0:T(8,128)(2,1)S(1)}, u32[]{:S(2)}, u32[]{:S(2)}) collective-permute-start(bf16[576,640]{1,0:T(8,128)(2,1)S(1)} %bitcast.48), channel_id=1, source_target_pairs={{0,12},{12,0},{1,13},{13,1},{2,14},{14,2},{3,15},{15,3},{4,16},{16... | collective-permute-start | bytes 2211848 | tf_op jit(solution)/shard_map/ppermute | solution.py:104
  33.2 19.8 %all_gather.3 = bf16[288,1024]{1,0:T(8,128)(2,1)S(1)} all-gather(bf16[48,1024]{1,0:T(8,128)(2,1)S(1)} %pad_maximum_fusion.3), channel_id=1, replica_groups=mesh['x'=4,'yh'=4,'c'=2,'yl'=2,'zh'=6,'zl'=2] {'zh'}, dimensions={0}, use_global_device_ids=true | all-gather | bytes 688128 | tf_op jit(solution)/shard_map/all_gather | solution.py:105
  53.1 3.4 %collective-permute-start.5 = (bf16[288,1024]{1,0:T(8,128)(2,1)S(1)}, bf16[288,1024]{1,0:T(8,128)(2,1)S(1)}, u32[]{:S(2)}, u32[]{:S(2)}) collective-permute-start(bf16[288,1024]{1,0:T(8,128)(2,1)S(1)} %all_gather.3), channel_id=1, source_target_pairs={{0,1},{1,0},{2,3},{3,2},{4,5},{5,4},{6,7},{7,6},{8,9},{9,8},{10,11... | collective-permute-start | bytes 1769480 | tf_op jit(solution)/shard_map/ppermute | solution.py:107
  56.5 5.9 %convolution_convert_fusion = bf16[288,4096]{1,0:T(8,128)(2,1)} fusion(bf16[288,640]{1,0:T(8,128)(2,1)S(1)} %reshape.87, bf16[640,4096]{1,0:T(8,128)(2,1)} %weight_ref), kind=kOutput, calls=%fused_computation | convolution fusion | flops 1511129088 | bytes 7970816 | tf_op jit(solution)/shard_map/dot_general | solution.py:109
  62.8 2.6 %collective-permute-done.5 = bf16[288,1024]{1,0:T(8,128)(2,1)S(1)} collective-permute-done((bf16[288,1024]{1,0:T(8,128)(2,1)S(1)}, bf16[288,1024]{1,0:T(8,128)(2,1)S(1)}, u32[]{:S(2)}, u32[]{:S(2)}) %collective-permute-start.5) | collective-permute-done | bytes 589856 | tf_op jit(solution)/shard_map/ppermute | solution.py:107
  65.6 3.8 %multiply_convert_fusion = bf16[1024,1280]{1,0:T(8,128)(2,1)} fusion(bf16[576,1024]{1,0:T(8,128)(2,1)S(1)} %bitcast.56, bf16[576,1280]{1,0:T(8,128)(2,1)S(1)} %pad_maximum_fusion), kind=kOutput, calls=%fused_computation.1 | convolution fusion | flops 1512570880 | bytes 5275648 | tf_op jit(solution)/shard_map/dot_general | solution.py:122
  69.4 4.1 %all-to-all-start = ((bf16[4,256,1280]{2,1,0:T(8,128)(2,1)}), bf16[4,256,1280]{2,1,0:T(8,128)(2,1)S(1)}, u32[]{:S(2)}, u32[]{:S(2)}) async-start(bf16[4,256,1280]{2,1,0:T(8,128)(2,1)} %bitcast.49), calls=%async_computation.1 | async-start | bytes 5242880 | tf_op jit(solution)/shard_map/all_to_all | solution.py:127
  73.4 4.4 %collective-permute-start.6 = (bf16[576,1024]{1,0:T(8,128)(2,1)}, bf16[576,1024]{1,0:T(8,128)(2,1)}, u32[]{:S(2)}, u32[]{:S(2)}) collective-permute-start(bf16[576,1024]{1,0:T(8,128)(2,1)} %bitcast.57), channel_id=1, source_target_pairs={{0,12},{12,0},{1,13},{13,1},{2,14},{14,2},{3,15},{15,3},{4,16},{16... | collective-permute-start | bytes 3538952 | tf_op jit(solution)/shard_map/ppermute | solution.py:129
  77.9 6.0 %weight_quarters.1 = (bf16[640,1024]{1,0:T(8,128)(2,1)}, bf16[640,1024]{1,0:T(8,128)(2,1)}) custom-call(s32[1]{0:T(128)} %bitcast.place_ref, bf16[640,4096]{1,0:T(8,128)(2,1)} %weight_ref), custom_call_target="tpu_custom_call" | custom-call | tf_op jit(solution)/shard_map/weight_quarters/pallas_call | solution.py:62
  83.8 4.0 %fusion.17 = f32[576,640]{1,0:T(8,128)} fusion(bf16[576,1024]{1,0:T(8,128)(2,1)} %bitcast.58, bf16[640,1024]{1,0:T(8,128)(2,1)} %get-tuple-element.45), kind=kOutput, calls=%fused_computation.42 | convolution fusion | flops 754974720 | bytes 3964928 | tf_op jit(solution)/shard_map/dot_general | solution.py:131
  87.8 12.1 %all-to-all-done = bf16[4,256,1280]{2,1,0:T(8,128)(2,1)S(1)} async-done(((bf16[4,256,1280]{2,1,0:T(8,128)(2,1)}), bf16[4,256,1280]{2,1,0:T(8,128)(2,1)S(1)}, u32[]{:S(2)}, u32[]{:S(2)}) %all-to-all-start) | async-done | bytes 2621472 | tf_op jit(solution)/shard_map/all_to_all | solution.py:127
  99.9 0.8 reduce_sum.24
  100.8 1.0 copy.32
  102.2 2.5 %fusion.18 = f32[576,640]{1,0:T(8,128)S(1)} fusion(bf16[576,1024]{1,0:T(8,128)(2,1)} %collective-permute-done.6, bf16[640,1024]{1,0:T(8,128)(2,1)S(1)} %copy-done.7), kind=kOutput, calls=%fused_computation.43 | convolution fusion | flops 754974720 | bytes 3964928 | tf_op jit(solution)/shard_map/dot_general | solution.py:135
  105.0 8.4 %collective-permute-start.7 = (f32[12,24,640]{2,1,0:T(8,128)S(1)}, f32[12,24,640]{2,1,0:T(8,128)}, u32[]{:S(2)}, u32[]{:S(2)}) collective-permute-start(f32[12,24,640]{2,1,0:T(8,128)S(1)} %slice_bitcast_fusion), channel_id=1, source_target_pairs={{0,24},{24,0},{1,25},{25,1},{2,26},{26,2},{3,27},{27,3},{4,28},{28... | collective-permute-start | bytes 2211848 | tf_op jit(solution)/shard_map/ppermute | solution.py:137
  113.4 8.1 %all-to-all-start.1 = ((bf16[8,64,640]{2,1,0:T(8,128)(2,1)}), bf16[8,64,640]{2,1,0:T(8,128)(2,1)S(1)}, u32[]{:S(2)}, u32[]{:S(2)}) async-start(bf16[8,64,640]{2,1,0:T(8,128)(2,1)} %bitcast.14), calls=%async_computation.2 | async-start | bytes 1310720 | tf_op jit(solution)/shard_map/all_to_all | solution.py:146
  121.4 1.2 fusion.12
  122.9 0.8 copy-done.1
  123.8 1.2 fusion.11
  125.1 1.0 constant_dynamic-slice_fusion
  126.1 3.4 %collective-permute-start.4 = (bf16[12,4096]{1,0:T(8,128)(2,1)S(1)}, bf16[12,4096]{1,0:T(8,128)(2,1)S(1)}, u32[]{:S(2)}, u32[]{:S(2)}) collective-permute-start(bf16[12,4096]{1,0:T(8,128)(2,1)S(1)} %constant_dynamic-slice_fusion), channel_id=1, source_target_pairs={{0,12},{12,0},{1,13},{13,1},{2,14},{14,2},{3,15},{15,3},{4,16},{16... | collective-permute-start | bytes 294920 | tf_op jit(solution)/shard_map/ppermute | solution.py:152
  129.5 12.7 %all-to-all-done.1 = bf16[8,64,640]{2,1,0:T(8,128)(2,1)S(1)} async-done(((bf16[8,64,640]{2,1,0:T(8,128)(2,1)}), bf16[8,64,640]{2,1,0:T(8,128)(2,1)S(1)}, u32[]{:S(2)}, u32[]{:S(2)}) %all-to-all-start.1) | async-done | bytes 655392 | tf_op jit(solution)/shard_map/all_to_all | solution.py:146
  142.3 0.8 copy.36
  143.1 0.7 add_convert_fusion
  (43 shorter events, 2.4 us)
Async XLA Ops:
  7.2 117.9 %reduce-scatter.2.cloned.1.call-start = ((), (), s32[]{:S(2)}) async-start(), calls=%async_computation.3 | async-start | bytes 2555904 | tf_op jit(solution)/shard_map/reduce_scatter | solution.py:110
  9.7 14.1 %collective-permute-start = (bf16[24,1024]{1,0:T(8,128)(2,1)S(1)}, bf16[24,1024]{1,0:T(8,128)(2,1)S(1)}, u32[]{:S(2)}, u32[]{:S(2)}) collective-permute-start(bf16[24,1024]{1,0:T(8,128)(2,1)S(1)} %pad_maximum_fusion.4), channel_id=1, source_target_pairs={{0,24},{24,0},{1,25},{25,1},{2,26},{26,2},{3,27},{27,3},{4,28},{28... | collective-permute-start | bytes 147464 | tf_op jit(solution)/shard_map/ppermute | solution.py:87
  23.5 0.8 copy-start.5
  23.5 6.0 %copy-start.6 = (bf16[12,1024]{1,0:T(8,128)(2,1)S(1)}, bf16[12,1024]{1,0:T(8,128)(2,1)}, u32[]{:S(2)}) copy-start(bf16[12,1024]{1,0:T(8,128)(2,1)} %get-tuple-element.28) | copy-start | bytes 73732
  24.2 5.3 %collective-permute-start.1 = (bf16[24,1024]{1,0:T(8,128)(2,1)S(1)}, bf16[24,1024]{1,0:T(8,128)(2,1)S(1)}, u32[]{:S(2)}, u32[]{:S(2)}) collective-permute-start(bf16[24,1024]{1,0:T(8,128)(2,1)S(1)} %pad_maximum_fusion.6), channel_id=1, source_target_pairs={{0,12},{12,0},{1,13},{13,1},{2,14},{14,2},{3,15},{15,3},{4,16},{16... | collective-permute-start | bytes 147464 | tf_op jit(solution)/shard_map/ppermute | solution.py:98
  26.2 3.6 %collective-permute-start.2 = (bf16[288,640]{1,0:T(8,128)(2,1)S(1)}, bf16[288,640]{1,0:T(8,128)(2,1)S(1)}, u32[]{:S(2)}, u32[]{:S(2)}) collective-permute-start(bf16[288,640]{1,0:T(8,128)(2,1)S(1)} %reshape.87), channel_id=1, source_target_pairs={{0,24},{24,0},{1,25},{25,1},{2,26},{26,2},{3,27},{27,3},{4,28},{28... | collective-permute-start | bytes 1105928 | tf_op jit(solution)/shard_map/ppermute | solution.py:95
  29.8 23.2 %collective-permute-start.3 = (bf16[576,640]{1,0:T(8,128)(2,1)S(1)}, bf16[576,640]{1,0:T(8,128)(2,1)S(1)}, u32[]{:S(2)}, u32[]{:S(2)}) collective-permute-start(bf16[576,640]{1,0:T(8,128)(2,1)S(1)} %bitcast.48), channel_id=1, source_target_pairs={{0,12},{12,0},{1,13},{13,1},{2,14},{14,2},{3,15},{15,3},{4,16},{16... | collective-permute-start | bytes 2211848 | tf_op jit(solution)/shard_map/ppermute | solution.py:104
  53.1 12.3 %collective-permute-start.5 = (bf16[288,1024]{1,0:T(8,128)(2,1)S(1)}, bf16[288,1024]{1,0:T(8,128)(2,1)S(1)}, u32[]{:S(2)}, u32[]{:S(2)}) collective-permute-start(bf16[288,1024]{1,0:T(8,128)(2,1)S(1)} %all_gather.3), channel_id=1, source_target_pairs={{0,1},{1,0},{2,3},{3,2},{4,5},{5,4},{6,7},{7,6},{8,9},{9,8},{10,11... | collective-permute-start | bytes 1769480 | tf_op jit(solution)/shard_map/ppermute | solution.py:107
  65.6 3.8 %copy-start.3 = (bf16[6,2,48,1024]{3,2,1,0:T(8,128)(2,1)}, bf16[6,2,48,1024]{3,2,1,0:T(8,128)(2,1)S(1)}, u32[]{:S(2)}) copy-start(bf16[6,2,48,1024]{3,2,1,0:T(8,128)(2,1)S(1)} %pad_maximum_fusion.1) | copy-start | bytes 3538948
  69.4 30.5 %all-to-all-start = ((bf16[4,256,1280]{2,1,0:T(8,128)(2,1)}), bf16[4,256,1280]{2,1,0:T(8,128)(2,1)S(1)}, u32[]{:S(2)}, u32[]{:S(2)}) async-start(bf16[4,256,1280]{2,1,0:T(8,128)(2,1)} %bitcast.49), calls=%async_computation.1 | async-start | bytes 5242880 | tf_op jit(solution)/shard_map/all_to_all | solution.py:127
  73.4 28.4 %collective-permute-start.6 = (bf16[576,1024]{1,0:T(8,128)(2,1)}, bf16[576,1024]{1,0:T(8,128)(2,1)}, u32[]{:S(2)}, u32[]{:S(2)}) collective-permute-start(bf16[576,1024]{1,0:T(8,128)(2,1)} %bitcast.57), channel_id=1, source_target_pairs={{0,12},{12,0},{1,13},{13,1},{2,14},{14,2},{3,15},{15,3},{4,16},{16... | collective-permute-start | bytes 3538952 | tf_op jit(solution)/shard_map/ppermute | solution.py:129
  100.7 1.6 %copy-start.7 = (bf16[640,1024]{1,0:T(8,128)(2,1)S(1)}, bf16[640,1024]{1,0:T(8,128)(2,1)}, u32[]{:S(2)}) copy-start(bf16[640,1024]{1,0:T(8,128)(2,1)} %get-tuple-element.48) | copy-start | bytes 3932164
  102.2 2.5 %copy-start = (f32[576,640]{1,0:T(8,128)S(1)}, f32[576,640]{1,0:T(8,128)}, u32[]{:S(2)}) copy-start(f32[576,640]{1,0:T(8,128)} %fusion.17) | copy-start | bytes 4423684
  105.0 16.5 %collective-permute-start.7 = (f32[12,24,640]{2,1,0:T(8,128)S(1)}, f32[12,24,640]{2,1,0:T(8,128)}, u32[]{:S(2)}, u32[]{:S(2)}) collective-permute-start(f32[12,24,640]{2,1,0:T(8,128)S(1)} %slice_bitcast_fusion), channel_id=1, source_target_pairs={{0,24},{24,0},{1,25},{25,1},{2,26},{26,2},{3,27},{27,3},{4,28},{28... | collective-permute-start | bytes 2211848 | tf_op jit(solution)/shard_map/ppermute | solution.py:137
  113.4 28.9 %all-to-all-start.1 = ((bf16[8,64,640]{2,1,0:T(8,128)(2,1)}), bf16[8,64,640]{2,1,0:T(8,128)(2,1)S(1)}, u32[]{:S(2)}, u32[]{:S(2)}) async-start(bf16[8,64,640]{2,1,0:T(8,128)(2,1)} %bitcast.14), calls=%async_computation.2 | async-start | bytes 1310720 | tf_op jit(solution)/shard_map/all_to_all | solution.py:146
  122.7 1.0 copy-start.1
  122.7 1.1 copy-start.2
  125.1 18.1 %copy-start.4 = (bf16[24,4096]{1,0:T(8,128)(2,1)S(1)}, bf16[24,4096]{1,0:T(8,128)(2,1)}, u32[]{:S(2)}) copy-start(bf16[24,4096]{1,0:T(8,128)(2,1)} %reduce-scatter.2.cloned.1.call-done) | copy-start | bytes 589828
  126.1 17.0 %collective-permute-start.4 = (bf16[12,4096]{1,0:T(8,128)(2,1)S(1)}, bf16[12,4096]{1,0:T(8,128)(2,1)S(1)}, u32[]{:S(2)}, u32[]{:S(2)}) collective-permute-start(bf16[12,4096]{1,0:T(8,128)(2,1)S(1)} %constant_dynamic-slice_fusion), channel_id=1, source_target_pairs={{0,12},{12,0},{1,13},{13,1},{2,14},{14,2},{3,15},{15,3},{4,16},{16... | collective-permute-start | bytes 294920 | tf_op jit(solution)/shard_map/ppermute | solution.py:152
Sparse Core Ops, SparseCore 0:
  62.6 57.4 reduce-scatter.1

commit v11 on v10

--- a/solution.py
+++ b/solution.py
@@ -29,9 +29,12 @@
 
             @pl.when(place_ref[0] == core * NYL + yl)
             def _():
-                wanted = ((core, yl), (1 - core, yl), (core, 1 - yl), (1 - core, 1 - yl))
-                for out_ref, (c, y) in zip(out_refs, wanted):
-                    out_ref[...] = quarter(cot_ref, c, y)
+                mine_ref, yl_ref, core_ref = out_refs
+                width = mine_ref.shape[1]
+                mine_ref[...] = quarter(cot_ref, core, yl)
+                yl_ref[...] = quarter(cot_ref, core, 1 - yl)
+                core_ref[:, :width] = quarter(cot_ref, 1 - core, yl)
+                core_ref[:, width:] = quarter(cot_ref, 1 - core, 1 - yl)
 
 
 def split_columns(place, cot):
@@ -39,9 +42,9 @@
     vmem = pl.BlockSpec(memory_space=pltpu.VMEM)
     return pl.pallas_call(
         split_kernel,
-        out_shape=[jax.ShapeDtypeStruct((rows, feat // 4), cot.dtype)] * 4,
+        out_shape=[jax.ShapeDtypeStruct((rows, feat // n), cot.dtype) for n in (4, 4, 2)],
         in_specs=[pl.BlockSpec(memory_space=pltpu.SMEM), vmem],
-        out_specs=[vmem] * 4,
+        out_specs=[vmem] * 3,
         name="split_columns",
     )(place, cot)
 
@@ -83,8 +86,9 @@
     place = (core * NYL + yl).reshape(1)
     across = (((1,), (1,)), ((), ()))
 
-    mine, to_core, to_yl, to_diag = split_columns(place, cotangent)
-    from_core = lax.ppermute(jnp.concatenate([to_core, to_diag], axis=0), "c", SWAP)
+    mine, to_yl, to_core = split_columns(place, cotangent)
+    from_core = lax.ppermute(to_core, "c", SWAP)
+    width = mine.shape[1]
 
     gate_wide = gate_pre.astype(F32)
     up_wide = up_pre.astype(F32)
@@ -94,8 +98,8 @@
     hidden_z = hidden.reshape(NYL, NZ, rows, ff).transpose(1, 0, 2, 3).reshape(tok, ff)
     hidden_core = lax.ppermute(hidden_z, "c", SWAP)
     hidden_z, from_core = tie((hidden_z, from_core))
-    mine_both = jnp.concatenate([mine, from_core[:rows]], axis=0)
-    from_yl = lax.ppermute(jnp.concatenate([to_yl, from_core[rows:]], axis=0), "yl", SWAP)
+    mine_both = jnp.concatenate([mine, from_core[:, :width]], axis=0)
+    from_yl = lax.ppermute(jnp.concatenate([to_yl, from_core[:, width:]], axis=0), "yl", SWAP)
 
     low, high = jnp.where(first, mine_both, from_yl), jnp.where(first, from_yl, mine_both)
     shard = jnp.concatenate([low[:rows], high[:rows], low[rows:], high[rows:]], axis=0)

time: 152 us -> 151 us (level)
  no operation moved by 1% of the time
where the time goes in v11:
time: 151 us; the launch traced here: 150 us
  starting transfers between devices  51.5 us (34%)
  waiting for transfers between devices  29 us (19%)
  blocking collectives  19.8 us (13%)
  matrix products  16.2 us (11%)
  between operations  14.3 us (9%)
  Pallas kernels  7.62 us (5%)
  other arithmetic  6.19 us (4%)
  local copies, waits for them, and re-layouts  5.31 us (4%)
    all_gather x1, blocking collectives, per_device(): mine_z = lax.all_gather(shard, 'zh', axis=0, tiled=True)  19.8 us
    all_to_all x1, waiting for transfers between devices, per_device(): by_y = lax.all_to_all(sum_x, ('yh', 'yl'), 0, 0)  12.7 us
    ppermute x1, starting transfers between devices, per_device(): from_core = lax.ppermute(to_core, 'c', SWAP)  12.4 us
    all_to_all x1, waiting for transfers between devices, per_device(): by_x = lax.all_to_all(term, 'x', 0, 0)  12.1 us
    ppermute x1, starting transfers between devices, per_device(): back_z = back[:, 0] + lax.ppermute(back[:, 1], 'c', SWAP)  8.39 us
    all_to_all x1, starting transfers between devices, per_device(): by_y = lax.all_to_all(sum_x, ('yh', 'yl'), 0, 0)  8.07 us
    pallas_call x1, Pallas kernels, weight_quarters(): pl.pallas_call(weight_kernel, out_shape=[jax.ShapeDtypeStruct((ff, feat /...  5.95 us
    dot_general x1, matrix products, per_device(): jnp.dot(hidden_z, down_weight, preferred_element_type=F32).astype(BF)  5.92 us
  transfers between devices with their start and end apart: 11, of which 5 were waited for; matrix products, arithmetic and copies ran while one was open for 17% of the time, Pallas kernels for 4%

profile of v11, /device:TPU:1, one launch (start us, length us, event | category | flops | bytes accessed | tf_op | source)
XLA Modules:
  0.0 149.9 jit_solution(9092694111501090750)
XLA Ops:
  7.2 1.7 %split_columns.1 = (bf16[12,1024]{1,0:T(8,128)(2,1)}, bf16[12,1024]{1,0:T(8,128)(2,1)}, bf16[12,2048]{1,0:T(8,128)(2,1)}) custom-call(s32[1]{0:T(128)} %bitcast.place_ref, bf16[12,4096]{1,0:T(8,128)(2,1)} %cot_ref.1), custom_call_target="tpu_custom_call" | custom-call | tf_op jit(solution)/shard_map/split_columns/pallas_call | solution.py:43
  8.9 12.4 %collective-permute-start = (bf16[12,2048]{1,0:T(8,128)(2,1)}, bf16[12,2048]{1,0:T(8,128)(2,1)S(1)}, u32[]{:S(2)}, u32[]{:S(2)}) collective-permute-start(bf16[12,2048]{1,0:T(8,128)(2,1)} %get-tuple-element.28), channel_id=1, source_target_pairs={{0,24},{24,0},{1,25},{25,1},{2,26},{26,2},{3,27},{27,3},{4,28},{28... | collective-permute-start | bytes 147464 | tf_op jit(solution)/shard_map/ppermute | solution.py:90
  21.3 1.3 fusion.13
  23.0 0.5 copy-done.5
  23.4 1.9 %collective-permute-start.1 = (bf16[24,1024]{1,0:T(8,128)(2,1)S(1)}, bf16[24,1024]{1,0:T(8,128)(2,1)S(1)}, u32[]{:S(2)}, u32[]{:S(2)}) collective-permute-start(bf16[24,1024]{1,0:T(8,128)(2,1)S(1)} %pad_maximum_fusion.5), channel_id=1, source_target_pairs={{0,12},{12,0},{1,13},{13,1},{2,14},{14,2},{3,15},{15,3},{4,16},{16... | collective-permute-start | bytes 147464 | tf_op jit(solution)/shard_map/ppermute | solution.py:102
  25.4 1.9 %collective-permute-start.2 = (bf16[288,640]{1,0:T(8,128)(2,1)S(1)}, bf16[288,640]{1,0:T(8,128)(2,1)S(1)}, u32[]{:S(2)}, u32[]{:S(2)}) collective-permute-start(bf16[288,640]{1,0:T(8,128)(2,1)S(1)} %reshape.87), channel_id=1, source_target_pairs={{0,24},{24,0},{1,25},{25,1},{2,26},{26,2},{3,27},{27,3},{4,28},{28... | collective-permute-start | bytes 1105928 | tf_op jit(solution)/shard_map/ppermute | solution.py:99
  27.3 1.4 collective-permute-done.1
  29.0 3.4 %collective-permute-start.3 = (bf16[576,640]{1,0:T(8,128)(2,1)S(1)}, bf16[576,640]{1,0:T(8,128)(2,1)S(1)}, u32[]{:S(2)}, u32[]{:S(2)}) collective-permute-start(bf16[576,640]{1,0:T(8,128)(2,1)S(1)} %bitcast.48), channel_id=1, source_target_pairs={{0,12},{12,0},{1,13},{13,1},{2,14},{14,2},{3,15},{15,3},{4,16},{16... | collective-permute-start | bytes 2211848 | tf_op jit(solution)/shard_map/ppermute | solution.py:108
  32.4 19.8 %all_gather.3 = bf16[288,1024]{1,0:T(8,128)(2,1)S(1)} all-gather(bf16[48,1024]{1,0:T(8,128)(2,1)S(1)} %pad_maximum_fusion.3), channel_id=1, replica_groups=mesh['x'=4,'yh'=4,'c'=2,'yl'=2,'zh'=6,'zl'=2] {'zh'}, dimensions={0}, use_global_device_ids=true | all-gather | bytes 688128 | tf_op jit(solution)/shard_map/all_gather | solution.py:109
  52.3 3.4 %collective-permute-start.5 = (bf16[288,1024]{1,0:T(8,128)(2,1)S(1)}, bf16[288,1024]{1,0:T(8,128)(2,1)S(1)}, u32[]{:S(2)}, u32[]{:S(2)}) collective-permute-start(bf16[288,1024]{1,0:T(8,128)(2,1)S(1)} %all_gather.3), channel_id=1, source_target_pairs={{0,1},{1,0},{2,3},{3,2},{4,5},{5,4},{6,7},{7,6},{8,9},{9,8},{10,11... | collective-permute-start | bytes 1769480 | tf_op jit(solution)/shard_map/ppermute | solution.py:111
  55.7 5.9 %convolution_convert_fusion = bf16[288,4096]{1,0:T(8,128)(2,1)} fusion(bf16[288,640]{1,0:T(8,128)(2,1)S(1)} %reshape.87, bf16[640,4096]{1,0:T(8,128)(2,1)} %weight_ref), kind=kOutput, calls=%fused_computation | convolution fusion | flops 1511129088 | bytes 7970816 | tf_op jit(solution)/shard_map/dot_general | solution.py:113
  62.0 2.6 %collective-permute-done.5 = bf16[288,1024]{1,0:T(8,128)(2,1)S(1)} collective-permute-done((bf16[288,1024]{1,0:T(8,128)(2,1)S(1)}, bf16[288,1024]{1,0:T(8,128)(2,1)S(1)}, u32[]{:S(2)}, u32[]{:S(2)}) %collective-permute-start.5) | collective-permute-done | bytes 589856 | tf_op jit(solution)/shard_map/ppermute | solution.py:111
  64.8 3.8 %multiply_convert_fusion = bf16[1024,1280]{1,0:T(8,128)(2,1)} fusion(bf16[576,1024]{1,0:T(8,128)(2,1)S(1)} %bitcast.56, bf16[576,1280]{1,0:T(8,128)(2,1)S(1)} %pad_maximum_fusion), kind=kOutput, calls=%fused_computation.1 | convolution fusion | flops 1512570880 | bytes 5275648 | tf_op jit(solution)/shard_map/dot_general | solution.py:126
  68.6 4.1 %all-to-all-start = ((bf16[4,256,1280]{2,1,0:T(8,128)(2,1)}), bf16[4,256,1280]{2,1,0:T(8,128)(2,1)S(1)}, u32[]{:S(2)}, u32[]{:S(2)}) async-start(bf16[4,256,1280]{2,1,0:T(8,128)(2,1)} %bitcast.49), calls=%async_computation.1 | async-start | bytes 5242880 | tf_op jit(solution)/shard_map/all_to_all | solution.py:131
  72.6 4.4 %collective-permute-start.6 = (bf16[576,1024]{1,0:T(8,128)(2,1)}, bf16[576,1024]{1,0:T(8,128)(2,1)}, u32[]{:S(2)}, u32[]{:S(2)}) collective-permute-start(bf16[576,1024]{1,0:T(8,128)(2,1)} %bitcast.57), channel_id=1, source_target_pairs={{0,12},{12,0},{1,13},{13,1},{2,14},{14,2},{3,15},{15,3},{4,16},{16... | collective-permute-start | bytes 3538952 | tf_op jit(solution)/shard_map/ppermute | solution.py:133
  77.1 5.9 %weight_quarters.1 = (bf16[640,1024]{1,0:T(8,128)(2,1)}, bf16[640,1024]{1,0:T(8,128)(2,1)}) custom-call(s32[1]{0:T(128)} %bitcast.place_ref, bf16[640,4096]{1,0:T(8,128)(2,1)} %weight_ref), custom_call_target="tpu_custom_call" | custom-call | tf_op jit(solution)/shard_map/weight_quarters/pallas_call | solution.py:65
  83.0 4.0 %fusion.17 = f32[576,640]{1,0:T(8,128)} fusion(bf16[576,1024]{1,0:T(8,128)(2,1)} %bitcast.58, bf16[640,1024]{1,0:T(8,128)(2,1)} %get-tuple-element.43), kind=kOutput, calls=%fused_computation.41 | convolution fusion | flops 754974720 | bytes 3964928 | tf_op jit(solution)/shard_map/dot_general | solution.py:135
  87.0 12.1 %all-to-all-done = bf16[4,256,1280]{2,1,0:T(8,128)(2,1)S(1)} async-done(((bf16[4,256,1280]{2,1,0:T(8,128)(2,1)}), bf16[4,256,1280]{2,1,0:T(8,128)(2,1)S(1)}, u32[]{:S(2)}, u32[]{:S(2)}) %all-to-all-start) | async-done | bytes 2621472 | tf_op jit(solution)/shard_map/all_to_all | solution.py:131
  99.1 0.8 reduce_sum.24
  100.0 1.0 copy.32
  101.0 0.4 copy-done.7
  101.4 2.5 %fusion.18 = f32[576,640]{1,0:T(8,128)S(1)} fusion(bf16[576,1024]{1,0:T(8,128)(2,1)} %collective-permute-done.6, bf16[640,1024]{1,0:T(8,128)(2,1)S(1)} %copy-done.7), kind=kOutput, calls=%fused_computation.42 | convolution fusion | flops 754974720 | bytes 3964928 | tf_op jit(solution)/shard_map/dot_general | solution.py:139
  104.2 8.4 %collective-permute-start.7 = (f32[12,24,640]{2,1,0:T(8,128)S(1)}, f32[12,24,640]{2,1,0:T(8,128)}, u32[]{:S(2)}, u32[]{:S(2)}) collective-permute-start(f32[12,24,640]{2,1,0:T(8,128)S(1)} %slice_bitcast_fusion), channel_id=1, source_target_pairs={{0,24},{24,0},{1,25},{25,1},{2,26},{26,2},{3,27},{27,3},{4,28},{28... | collective-permute-start | bytes 2211848 | tf_op jit(solution)/shard_map/ppermute | solution.py:141
  112.6 8.1 %all-to-all-start.1 = ((bf16[8,64,640]{2,1,0:T(8,128)(2,1)}), bf16[8,64,640]{2,1,0:T(8,128)(2,1)S(1)}, u32[]{:S(2)}, u32[]{:S(2)}) async-start(bf16[8,64,640]{2,1,0:T(8,128)(2,1)} %bitcast.14), calls=%async_computation.2 | async-start | bytes 1310720 | tf_op jit(solution)/shard_map/all_to_all | solution.py:150
  120.6 1.2 fusion.12
  122.1 0.8 copy-done.1
  123.0 1.2 fusion.11
  124.3 1.0 constant_dynamic-slice_fusion
  125.3 3.4 %collective-permute-start.4 = (bf16[12,4096]{1,0:T(8,128)(2,1)S(1)}, bf16[12,4096]{1,0:T(8,128)(2,1)S(1)}, u32[]{:S(2)}, u32[]{:S(2)}) collective-permute-start(bf16[12,4096]{1,0:T(8,128)(2,1)S(1)} %constant_dynamic-slice_fusion), channel_id=1, source_target_pairs={{0,12},{12,0},{1,13},{13,1},{2,14},{14,2},{3,15},{15,3},{4,16},{16... | collective-permute-start | bytes 294920 | tf_op jit(solution)/shard_map/ppermute | solution.py:156
  128.7 12.7 %all-to-all-done.1 = bf16[8,64,640]{2,1,0:T(8,128)(2,1)S(1)} async-done(((bf16[8,64,640]{2,1,0:T(8,128)(2,1)}), bf16[8,64,640]{2,1,0:T(8,128)(2,1)S(1)}, u32[]{:S(2)}, u32[]{:S(2)}) %all-to-all-start.1) | async-done | bytes 655392 | tf_op jit(solution)/shard_map/all_to_all | solution.py:150
  141.5 0.8 copy.36
  142.3 0.7 add_convert_fusion
  (42 shorter events, 2.0 us)
Async XLA Ops:
  7.2 117.1 %reduce-scatter.2.cloned.1.call-start = ((), (), s32[]{:S(2)}) async-start(), calls=%async_computation.3 | async-start | bytes 2555904 | tf_op jit(solution)/shard_map/reduce_scatter | solution.py:114
  8.9 14.0 %collective-permute-start = (bf16[12,2048]{1,0:T(8,128)(2,1)}, bf16[12,2048]{1,0:T(8,128)(2,1)S(1)}, u32[]{:S(2)}, u32[]{:S(2)}) collective-permute-start(bf16[12,2048]{1,0:T(8,128)(2,1)} %get-tuple-element.28), channel_id=1, source_target_pairs={{0,24},{24,0},{1,25},{25,1},{2,26},{26,2},{3,27},{27,3},{4,28},{28... | collective-permute-start | bytes 147464 | tf_op jit(solution)/shard_map/ppermute | solution.py:90
  22.7 0.8 copy-start.5
  22.7 6.0 %copy-start.6 = (bf16[12,1024]{1,0:T(8,128)(2,1)S(1)}, bf16[12,1024]{1,0:T(8,128)(2,1)}, u32[]{:S(2)}) copy-start(bf16[12,1024]{1,0:T(8,128)(2,1)} %get-tuple-element.27) | copy-start | bytes 73732
  23.4 5.3 %collective-permute-start.1 = (bf16[24,1024]{1,0:T(8,128)(2,1)S(1)}, bf16[24,1024]{1,0:T(8,128)(2,1)S(1)}, u32[]{:S(2)}, u32[]{:S(2)}) collective-permute-start(bf16[24,1024]{1,0:T(8,128)(2,1)S(1)} %pad_maximum_fusion.5), channel_id=1, source_target_pairs={{0,12},{12,0},{1,13},{13,1},{2,14},{14,2},{3,15},{15,3},{4,16},{16... | collective-permute-start | bytes 147464 | tf_op jit(solution)/shard_map/ppermute | solution.py:102
  25.4 3.6 %collective-permute-start.2 = (bf16[288,640]{1,0:T(8,128)(2,1)S(1)}, bf16[288,640]{1,0:T(8,128)(2,1)S(1)}, u32[]{:S(2)}, u32[]{:S(2)}) collective-permute-start(bf16[288,640]{1,0:T(8,128)(2,1)S(1)} %reshape.87), channel_id=1, source_target_pairs={{0,24},{24,0},{1,25},{25,1},{2,26},{26,2},{3,27},{27,3},{4,28},{28... | collective-permute-start | bytes 1105928 | tf_op jit(solution)/shard_map/ppermute | solution.py:99
  29.0 23.2 %collective-permute-start.3 = (bf16[576,640]{1,0:T(8,128)(2,1)S(1)}, bf16[576,640]{1,0:T(8,128)(2,1)S(1)}, u32[]{:S(2)}, u32[]{:S(2)}) collective-permute-start(bf16[576,640]{1,0:T(8,128)(2,1)S(1)} %bitcast.48), channel_id=1, source_target_pairs={{0,12},{12,0},{1,13},{13,1},{2,14},{14,2},{3,15},{15,3},{4,16},{16... | collective-permute-start | bytes 2211848 | tf_op jit(solution)/shard_map/ppermute | solution.py:108
  52.3 12.3 %collective-permute-start.5 = (bf16[288,1024]{1,0:T(8,128)(2,1)S(1)}, bf16[288,1024]{1,0:T(8,128)(2,1)S(1)}, u32[]{:S(2)}, u32[]{:S(2)}) collective-permute-start(bf16[288,1024]{1,0:T(8,128)(2,1)S(1)} %all_gather.3), channel_id=1, source_target_pairs={{0,1},{1,0},{2,3},{3,2},{4,5},{5,4},{6,7},{7,6},{8,9},{9,8},{10,11... | collective-permute-start | bytes 1769480 | tf_op jit(solution)/shard_map/ppermute | solution.py:111
  64.8 3.8 %copy-start.3 = (bf16[6,2,48,1024]{3,2,1,0:T(8,128)(2,1)}, bf16[6,2,48,1024]{3,2,1,0:T(8,128)(2,1)S(1)}, u32[]{:S(2)}) copy-start(bf16[6,2,48,1024]{3,2,1,0:T(8,128)(2,1)S(1)} %pad_maximum_fusion.1) | copy-start | bytes 3538948
  68.6 30.5 %all-to-all-start = ((bf16[4,256,1280]{2,1,0:T(8,128)(2,1)}), bf16[4,256,1280]{2,1,0:T(8,128)(2,1)S(1)}, u32[]{:S(2)}, u32[]{:S(2)}) async-start(bf16[4,256,1280]{2,1,0:T(8,128)(2,1)} %bitcast.49), calls=%async_computation.1 | async-start | bytes 5242880 | tf_op jit(solution)/shard_map/all_to_all | solution.py:131
  72.6 28.4 %collective-permute-start.6 = (bf16[576,1024]{1,0:T(8,128)(2,1)}, bf16[576,1024]{1,0:T(8,128)(2,1)}, u32[]{:S(2)}, u32[]{:S(2)}) collective-permute-start(bf16[576,1024]{1,0:T(8,128)(2,1)} %bitcast.57), channel_id=1, source_target_pairs={{0,12},{12,0},{1,13},{13,1},{2,14},{14,2},{3,15},{15,3},{4,16},{16... | collective-permute-start | bytes 3538952 | tf_op jit(solution)/shard_map/ppermute | solution.py:133
  99.9 1.6 %copy-start.7 = (bf16[640,1024]{1,0:T(8,128)(2,1)S(1)}, bf16[640,1024]{1,0:T(8,128)(2,1)}, u32[]{:S(2)}) copy-start(bf16[640,1024]{1,0:T(8,128)(2,1)} %get-tuple-element.46) | copy-start | bytes 3932164
  101.4 2.5 %copy-start = (f32[576,640]{1,0:T(8,128)S(1)}, f32[576,640]{1,0:T(8,128)}, u32[]{:S(2)}) copy-start(f32[576,640]{1,0:T(8,128)} %fusion.17) | copy-start | bytes 4423684
  104.2 16.5 %collective-permute-start.7 = (f32[12,24,640]{2,1,0:T(8,128)S(1)}, f32[12,24,640]{2,1,0:T(8,128)}, u32[]{:S(2)}, u32[]{:S(2)}) collective-permute-start(f32[12,24,640]{2,1,0:T(8,128)S(1)} %slice_bitcast_fusion), channel_id=1, source_target_pairs={{0,24},{24,0},{1,25},{25,1},{2,26},{26,2},{3,27},{27,3},{4,28},{28... | collective-permute-start | bytes 2211848 | tf_op jit(solution)/shard_map/ppermute | solution.py:141
  112.6 28.9 %all-to-all-start.1 = ((bf16[8,64,640]{2,1,0:T(8,128)(2,1)}), bf16[8,64,640]{2,1,0:T(8,128)(2,1)S(1)}, u32[]{:S(2)}, u32[]{:S(2)}) async-start(bf16[8,64,640]{2,1,0:T(8,128)(2,1)} %bitcast.14), calls=%async_computation.2 | async-start | bytes 1310720 | tf_op jit(solution)/shard_map/all_to_all | solution.py:150
  121.9 1.0 copy-start.1
  121.9 1.1 copy-start.2
  124.3 18.1 %copy-start.4 = (bf16[24,4096]{1,0:T(8,128)(2,1)S(1)}, bf16[24,4096]{1,0:T(8,128)(2,1)}, u32[]{:S(2)}) copy-start(bf16[24,4096]{1,0:T(8,128)(2,1)} %reduce-scatter.2.cloned.1.call-done) | copy-start | bytes 589828
  125.3 17.0 %collective-permute-start.4 = (bf16[12,4096]{1,0:T(8,128)(2,1)S(1)}, bf16[12,4096]{1,0:T(8,128)(2,1)S(1)}, u32[]{:S(2)}, u32[]{:S(2)}) collective-permute-start(bf16[12,4096]{1,0:T(8,128)(2,1)S(1)} %constant_dynamic-slice_fusion), channel_id=1, source_target_pairs={{0,12},{12,0},{1,13},{13,1},{2,14},{14,2},{3,15},{15,3},{4,16},{16... | collective-permute-start | bytes 294920 | tf_op jit(solution)/shard_map/ppermute | solution.py:156
Sparse Core Ops, SparseCore 0:
  61.8 57.5 reduce-scatter.1
